TPU v7x, 256 devices: a whole 4x4x8 slice. The times are simulated.
256 devices in a mesh: table: 32 (over x, y, core), fsdp: 8 (over z).
Axes of the slice: x: 4, y: 4, z: 8, core: 2. Of those that a mesh axis runs over, the one named last changes fastest.
Arguments:
- item_table: bfloat16 [65536, 1024], P('table'), may hold values from -36 to 36
- item_row: int32 [32768], P(('table', 'fsdp')), may hold values from 0 to 2047
- item_owner: int32 [32768, 1], P(('table', 'fsdp')), may hold values from 0 to 31; in each aligned block of 128 rows (0 to 127, 128 to 255, ...) at most 6 rows name the same one
- user_lengths: int32 [256, 8], P(('table', 'fsdp')), may hold values from 1 to 64, 128 in all within a row
- w_mix: bfloat16 [1024, 2048], P('fsdp'), may hold values from -0.1875 to 0.1875
- w_out: bfloat16 [512, 1024], P('fsdp'), may hold values from -0.25 to 0.25
- gain_in: float32 [1024], replicated, may hold values from 0.4 to 7.2
- gain_attn: float32 [512], replicated, may hold values from 0.4 to 7.2
- cotangent: bfloat16 [32768, 1024], P(('table', 'fsdp')), may hold values from -6 to 6
Outputs:
- layer_out: bfloat16 [32768, 1024], P(('table', 'fsdp'))
- table_grad: float32 [65536, 1024], P(('table', 'fsdp'))
- mix_grad: float32 [1024, 2048], P('fsdp')
- out_grad: float32 [512, 1024], P('fsdp')
Inputs may be any that keep to these rules, and one draw needn't show every extreme that they name: `item_owner`: among the 128 actions of one device, at most 6 name one owner, and in every draw some owner is named by exactly 6 actions of some device. `user_lengths`: each row sums to 128 and its longest history has 64 actions.
All inputs are finite; a program needn't handle non-finite values.
Results may differ from a plain program's by a relative error of at most 0.025.
Values may be sent and summed in bfloat16 or wider, within the bound.
No kernel may reach another device: no remote copies, remote signals or barrier semaphores. Data moves between devices by JAX's collectives and lax.ppermute only.
A program may use at most 128 MiB of HBM per device.

v0:
```python
import jax
import jax.numpy as jnp
from jax import lax
from jax.sharding import PartitionSpec as P

H = 4
DH = 128
MAXLEN = 64


def segment_mask(lengths_row, row_count):
    seg_ends = jnp.cumsum(lengths_row)
    position = jnp.arange(row_count, dtype=jnp.int32)
    segment = jnp.sum((position[:, None] >= seg_ends[None, :]).astype(jnp.int32), axis=1)
    same_user = segment[:, None] == segment[None, :]
    causal = position[None, :] <= position[:, None]
    return same_user & causal


def layer_norm(inputs, scales):
    average = jnp.mean(inputs, axis=-1, keepdims=True)
    centered = inputs - average
    variance = jnp.mean(centered * centered, axis=-1, keepdims=True)
    return centered * lax.rsqrt(variance + 1e-05) * scales


def layer_forward(embedded, w_mix, w_out, gain_in, gain_attn, allowed):
    row_count = embedded.shape[0]
    attn_width = H * DH
    widened = embedded.astype(jnp.float32)
    normed = layer_norm(widened, gain_in).astype(jnp.bfloat16)
    mixture = jnp.dot(normed, w_mix, preferred_element_type=jnp.float32)
    activated = jax.nn.silu(mixture).astype(jnp.bfloat16)
    gate_u = activated[:, :attn_width]
    value_heads = activated[:, attn_width : 2 * attn_width].reshape(row_count, H, DH)
    query_heads = activated[:, 2 * attn_width : 3 * attn_width].reshape(row_count, H, DH)
    key_heads = activated[:, 3 * attn_width :].reshape(row_count, H, DH)
    scores = jnp.einsum(
        "ihd,jhd->hij", query_heads, key_heads, preferred_element_type=jnp.float32
    ) * DH ** (-0.5)
    weights = (jnp.where(allowed[None], jax.nn.silu(scores), 0.0) / MAXLEN).astype(jnp.bfloat16)
    attended = jnp.einsum("hij,jhd->ihd", weights, value_heads, preferred_element_type=jnp.float32)
    attended = attended.reshape(row_count, attn_width).astype(jnp.bfloat16)
    gated_rows = (
        layer_norm(attended.astype(jnp.float32), gain_attn) * gate_u.astype(jnp.float32)
    ).astype(jnp.bfloat16)
    layer_out = widened + jnp.dot(gated_rows, w_out, preferred_element_type=jnp.float32)
    return layer_out.astype(jnp.bfloat16)


def shards(
    item_table, item_row, item_owner, user_lengths, w_mix, w_out, gain_in, gain_attn, cotangent
):
    owners = lax.axis_size("table")
    fsdp_count = lax.axis_size("fsdp")
    tok_rows = item_row.shape[0]
    table_rows = item_table.shape[0]
    width_model = item_table.shape[1]
    capacity = 3 * tok_rows // (2 * owners)
    owner_col = item_owner[:, 0]
    onehot = (owner_col[:, None] == jnp.arange(owners, dtype=jnp.int32)[None, :]).astype(jnp.int32)
    before = jnp.cumsum(onehot, axis=0) - onehot
    slot_index = jnp.sum(before * onehot, axis=1)
    target = owner_col * capacity + slot_index
    requests = (
        jnp.zeros((owners * capacity,), jnp.int32)
        .at[target]
        .set(item_row)
        .reshape(owners, capacity)
    )
    asked_rows = lax.all_to_all(requests, "table", split_axis=0, concat_axis=0, tiled=True)
    found_rows = jnp.take(item_table, asked_rows, axis=0)
    returned = lax.all_to_all(found_rows, "table", split_axis=0, concat_axis=0, tiled=True)
    embedded = jnp.take(returned.reshape(owners * capacity, width_model), target, axis=0)
    mix_full, out_full = (
        lax.all_gather(w_mix, "fsdp", axis=0, tiled=True),
        lax.all_gather(w_out, "fsdp", axis=0, tiled=True),
    )
    allowed = segment_mask(user_lengths[0], tok_rows)

    def apply_layer(emb_rows, mix_weights, out_weights):
        return layer_forward(emb_rows, mix_weights, out_weights, gain_in, gain_attn, allowed)

    layer_out, pullback = jax.vjp(apply_layer, embedded, mix_full, out_full)
    d_emb, d_mix, d_out = pullback(cotangent)

    def spread(gradient):
        total_rows = gradient.shape[0]
        piece_rows = total_rows // (fsdp_count * owners)
        wide_grad = gradient.astype(jnp.float32).reshape(
            fsdp_count, owners, piece_rows, gradient.shape[1]
        )
        return wide_grad.transpose(1, 0, 2, 3).reshape(total_rows, gradient.shape[1])

    mix_share, out_share = (
        lax.psum_scatter(spread(d_mix), ("table", "fsdp"), scatter_dimension=0, tiled=True),
        lax.psum_scatter(spread(d_out), ("table", "fsdp"), scatter_dimension=0, tiled=True),
    )
    mix_sum, out_sum = (
        lax.all_gather(mix_share.astype(jnp.bfloat16), "table", axis=0, tiled=True).astype(
            mix_share.dtype
        ),
        lax.all_gather(out_share.astype(jnp.bfloat16), "table", axis=0, tiled=True).astype(
            out_share.dtype
        ),
    )
    mix_squares, out_squares = lax.psum(
        (jnp.sum(mix_sum * mix_sum), jnp.sum(out_sum * out_sum)), "fsdp"
    )
    mix_count = float(mix_sum.shape[0] * fsdp_count * mix_sum.shape[1])
    out_count = float(out_sum.shape[0] * fsdp_count * out_sum.shape[1])
    mix_root = jnp.sqrt(mix_squares / mix_count + 1e-06)
    out_root = jnp.sqrt(out_squares / out_count + 1e-06)
    mix_grad = mix_sum * jnp.minimum(1.0, 1.0 / mix_root)
    out_grad = out_sum * jnp.minimum(1.0, 1.0 / out_root)
    grad_slots = jnp.zeros((owners * capacity, width_model), jnp.bfloat16).at[target].set(d_emb)
    received = lax.all_to_all(
        grad_slots.reshape(owners, capacity, width_model),
        "table",
        split_axis=0,
        concat_axis=0,
        tiled=True,
    )
    asked_flat = asked_rows.reshape(owners * capacity)
    received_flat = received.reshape(owners * capacity, width_model)
    partial_grad = (
        jnp.zeros((table_rows, width_model), jnp.float32)
        .at[asked_flat]
        .add(received_flat.astype(jnp.float32))
    )
    table_grad = lax.psum_scatter(
        partial_grad.astype(jnp.bfloat16), "fsdp", scatter_dimension=0, tiled=True
    ).astype(jnp.float32)
    return (layer_out, table_grad, mix_grad, out_grad)


def solution(mesh):
    in_specs = (
        P("table", None),
        P(("table", "fsdp")),
        P(("table", "fsdp"), None),
        P(("table", "fsdp"), None),
        P("fsdp", None),
        P("fsdp", None),
        P(),
        P(),
        P(("table", "fsdp"), None),
    )
    out_specs = (
        P(("table", "fsdp"), None),
        P(("table", "fsdp"), None),
        P("fsdp", None),
        P("fsdp", None),
    )
    return jax.shard_map(shards, mesh=mesh, in_specs=in_specs, out_specs=out_specs, check_vma=False)
```

profile of v0, /device:TPU:1, one launch (start us, length us, event | category | flops | bytes accessed | tf_op | source)
XLA Modules:
  0.0 419.2 jit_solution(7593991610046955257)
XLA Ops:
  12.2 8.6 %all-to-all-start = ((s32[32,1,6]{2,1,0:T(1,128)}), s32[32,1,6]{2,1,0:T(1,128)S(1)}, u32[]{:S(2)}, u32[]{:S(2)}) async-start(s32[32,1,6]{2,1,0:T(1,128)} %bitcast.4), calls=%async_computation | async-start | bytes 32768 | tf_op jit(solution)/shard_map/all_to_all | solution.py:71
  21.5 6.1 %all-to-all-done = s32[32,1,6]{2,1,0:T(1,128)S(1)} async-done(((s32[32,1,6]{2,1,0:T(1,128)}), s32[32,1,6]{2,1,0:T(1,128)S(1)}, u32[]{:S(2)}, u32[]{:S(2)}) %all-to-all-start) | async-done | bytes 800 | tf_op jit(solution)/shard_map/all_to_all | solution.py:71
  27.8 4.0 gather_fusion
  32.9 4.2 %all-to-all-start.1 = ((bf16[32,6,1024]{2,1,0:T(8,128)(2,1)}), bf16[32,6,1024]{2,1,0:T(8,128)(2,1)S(1)}, u32[]{:S(2)}, u32[]{:S(2)}) async-start(bf16[32,6,1024]{2,1,0:T(8,128)(2,1)} %broadcast_select_fusion), calls=%async_computation.1 | async-start | bytes 1048576 | tf_op jit(solution)/shard_map/all_to_all | solution.py:73
  37.5 11.3 %all-to-all-done.1 = bf16[32,6,1024]{2,1,0:T(8,128)(2,1)S(1)} async-done(((bf16[32,6,1024]{2,1,0:T(8,128)(2,1)}), bf16[32,6,1024]{2,1,0:T(8,128)(2,1)S(1)}, u32[]{:S(2)}, u32[]{:S(2)}) %all-to-all-start.1) | async-done | bytes 393248 | tf_op jit(solution)/shard_map/all_to_all | solution.py:73
  50.3 18.1 %all-gather.5.cloned.1.call-done = bf16[1024,2048]{1,0:T(8,128)(2,1)} async-done(((bf16[128,2048]{1,0:T(8,128)(2,1)}), bf16[1024,2048]{1,0:T(8,128)(2,1)}) %all-gather.5.cloned.1.call-update) | async-done | bytes 4194320 | tf_op jit(solution)/shard_map/all_gather | solution.py:76
  68.4 3.1 multiply_convert_fusion
  72.7 29.8 %all-gather.7.cloned.1.call-done = bf16[512,1024]{1,0:T(8,128)(2,1)} async-done(((bf16[64,1024]{1,0:T(8,128)(2,1)}), bf16[512,1024]{1,0:T(8,128)(2,1)}) %all-gather.7.cloned.1.call-update) | async-done | bytes 1048592 | tf_op jit(solution)/shard_map/all_gather | solution.py:77
  107.6 3.9 fusion.21
  114.3 12.6 %all-to-all-start.2 = ((bf16[32,6,1024]{2,1,0:T(8,128)(2,1)}), bf16[32,6,1024]{2,1,0:T(8,128)(2,1)S(1)}, u32[]{:S(2)}, u32[]{:S(2)}) async-start(bf16[32,6,1024]{2,1,0:T(8,128)(2,1)} %reshape.268), calls=%async_computation.2 | async-start | bytes 1048576 | tf_op jit(solution)/shard_map/all_to_all | solution.py:117
  128.5 10.1 %all-to-all-done.2 = bf16[32,6,1024]{2,1,0:T(8,128)(2,1)S(1)} async-done(((bf16[32,6,1024]{2,1,0:T(8,128)(2,1)}), bf16[32,6,1024]{2,1,0:T(8,128)(2,1)S(1)}, u32[]{:S(2)}, u32[]{:S(2)}) %all-to-all-start.2) | async-done | bytes 393248 | tf_op jit(solution)/shard_map/all_to_all | solution.py:117
  138.7 5.8 %scatter_custom_fusion.2 = f32[2048,1024]{1,0:T(8,128)} fusion(s32[192]{0:T(256)S(1)} %bitcast.98, f32[192,1024]{1,0:T(8,128)S(1)} %reshape.323, f32[]{:T(128)} %constant.76.clone.1), kind=kCustom, calls=%fused_computation.7 | custom fusion | flops 196608 | bytes 8388612 | tf_op jit(solution)/shard_map/scatter-add | solution.py:129
  144.5 6.0 %convert_element_type.166 = bf16[2048,1024]{1,0:T(8,128)(2,1)} convert(f32[2048,1024]{1,0:T(8,128)} %scatter_custom_fusion.2) | non-fusion elementwise | flops 2097152 | bytes 12582912 | tf_op jit(solution)/shard_map/convert_element_type | solution.py:132
  152.3 2.5 reshape.286
  154.8 2.6 copy.91
  157.4 2.7 reshape.280
  160.2 5.9 %convert_convert_fusion = f32[1024,2048]{1,0:T(8,128)} fusion(f32[1024]{0:T(1024)S(1)} %copy-done.5, f32[128]{0:T(128)S(1)} %copy-done.15, f32[128]{0:T(128)S(1)} %copy-done.13, bf16[128,1024]{1,0:T(8,128)(2,1)S(1)} %gather_fusion.1, pred[128]{0:T(512)(128)(4,1)S(1)} %copy-done.8, f32[128,2048]{1,0:T(8,128)} %copy-done.2, ...), kind=kOutput, calls=%fused_computation.6 | convolution fusion | flops 546308096 | bytes 10228864 | tf_op jit(solution)/shard_map/transpose(jvp())/dot_general | solution.py:32
  166.1 9.8 %reshape.284 = f32[8,32,4,2048]{3,2,1,0:T(4,128)} reshape(f32[1024,2048]{1,0:T(8,128)} %convert_convert_fusion) | data formatting | bytes 16777216 | tf_op jit(solution)/shard_map/reshape | solution.py:93
  175.9 10.4 %copy.90 = f32[8,32,4,2048]{3,2,0,1:T(4,128)} copy(f32[8,32,4,2048]{3,2,1,0:T(4,128)} %reshape.284) | data formatting | bytes 16777216 | tf_op jit(solution)/shard_map/reshape | solution.py:93
  186.4 10.0 %reshape.278 = f32[1024,2048]{1,0:T(8,128)} reshape(f32[32,8,4,2048]{3,2,1,0:T(4,128)} %bitcast.75) | data formatting | bytes 16777216 | tf_op jit(solution)/shard_map/reshape | solution.py:93
  196.4 145.3 %all-reduce.9 = (bf16[1024,2048]{1,0:T(8,128)(2,1)}, bf16[512,1024]{1,0:T(8,128)(2,1)}) all-reduce(f32[1024,2048]{1,0:T(8,128)} %reshape.278, f32[512,1024]{1,0:T(8,128)S(1)} %reshape.280), channel_id=3, replica_groups=mesh['table'=32,'fsdp'=8] {'table','fsdp'}, use_global_device_ids=true, to_apply=%region_16.17.clone | all-reduce | flops 2621440 | bytes 15728640
  342.5 24.2 %all-gather.1 = bf16[32,2,1024]{2,1,0:T(2,128)(2,1)S(1)} all-gather(bf16[1,2,1024]{2,1,0:T(2,128)(2,1)S(1)} %fusion.38), channel_id=1, replica_groups=mesh['table'=32,'fsdp'=8] {'table'}, dimensions={0}, use_global_device_ids=true | all-gather | bytes 135168 | tf_op jit(solution)/shard_map/all_gather | solution.py:103
  367.5 23.7 %all-gather = bf16[32,4,2048]{2,1,0:T(4,128)(2,1)S(1)} all-gather(bf16[1,4,2048]{2,1,0:T(4,128)(2,1)S(1)} %fusion.37), channel_id=1, replica_groups=mesh['table'=32,'fsdp'=8] {'table'}, dimensions={0}, use_global_device_ids=true | all-gather | bytes 540672 | tf_op jit(solution)/shard_map/all_gather | solution.py:100
  393.2 12.6 %all-reduce.7 = (f32[]{:T(128)}, f32[]{:T(128)}) all-reduce(f32[]{:T(128)} %fusion.13, f32[]{:T(128)} %fusion.24), channel_id=1, replica_groups=mesh['table'=32,'fsdp'=8] {'fsdp'}, use_global_device_ids=true, to_apply=%region_18.19 | all-reduce | flops 2 | bytes 16 | tf_op jit(solution)/shard_map/psum | solution.py:107
  (115 shorter events, 30.1 us)
Async XLA Ops:
  7.2 61.3 %all-gather.5.cloned.1.call-start = ((), (), s32[]{:S(2)}) async-start(), calls=%async_computation.4 | async-start | bytes 4718592 | tf_op jit(solution)/shard_map/all_gather | solution.py:76
  7.9 29.2 %copy-start.21 = (s32[1,8]{1,0:T(1,128)S(1)}, s32[1,8]{1,0:T(1,128)}, u32[]{:S(2)}) copy-start(s32[1,8]{1,0:T(1,128)} %param.12) | copy-start | bytes 100
  10.3 27.0 %copy-start.18 = (s32[128,1]{0,1:T(1,128)}, s32[128,1]{0,1:T(1,128)S(1)}, u32[]{:S(2)}) copy-start(s32[128,1]{0,1:T(1,128)S(1)} %get-tuple-element.11) | copy-start | bytes 1540
  10.3 58.1 %copy-start.6 = (pred[128]{0:T(512)(128)(4,1)}, pred[128]{0:T(512)(128)(4,1)S(1)}, u32[]{:S(2)}) copy-start(pred[128]{0:T(512)(128)(4,1)S(1)} %get-tuple-element.10) | copy-start | bytes 388
  12.2 15.5 %all-to-all-start = ((s32[32,1,6]{2,1,0:T(1,128)}), s32[32,1,6]{2,1,0:T(1,128)S(1)}, u32[]{:S(2)}, u32[]{:S(2)}) async-start(s32[32,1,6]{2,1,0:T(1,128)} %bitcast.4), calls=%async_computation | async-start | bytes 32768 | tf_op jit(solution)/shard_map/all_to_all | solution.py:71
  20.8 81.7 %all-gather.7.cloned.1.call-start = ((), (), s32[]{:S(2)}) async-start(), calls=%async_computation.5 | async-start | bytes 1179648 | tf_op jit(solution)/shard_map/all_gather | solution.py:77
  31.8 36.6 %copy-start.3 = (f32[1024]{0:T(1024)S(1)}, f32[1024]{0:T(1024)}, u32[]{:S(2)}) copy-start(f32[1024]{0:T(1024)} %param.15) | copy-start | bytes 12292
  32.9 15.9 %all-to-all-start.1 = ((bf16[32,6,1024]{2,1,0:T(8,128)(2,1)}), bf16[32,6,1024]{2,1,0:T(8,128)(2,1)S(1)}, u32[]{:S(2)}, u32[]{:S(2)}) async-start(bf16[32,6,1024]{2,1,0:T(8,128)(2,1)} %broadcast_select_fusion), calls=%async_computation.1 | async-start | bytes 1048576 | tf_op jit(solution)/shard_map/all_to_all | solution.py:73
  37.5 34.7 %copy-start.9 = (pred[128,128]{1,0:T(8,128)(4,1)}, pred[128,128]{1,0:T(8,128)(4,1)S(1)}, u32[]{:S(2)}) copy-start(pred[128,128]{1,0:T(8,128)(4,1)S(1)} %fusion.36) | copy-start | bytes 49156
  50.0 21.5 %copy-start.11 = (f32[128]{0:T(128)}, f32[128]{0:T(128)S(1)}, u32[]{:S(2)}) copy-start(f32[128]{0:T(128)S(1)} %broadcast_multiply_fusion.1) | copy-start | bytes 1540
  50.3 21.3 %copy-start.19 = (f32[128]{0:T(128)}, f32[128]{0:T(128)S(1)}, u32[]{:S(2)}) copy-start(f32[128]{0:T(128)S(1)} %fusion.18) | copy-start | bytes 1540
  50.3 21.3 %copy-start.14 = (f32[128]{0:T(128)}, f32[128]{0:T(128)S(1)}, u32[]{:S(2)}) copy-start(f32[128]{0:T(128)S(1)} %fusion.41) | copy-start | bytes 1540
  71.6 35.9 %copy-start.2 = (f32[128,2048]{1,0:T(8,128)}, f32[128,2048]{1,0:T(8,128)S(1)}, u32[]{:S(2)}) copy-start(f32[128,2048]{1,0:T(8,128)S(1)} %get-tuple-element.20) | copy-start | bytes 3145732
  71.6 30.9 %copy-start.1 = (bf16[128,1024]{1,0:T(8,128)(2,1)S(1)}, bf16[128,1024]{1,0:T(8,128)(2,1)}, u32[]{:S(2)}) copy-start(bf16[128,1024]{1,0:T(8,128)(2,1)} %param.17) | copy-start | bytes 786436
  71.6 30.9 %copy-start.16 = (f32[512]{0:T(512)S(1)}, f32[512]{0:T(512)}, u32[]{:S(2)}) copy-start(f32[512]{0:T(512)} %param.16) | copy-start | bytes 6148
  72.6 31.7 %copy-start.17 = (f32[128]{0:T(128)}, f32[128]{0:T(128)S(1)}, u32[]{:S(2)}) copy-start(f32[128]{0:T(128)S(1)} %broadcast_multiply_fusion) | copy-start | bytes 1540
  72.7 33.8 %copy-start.10 = (pred[128,128]{1,0:T(8,128)(4,1)S(1)}, pred[128,128]{1,0:T(8,128)(4,1)}, u32[]{:S(2)}) copy-start(pred[128,128]{1,0:T(8,128)(4,1)} %copy-done.9) | copy-start | bytes 49156
  72.7 34.8 %copy-start.4 = (f32[1024]{0:T(1024)S(1)}, f32[1024]{0:T(1024)}, u32[]{:S(2)}) copy-start(f32[1024]{0:T(1024)} %param.15) | copy-start | bytes 12292
  72.7 34.8 %copy-start.7 = (pred[128]{0:T(512)(128)(4,1)S(1)}, pred[128]{0:T(512)(128)(4,1)}, u32[]{:S(2)}) copy-start(pred[128]{0:T(512)(128)(4,1)} %copy-done.6) | copy-start | bytes 388
  72.7 34.8 %copy-start.12 = (f32[128]{0:T(128)S(1)}, f32[128]{0:T(128)}, u32[]{:S(2)}) copy-start(f32[128]{0:T(128)} %copy-done.11) | copy-start | bytes 1540
  114.3 24.3 %all-to-all-start.2 = ((bf16[32,6,1024]{2,1,0:T(8,128)(2,1)}), bf16[32,6,1024]{2,1,0:T(8,128)(2,1)S(1)}, u32[]{:S(2)}, u32[]{:S(2)}) async-start(bf16[32,6,1024]{2,1,0:T(8,128)(2,1)} %reshape.268), calls=%async_computation.2 | async-start | bytes 1048576 | tf_op jit(solution)/shard_map/all_to_all | solution.py:117
  126.9 283.6 %reduce-scatter.2.cloned.1.call-start = ((), (), s32[]{:S(2)}) async-start(), calls=%async_computation.6 | async-start | bytes 4718592 | tf_op jit(solution)/shard_map/reduce_scatter | solution.py:131
  154.8 5.3 %copy-start.5 = (f32[1024]{0:T(1024)S(1)}, f32[1024]{0:T(1024)}, u32[]{:S(2)}) copy-start(f32[1024]{0:T(1024)} %param.15) | copy-start | bytes 12292
  341.7 67.9 %copy-start = (bf16[512,1024]{1,0:T(8,128)(2,1)S(1)}, bf16[512,1024]{1,0:T(8,128)(2,1)}, u32[]{:S(2)}) copy-start(bf16[512,1024]{1,0:T(8,128)(2,1)} %all-gather.7.cloned.1.call-done) | copy-start | bytes 3145732
  (4 other events, 18.5 us)
Sparse Core Ops, SparseCore 0:
  9.8 58.6 all-gather.4
  70.2 32.2 all-gather.6
  150.6 49.9 reduce-scatter.1
where the time goes:
time: 422 us; the launch traced here: 419 us
  blocking collectives  206 us (49%)
  waiting for transfers between devices  76.8 us (18%)
  local copies, waits for them, and re-layouts  51.6 us (12%)
  starting transfers between devices  25.7 us (6%)
  other arithmetic  24 us (6%)
  matrix products  19.6 us (5%)
  between operations  15.7 us (4%)
    unnamed x1, blocking collectives  145 us
    reshape x6, local copies, waits for them, and re-layouts, spread(): wide_grad.transpose(1, 0, 2, 3).reshape(total_rows, gradient.shape[1])  38.1 us
    all_gather x1, waiting for transfers between devices, shards(): lax.all_gather(w_out, 'fsdp', axis=0, tiled=True)  29.8 us
    all_gather x1, blocking collectives, shards(): lax.all_gather(out_share.astype(jnp.bfloat16), 'table', axis=0, tiled=True)  24.2 us
    all_gather x1, blocking collectives, shards(): lax.all_gather(mix_share.astype(jnp.bfloat16), 'table', axis=0, tiled=True)  23.7 us
    all_gather x1, waiting for transfers between devices, shards(): lax.all_gather(w_mix, 'fsdp', axis=0, tiled=True)  18.1 us
    dot_general x3, matrix products, layer_forward(): mixture = jnp.dot(normed, w_mix, preferred_element_type=jnp.float32)  12.9 us
    all_to_all x1, starting transfers between devices, shards(): lax.all_to_all(grad_slots.reshape(owners, capacity, width_model), 'table'...  12.6 us
  transfers between devices with their start and end apart: 6, of which 5 were waited for; matrix products, arithmetic and copies ran while one was open for 16% of the time, Pallas kernels for 0%

commit v1 on v0

v1 whole, which is shorter than its diff:
```python
import jax
import jax.numpy as jnp
from jax import lax
from jax.experimental import pallas as pl
from jax.experimental.pallas import tpu as pltpu
from jax.sharding import Mesh
from jax.sharding import PartitionSpec as P

H = 4
DH = 128
MAXLEN = 64
TOK = 128
D = 1024
AW = H * DH
OWNERS = 32
CAP = 6
SLOTS = 8
NZ = 8
XY = 16
PROWS = 16
PCOLS = 640
GROWS = OWNERS * CAP + 16
TABLE = ("x", "y", "core")
ALL = ("x", "y", "core", "z")
F32 = jnp.float32
BF16 = jnp.bfloat16
MB = 1024 * 1024


def mm(a, b):
    return lax.dot_general(a, b, (((1,), (0,)), ((), ())), preferred_element_type=F32)


def mm_nt(a, b):
    return lax.dot_general(a, b, (((1,), (1,)), ((), ())), preferred_element_type=F32)


def mm_tn(a, b):
    return lax.dot_general(a, b, (((0,), (0,)), ((), ())), preferred_element_type=F32)


def iota(shape, dim):
    return lax.broadcasted_iota(jnp.int32, shape, dim)


def plan_kernel(owner_ref, row_ref, req_ref, tgt_ref):
    square = (TOK, TOK)
    lane = iota(square, 1)

    def column(values):
        return jnp.broadcast_to(values.astype(F32), square).T

    row = row_ref[...]
    owner = column(owner_ref[...])
    low, high = column(row & 127), column(row >> 7)
    onehot = owner == lane.astype(F32)
    onehot_f = onehot.astype(F32)
    onehot_b = onehot_f.astype(BF16)
    earlier = (lane < iota(square, 0)).astype(F32).astype(BF16)
    before = mm(earlier, onehot_b)
    slot = jnp.sum(before * onehot_f, axis=1, keepdims=True)
    tgt_ref[...] = (owner * SLOTS + slot).astype(jnp.int32)
    here = slot == lane.astype(F32)
    low = jnp.where(here, low, 0.0).astype(BF16)
    high = jnp.where(here, high, 0.0).astype(BF16)
    requests = mm_tn(onehot_b, low) + 128.0 * mm_tn(onehot_b, high)
    req_ref[...] = requests[:OWNERS].astype(jnp.int32)


def layer_kernel(
    lens_ref, got_ref, tgt_ref, weights_ref, gin_ref, gat_ref, ct_ref,
    out_ref, slots_ref, keep_ref, send_ref,
    wm, wo, dmx, sems,
):
    core = lax.axis_index("core")
    copies = []
    for half in range(2):
        copies.append(
            pltpu.make_async_copy(
                weights_ref.at[half, :, pl.ds(0, TOK), :], wm.at[half], sems.at[half]
            )
        )
    for half in range(2):
        copies.append(
            pltpu.make_async_copy(
                weights_ref.at[half, :, pl.ds(TOK, 32), :], wo.at[:, half], sems.at[2 + half]
            )
        )
    for copy in copies:
        copy.start()

    pick = (tgt_ref[:, :1] == iota((TOK, OWNERS * SLOTS), 1)).astype(F32).astype(BF16)
    emb = mm(pick, got_ref[...])
    gin = gin_ref[...]
    gat = gat_ref[...]
    centered = emb - jnp.mean(emb, axis=1, keepdims=True)
    rstd = lax.rsqrt(jnp.mean(centered * centered, axis=1, keepdims=True) + 1e-05)
    xhat = centered * rstd
    normed = (xhat * gin).astype(BF16)

    position, other = iota((TOK, TOK), 0), iota((TOK, TOK), 1)
    seg_row = jnp.zeros((TOK, TOK), jnp.int32)
    seg_col = jnp.zeros((TOK, TOK), jnp.int32)
    end = 0
    for user in range(lens_ref.shape[1]):
        end = end + lens_ref[0, user]
        seg_row = seg_row + (position >= end).astype(jnp.int32)
        seg_col = seg_col + (other >= end).astype(jnp.int32)
    allowed = (seg_row == seg_col) & (other <= position)

    copies[0].wait()
    wm0 = wm[0].reshape(D, D)
    mix0 = mm(normed, wm0)
    copies[1].wait()
    wm1 = wm[1].reshape(D, D)
    mix1 = mm(normed, wm1)

    sig0, sig1 = jax.nn.sigmoid(mix0), jax.nn.sigmoid(mix1)
    act0, act1 = (mix0 * sig0).astype(BF16), (mix1 * sig1).astype(BF16)
    slope0 = sig0 * (1.0 + mix0 * (1.0 - sig0))
    slope1 = sig1 * (1.0 + mix1 * (1.0 - sig1))
    gate_u = act0[:, :AW].astype(F32)

    heads = []
    attended = []
    for h in range(H):
        val = act0[:, AW + h * DH : AW + (h + 1) * DH]
        qry = act1[:, h * DH : (h + 1) * DH]
        key = act1[:, AW + h * DH : AW + (h + 1) * DH]
        score = mm_nt(qry, key) * DH ** (-0.5)
        sig = jax.nn.sigmoid(score)
        wgt = (jnp.where(allowed, score * sig, 0.0) / MAXLEN).astype(BF16)
        attended.append(mm(wgt, val).astype(BF16))
        slope = jnp.where(allowed, sig * (1.0 + score * (1.0 - sig)), 0.0) * (
            DH ** (-0.5) / MAXLEN
        )
        heads.append((val, qry, key, wgt, slope))
    att = jnp.concatenate(attended, axis=1).astype(F32)
    acent = att - jnp.mean(att, axis=1, keepdims=True)
    arstd = lax.rsqrt(jnp.mean(acent * acent, axis=1, keepdims=True) + 1e-05)
    ahat = acent * arstd
    scaled = ahat * gat
    gated = (scaled * gate_u).astype(BF16)

    copies[2].wait()
    copies[3].wait()
    w_out = wo[...].reshape(AW, D)
    ct = ct_ref[...]
    out_ref[...] = (emb + mm(gated, w_out)).astype(BF16)

    d_gated = mm_nt(ct, w_out).astype(BF16).astype(F32)
    d_gate = (d_gated * scaled).astype(BF16).astype(F32)
    d_ahat = d_gated * gate_u * gat
    d_att = arstd * (
        d_ahat
        - jnp.mean(d_ahat, axis=1, keepdims=True)
        - ahat * jnp.mean(d_ahat * ahat, axis=1, keepdims=True)
    )
    d_att = d_att.astype(BF16)
    d_val, d_qry, d_key = [], [], []
    for h in range(H):
        val, qry, key, wgt, slope = heads[h]
        d_head = d_att[:, h * DH : (h + 1) * DH]
        d_wgt = mm_nt(d_head, val).astype(BF16).astype(F32)
        d_val.append(mm_tn(wgt, d_head).astype(BF16))
        d_score = (d_wgt * slope).astype(BF16)
        d_qry.append(mm(d_score, key).astype(BF16))
        d_key.append(mm_tn(d_score, qry).astype(BF16))
    d_act0 = jnp.concatenate([d_gate] + [v.astype(F32) for v in d_val], axis=1)
    d_act1 = jnp.concatenate([v.astype(F32) for v in d_qry + d_key], axis=1)
    d_mix0 = (d_act0 * slope0).astype(BF16)
    d_mix1 = (d_act1 * slope1).astype(BF16)
    dmx[0] = d_mix0
    dmx[1] = d_mix1
    d_normed = (mm_nt(d_mix0, wm0) + mm_nt(d_mix1, wm1)).astype(BF16).astype(F32)
    d_xhat = d_normed * gin
    d_emb = (
        rstd
        * (
            d_xhat
            - jnp.mean(d_xhat, axis=1, keepdims=True)
            - xhat * jnp.mean(d_xhat * xhat, axis=1, keepdims=True)
        )
        + ct.astype(F32)
    ).astype(BF16)
    slots_ref[...] = mm_tn(pick, d_emb).astype(BF16)

    for side, dst in ((1 - core, send_ref), (core, keep_ref)):
        d_mix = dmx[side]
        ct_half = ct_ref[:, pl.ds(pl.multiple_of(side * AW, AW), AW)]
        for z in range(NZ):
            grad = mm_tn(normed[:, z * TOK : (z + 1) * TOK], d_mix).astype(BF16)
            for g in range(8):
                for c in range(2):
                    dst[g * 2 + c, z, :, 0:512] = grad[
                        g * PROWS : (g + 1) * PROWS, c * 512 : (c + 1) * 512
                    ]
        for pair in range(NZ // 2):
            grad = mm_tn(gated[:, pair * TOK : (pair + 1) * TOK], ct_half).astype(BF16)
            for sub in range(2):
                for r in range(4):
                    for c in range(4):
                        dst[r * 4 + c, pair * 2 + sub, :, 512:PCOLS] = grad[
                            sub * 64 + r * PROWS : sub * 64 + (r + 1) * PROWS,
                            c * 128 : (c + 1) * 128,
                        ]


def pack_kernel(rows_ref, asked_ref, out_ref):
    used = OWNERS * CAP
    r, k = iota((used, OWNERS * SLOTS), 0), iota((used, OWNERS * SLOTS), 1)
    take = (r // CAP == k // SLOTS) & (r % CAP == k % SLOTS)
    out_ref[:used] = mm(take.astype(F32).astype(BF16), rows_ref[...]).astype(BF16)
    asked = asked_ref[...]
    owner = (iota((256, OWNERS), 0) // CAP == iota((256, OWNERS), 1)).astype(F32).astype(BF16)
    slot = iota((256, 128), 0) % CAP == iota((256, 128), 1)
    parts = []
    for part in (asked & 127, asked >> 7):
        spread = mm(owner, part.astype(F32).astype(BF16))
        column = jnp.sum(jnp.where(slot, spread, 0.0), axis=1, keepdims=True)
        parts.append(jnp.broadcast_to(column, (256, 128)).T[:PROWS])
    which = iota((PROWS, 256), 0)
    numbers = jnp.where(which == 0, parts[0], jnp.where(which == 1, parts[1], 0.0))
    out_ref[used:] = jnp.concatenate(
        [numbers.astype(BF16), jnp.zeros((PROWS, D - 256), BF16)], axis=1
    )


def table_kernel(rows_ref, out_ref):
    used = OWNERS * CAP
    first = lax.axis_index("z") * 256
    total = jnp.zeros((256, D), F32)
    for z in range(NZ):
        low = rows_ref[z, used : used + PROWS, :256].astype(F32)
        number = (low[0:1] + 128.0 * low[1:2]).astype(jnp.int32)[:, :used] - first
        here = (iota((256, used), 0) == number).astype(F32).astype(BF16)
        total = total + mm(here, rows_ref[z, :used])
    out_ref[...] = total


def square_kernel(sums_ref, out_ref):
    sums = sums_ref[...].astype(F32)
    sq = sums * sums
    mix = jnp.sum(sq[:, :, :512])
    out = jnp.sum(sq[:, :, 512:])
    lane = iota((NZ, 8, 128), 2)
    out_ref[...] = jnp.where(lane == 0, mix, jnp.where(lane == 1, out, 0.0))


def scale_kernel(sums_ref, squares_ref, mix_ref, out_ref):
    total = jnp.sum(squares_ref[...], axis=0)[0:1]
    mix_sq, out_sq = total[:, 0:1], total[:, 1:2]
    mix_scale = jnp.minimum(1.0, 1.0 / jnp.sqrt(mix_sq / float(D * 4 * AW) + 1e-06))
    out_scale = jnp.minimum(1.0, 1.0 / jnp.sqrt(out_sq / float(D * AW) + 1e-06))
    for core in range(2):
        for g in range(8):
            for c in range(2):
                mix_ref[
                    g * PROWS : (g + 1) * PROWS, core * D + c * 512 : core * D + (c + 1) * 512
                ] = sums_ref[(g * 2 + c) * 2 + core, :, 0:512].astype(F32) * mix_scale
        for r in range(4):
            for c in range(4):
                out_ref[
                    r * PROWS : (r + 1) * PROWS, core * AW + c * 128 : core * AW + (c + 1) * 128
                ] = sums_ref[(r * 4 + c) * 2 + core, :, 512:PCOLS].astype(F32) * out_scale


def vmem():
    return pl.BlockSpec(memory_space=pltpu.VMEM)


def call(body, outs, args, specs=None, **kwargs):
    shapes = [jax.ShapeDtypeStruct(s, t) for s, t in outs]
    one = len(shapes) == 1
    return pl.pallas_call(
        body,
        out_shape=shapes[0] if one else shapes,
        in_specs=specs or [vmem()] * len(args),
        out_specs=vmem() if one else [vmem()] * len(shapes),
        **kwargs,
    )(*args)


def exchange(array, axes):
    return lax.all_to_all(array, axes, split_axis=0, concat_axis=0, tiled=True)


def shards(
    item_table, item_row, item_owner, user_lengths, w_mix, w_out, gain_in, gain_attn, cotangent
):
    core = lax.axis_index("core")
    share = jnp.concatenate(
        [
            lax.dynamic_slice(w_mix, (0, core * D), (TOK, D)),
            lax.dynamic_slice(w_out, (core * 32, 0), (32, D)),
        ],
        axis=0,
    )
    weights = lax.all_gather(share, ("core", "z"), axis=0, tiled=True).reshape(2, NZ, 160, D)

    requests, target = call(
        plan_kernel,
        [((OWNERS, 128), jnp.int32), ((TOK, TOK), jnp.int32)],
        (item_owner.reshape(1, TOK), item_row.reshape(1, TOK)),
    )
    asked = exchange(requests, TABLE)
    wanted = asked[:, :SLOTS].reshape(OWNERS * SLOTS)
    found = item_table.at[wanted].get(mode="promise_in_bounds")
    got = exchange(found.reshape(OWNERS, SLOTS, D), TABLE)

    smem = pl.BlockSpec(memory_space=pltpu.SMEM)
    anywhere = pl.BlockSpec(memory_space=pl.ANY)
    piece = (XY, NZ, PROWS, PCOLS)
    layer_out, grad_slots, keep, send = call(
        layer_kernel,
        [((TOK, D), BF16), ((OWNERS * SLOTS, D), BF16), (piece, BF16), (piece, BF16)],
        (
            user_lengths,
            got.reshape(OWNERS * SLOTS, D),
            target,
            weights,
            gain_in.reshape(1, D),
            gain_attn.reshape(1, AW),
            cotangent,
        ),
        specs=[smem, vmem(), vmem(), anywhere, vmem(), vmem(), vmem()],
        scratch_shapes=[
            pltpu.VMEM((2, NZ, TOK, D), BF16),
            pltpu.VMEM((NZ, 2, 32, D), BF16),
            pltpu.VMEM((2, TOK, D), BF16),
            pltpu.SemaphoreType.DMA((4,)),
        ],
        compiler_params=pltpu.CompilerParams(vmem_limit_bytes=40 * MB),
    )

    theirs = lax.ppermute(send, "core", [(0, 1), (1, 0)])
    pair_sum = (keep.astype(F32) + theirs.astype(F32)).astype(BF16)
    plane = exchange(pair_sum, ("x", "y"))
    plane_sum = jnp.sum(plane.astype(F32), axis=0).astype(BF16)
    column = exchange(plane_sum, "z")
    whole = jnp.sum(column.astype(F32), axis=0).astype(BF16)
    sums = exchange(jnp.broadcast_to(whole[None], (OWNERS, PROWS, PCOLS)), TABLE)
    squares = call(square_kernel, [((NZ, 8, 128), F32)], (sums,))
    squares = exchange(squares, "z")
    mix_grad, out_grad = call(
        scale_kernel, [((TOK, 4 * AW), F32), ((64, D), F32)], (sums, squares)
    )

    received = exchange(grad_slots.reshape(OWNERS, SLOTS, D), TABLE)
    packed = call(
        pack_kernel, [((GROWS, D), BF16)], (received.reshape(OWNERS * SLOTS, D), asked)
    )
    gathered = lax.all_gather(packed, "z", axis=0, tiled=True).reshape(NZ, GROWS, D)
    table_grad = call(
        table_kernel,
        [((256, D), F32)],
        (gathered,),
        compiler_params=pltpu.CompilerParams(vmem_limit_bytes=40 * MB),
    )
    return (layer_out, table_grad, mix_grad, out_grad)


def solution(mesh):
    cube = Mesh(mesh.devices.reshape(4, 4, 2, 8), ALL)
    in_specs = (
        P(TABLE, None),
        P(ALL),
        P(ALL, None),
        P(ALL, None),
        P("z", None),
        P("z", None),
        P(),
        P(),
        P(ALL, None),
    )
    out_specs = (
        P(ALL, None),
        P(ALL, None),
        P("z", None),
        P("z", None),
    )
    return jax.shard_map(shards, mesh=cube, in_specs=in_specs, out_specs=out_specs, check_vma=False)
```

time: 422 us -> 189 us (0.45)
  blocking collectives: 206 us -> 128 us
  waiting for transfers between devices: 76.8 us -> 11.5 us
  local copies, waits for them, and re-layouts: 51.6 us -> 11 us
  starting transfers between devices: 25.7 us -> 0.43 us
  other arithmetic: 24 us -> 3.68 us
  matrix products: 19.6 us -> 0 us
  Pallas kernels: 0 us -> 19.2 us
    unnamed x1 -> x0, blocking collectives: 145 us -> none
    all_to_all x0 -> x7, blocking collectives: none -> 128 us  [exchange(): return lax.all_to_all(array, axes, split_axis=0, concat_axis=0, tiled=True)]
    all_gather x2 -> x0, blocking collectives: 47.9 us -> none  [the longest x1 24.2 us: shards(): lax.all_gather(out_share.astype(jnp.bfloat16), 'table', axis=0, tiled=True)]
    reshape x15 -> x1, local copies, waits for them, and re-layouts: 39.9 us -> 0.09 us  [shards(): wanted = asked[:, :SLOTS].reshape(OWNERS * SLOTS)]
    all_gather x2, waiting for transfers between devices: 47.9 us -> 11.5 us  [the longest x1 11.5 us: shards(): lax.all_gather(share, ('core', 'z'), axis=0, tiled=True)]
    all_to_all x3 -> x0, waiting for transfers between devices: 27.5 us -> none  [the longest x1 11.3 us: shards(): lax.all_to_all(found_rows, 'table', split_axis=0, concat_axis=0, tiled=True)]
    all_to_all x3 -> x0, starting transfers between devices: 25.4 us -> none  [the longest x1 12.6 us: shards(): lax.all_to_all(grad_slots.reshape(owners, capacity, width_model), 'table'...]
    dot_general x12 -> x0, matrix products: 19.6 us -> none  [the longest x3 12.9 us: layer_forward(): mixture = jnp.dot(normed, w_mix, preferred_element_type=jnp.float32)]
  transfers between devices with their start and end apart: 6 -> 3, of which waited for: 5 -> 1; matrix products, arithmetic and copies ran while one was open for 16% -> 4% of each run, Pallas kernels for 0% -> 4%
where the time goes in v1:
time: 189 us; the launch traced here: 188 us
  blocking collectives  128 us (68%)
  Pallas kernels  19.2 us (10%)
  between operations  14.2 us (8%)
  waiting for transfers between devices  11.5 us (6%)
  local copies, waits for them, and re-layouts  11 us (6%)
  other arithmetic  3.68 us (2%)
    all_to_all x7, blocking collectives, exchange(): return lax.all_to_all(array, axes, split_axis=0, concat_axis=0, tiled=True)  128 us
    pallas_call x6, Pallas kernels, call(): pl.pallas_call(body, out_shape=shapes[0] if one else shapes, in_specs=spe...  19.2 us
    all_gather x1, waiting for transfers between devices, shards(): lax.all_gather(share, ('core', 'z'), axis=0, tiled=True)  11.5 us
    unnamed x20, local copies, waits for them, and re-layouts  5.64 us
    gather x1, local copies, waits for them, and re-layouts, shards(): found = item_table.at[wanted].get(mode='promise_in_bounds')  4.32 us
  transfers between devices with their start and end apart: 3, of which 1 were waited for; matrix products, arithmetic and copies ran while one was open for 4% of the time, Pallas kernels for 4%

profile of v1, /device:TPU:1, one launch (start us, length us, event | category | flops | bytes accessed | tf_op | source)
XLA Modules:
  0.0 188.4 jit_solution(9383111063502557188)
XLA Ops:
  7.2 0.9 constant_dynamic-slice_fusion
  8.1 0.1 copy-done
  8.3 0.7 pad_maximum_fusion
  9.1 1.7 shard_map.120
  10.8 15.5 %all_to_all.41 = s32[32,1,128]{2,1,0:T(1,128)S(1)} all-to-all(s32[32,1,128]{2,1,0:T(1,128)} %bitcast.26), channel_id=1, replica_groups=mesh['x'=4,'y'=4,'core'=2,'z'=8] {'x','y','core'}, dimensions={0} | all-to-all | bytes 32768 | tf_op jit(solution)/shard_map/all_to_all | solution.py:285
  26.4 4.3 %gather_fusion = bf16[256,1024]{1,0:T(8,128)(2,1)S(1)} fusion(bf16[2048,1024]{1,0:T(8,128)(2,1)} %param.9, s32[1024]{0:T(1024)S(1)} %pad_clamp_fusion), kind=kCustom, calls=%fused_computation | custom fusion | bytes 1049600 | tf_op jit(solution)/shard_map/gather | solution.py:308
  30.8 15.7 %all_to_all.42 = bf16[32,8,1024]{2,1,0:T(8,128)(2,1)} all-to-all(bf16[32,8,1024]{2,1,0:T(8,128)(2,1)S(1)} %bitcast.22), channel_id=1, replica_groups=mesh['x'=4,'y'=4,'core'=2,'z'=8] {'x','y','core'}, dimensions={0} | all-to-all | bytes 1048576 | tf_op jit(solution)/shard_map/all_to_all | solution.py:285
  46.5 11.5 %all-gather.3.cloned.1.call-done = bf16[2560,1024]{1,0:T(8,128)(2,1)} async-done(((bf16[160,1024]{1,0:T(8,128)(2,1)}), bf16[2560,1024]{1,0:T(8,128)(2,1)}) %all-gather.3.cloned.1.call-update) | async-done | bytes 5242896 | tf_op jit(solution)/shard_map/all_gather | solution.py:299
  58.0 2.5 %copy-done.1 = bf16[2560,1024]{1,0:T(8,128)(2,1)S(1)} copy-done((bf16[2560,1024]{1,0:T(8,128)(2,1)S(1)}, bf16[2560,1024]{1,0:T(8,128)(2,1)}, u32[]{:S(2)}) %copy-start.1) | copy-done | bytes 5242904
  60.5 1.0 copy-done.3
  61.5 8.6 %shard_map.121 = (bf16[128,1024]{1,0:T(8,128)(2,1)}, bf16[256,1024]{1,0:T(8,128)(2,1)S(1)}, bf16[16,8,16,640]{3,2,1,0:T(8,128)(2,1)S(1)}, bf16[16,8,16,640]{3,2,1,0:T(8,128)(2,1)}) custom-call(s32[1,8]{1,0:T(1,128)S(1)} %copy-done.8, bf16[256,1024]{1,0:T(8,128)(2,1)S(1)} %bitcast.18, s32[128,128]{1,0:T(8,128)S(1)} %copy-done.5, ...), custom_call_target="tpu_custom_call" | custom-call | tf_op jit(solution)/shard_map/pallas_call | solution.py:275
  70.1 0.3 collective-permute-start
  70.5 18.5 %all_to_all.43 = bf16[32,8,1024]{2,1,0:T(8,128)(2,1)} all-to-all(bf16[32,8,1024]{2,1,0:T(8,128)(2,1)S(1)} %bitcast.19), channel_id=1, replica_groups=mesh['x'=4,'y'=4,'core'=2,'z'=8] {'x','y','core'}, dimensions={0} | all-to-all | bytes 1048576 | tf_op jit(solution)/shard_map/all_to_all | solution.py:285
  89.0 2.3 %shard_map.122 = bf16[208,1024]{1,0:T(8,128)(2,1)} custom-call(bf16[256,1024]{1,0:T(8,128)(2,1)} %bitcast.23, s32[32,128]{1,0:T(8,128)} %bitcast.25), custom_call_target="tpu_custom_call" | custom-call | tf_op jit(solution)/shard_map/pallas_call | solution.py:275
  91.3 2.5 %add_convert_fusion = bf16[16,8,16,640]{3,2,1,0:T(8,128)(2,1)S(1)} fusion(bf16[16,8,16,640]{3,2,1,0:T(8,128)(2,1)} %collective-permute-done, bf16[16,8,16,640]{3,2,1,0:T(8,128)(2,1)S(1)} %get-tuple-element.16), kind=kLoop, calls=%fused_computation.1 | loop fusion | flops 5242880 | bytes 7864320 | tf_op jit(solution)/shard_map/convert_element_type | solution.py:337
  93.8 35.6 %all_to_all.44 = bf16[16,8,16,640]{3,2,1,0:T(8,128)(2,1)S(1)} all-to-all(bf16[16,8,16,640]{3,2,1,0:T(8,128)(2,1)S(1)} %add_convert_fusion), channel_id=1, replica_groups=mesh['x'=4,'y'=4,'core'=2,'z'=8] {'x','y'}, dimensions={0} | all-to-all | bytes 5242880 | tf_op jit(solution)/shard_map/all_to_all | solution.py:285
  129.5 0.4 reduce_sum.24
  129.9 12.5 %all_to_all.45 = bf16[8,16,640]{2,1,0:T(8,128)(2,1)S(1)} all-to-all(bf16[8,16,640]{2,1,0:T(8,128)(2,1)S(1)} %reduce_sum.24), channel_id=1, replica_groups=mesh['x'=4,'y'=4,'core'=2,'z'=8] {'z'}, dimensions={0} | all-to-all | bytes 327680 | tf_op jit(solution)/shard_map/all_to_all | solution.py:285
  142.5 19.8 %all_to_all.46.sums_ref = bf16[32,16,640]{2,1,0:T(8,128)(2,1)} all-to-all(bf16[32,16,640]{2,1,0:T(8,128)(2,1)S(1)} %broadcast_in_dim.2), channel_id=1, replica_groups=mesh['x'=4,'y'=4,'core'=2,'z'=8] {'x','y','core'}, dimensions={0} | all-to-all | bytes 1310720 | tf_op jit(solution)/shard_map/all_to_all | solution.py:285
  162.3 2.1 %shard_map.124 = f32[8,8,128]{2,1,0:T(8,128)} custom-call(bf16[32,16,640]{2,1,0:T(8,128)(2,1)} %all_to_all.46.sums_ref), custom_call_target="tpu_custom_call" | custom-call | tf_op jit(solution)/shard_map/pallas_call | solution.py:275
  164.4 10.8 %all_to_all.47.squares_ref = f32[8,8,128]{2,1,0:T(8,128)} all-to-all(f32[8,8,128]{2,1,0:T(8,128)} %shard_map.124), channel_id=1, replica_groups=mesh['x'=4,'y'=4,'core'=2,'z'=8] {'z'}, dimensions={0} | all-to-all | bytes 65536 | tf_op jit(solution)/shard_map/all_to_all | solution.py:285
  175.1 2.3 %shard_map.125 = (f32[128,2048]{1,0:T(8,128)}, f32[64,1024]{1,0:T(8,128)}) custom-call(bf16[32,16,640]{2,1,0:T(8,128)(2,1)} %all_to_all.46.sums_ref, f32[8,8,128]{2,1,0:T(8,128)} %all_to_all.47.squares_ref), custom_call_target="tpu_custom_call" | custom-call | tf_op jit(solution)/shard_map/pallas_call | solution.py:275
  177.4 2.0 %copy-done.2 = bf16[1664,1024]{1,0:T(8,128)(2,1)S(1)} copy-done((bf16[1664,1024]{1,0:T(8,128)(2,1)S(1)}, bf16[1664,1024]{1,0:T(8,128)(2,1)}, u32[]{:S(2)}) %copy-start.2) | copy-done | bytes 3407896
  179.4 2.2 %shard_map.123 = f32[256,1024]{1,0:T(8,128)} custom-call(bf16[8,208,1024]{2,1,0:T(8,128)(2,1)S(1)} %bitcast.17), custom_call_target="tpu_custom_call" | custom-call | tf_op jit(solution)/shard_map/pallas_call | solution.py:275
  (28 shorter events, 0.4 us)
Async XLA Ops:
  7.2 1.1 copy-start
  7.2 50.8 %all-gather.3.cloned.1.call-start = ((), (), s32[]{:S(2)}) async-start(), calls=%async_computation.7 | async-start | bytes 5570560 | tf_op jit(solution)/shard_map/all_gather | solution.py:299
  9.0 168.4 %all-gather.5.cloned.1.call-start = ((), (), s32[]{:S(2)}) async-start(), calls=%async_computation.8 | async-start | bytes 3833856 | tf_op jit(solution)/shard_map/all_gather | solution.py:353
  26.3 20.2 %copy-start.9 = (s32[32,1,128]{2,1,0:T(1,128)}, s32[32,1,128]{2,1,0:T(1,128)S(1)}, u32[]{:S(2)}) copy-start(s32[32,1,128]{2,1,0:T(1,128)S(1)} %all_to_all.41) | copy-start | bytes 49156
  26.4 31.6 %copy-start.4 = (bf16[128,1024]{1,0:T(8,128)(2,1)S(1)}, bf16[128,1024]{1,0:T(8,128)(2,1)}, u32[]{:S(2)}) copy-start(bf16[128,1024]{1,0:T(8,128)(2,1)} %ct_ref.1) | copy-start | bytes 786436
  26.4 31.6 %copy-start.5 = (s32[128,128]{1,0:T(8,128)S(1)}, s32[128,128]{1,0:T(8,128)}, u32[]{:S(2)}) copy-start(s32[128,128]{1,0:T(8,128)} %get-tuple-element.13.tgt_ref) | copy-start | bytes 196612
  26.4 31.6 %copy-start.6 = (f32[1024]{0:T(1024)S(1)}, f32[1024]{0:T(1024)}, u32[]{:S(2)}) copy-start(f32[1024]{0:T(1024)} %param.15) | copy-start | bytes 12292
  26.4 31.6 %copy-start.7 = (f32[512]{0:T(512)S(1)}, f32[512]{0:T(512)}, u32[]{:S(2)}) copy-start(f32[512]{0:T(512)} %param.16) | copy-start | bytes 6148
  26.4 31.6 %copy-start.8 = (s32[1,8]{1,0:T(1,128)S(1)}, s32[1,8]{1,0:T(1,128)}, u32[]{:S(2)}) copy-start(s32[1,8]{1,0:T(1,128)} %lens_ref.1) | copy-start | bytes 100
  58.0 2.5 %copy-start.1 = (bf16[2560,1024]{1,0:T(8,128)(2,1)S(1)}, bf16[2560,1024]{1,0:T(8,128)(2,1)}, u32[]{:S(2)}) copy-start(bf16[2560,1024]{1,0:T(8,128)(2,1)} %all-gather.3.cloned.1.call-done) | copy-start | bytes 15728644
  60.5 1.0 copy-start.3
  70.1 21.2 %collective-permute-start = (bf16[16,8,16,640]{3,2,1,0:T(8,128)(2,1)}, bf16[16,8,16,640]{3,2,1,0:T(8,128)(2,1)}, u32[]{:S(2)}, u32[]{:S(2)}) collective-permute-start(bf16[16,8,16,640]{3,2,1,0:T(8,128)(2,1)} %get-tuple-element.17), channel_id=1, source_target_pairs={{0,8},{8,0},{1,9},{9,1},{2,10},{10,2},{3,11},{11,3},{4,12},{12,4},... | collective-permute-start | bytes 7864328 | tf_op jit(solution)/shard_map/ppermute | solution.py:336
  177.4 2.0 %copy-start.2 = (bf16[1664,1024]{1,0:T(8,128)(2,1)S(1)}, bf16[1664,1024]{1,0:T(8,128)(2,1)}, u32[]{:S(2)}) copy-start(bf16[1664,1024]{1,0:T(8,128)(2,1)} %all-gather.5.cloned.1.call-done) | copy-start | bytes 10223620
Sparse Core Ops, SparseCore 0:
  10.4 47.5 all-gather.2
  91.4 42.4 all-gather.4

commit v2 on v1

--- a/solution.py
+++ b/solution.py
@@ -206,7 +206,7 @@
                         ]
 
 
-def pack_kernel(rows_ref, asked_ref, out_ref):
+def pack_kernel(rows_ref, asked_ref, after_ref, out_ref):
     used = OWNERS * CAP
     r, k = iota((used, OWNERS * SLOTS), 0), iota((used, OWNERS * SLOTS), 1)
     take = (r // CAP == k // SLOTS) & (r % CAP == k % SLOTS)
@@ -247,7 +247,7 @@
     out_ref[...] = jnp.where(lane == 0, mix, jnp.where(lane == 1, out, 0.0))
 
 
-def scale_kernel(sums_ref, squares_ref, mix_ref, out_ref):
+def scale_kernel(sums_ref, squares_ref, after_ref, mix_ref, out_ref):
     total = jnp.sum(squares_ref[...], axis=0)[0:1]
     mix_sq, out_sq = total[:, 0:1], total[:, 1:2]
     mix_scale = jnp.minimum(1.0, 1.0 / jnp.sqrt(mix_sq / float(D * 4 * AW) + 1e-06))
@@ -279,6 +279,10 @@
         out_specs=vmem() if one else [vmem()] * len(shapes),
         **kwargs,
     )(*args)
+
+
+def cost(us):
+    return pl.CostEstimate(flops=0, bytes_accessed=int(us * 3.0e6), transcendentals=0)
 
 
 def exchange(array, axes):
@@ -330,33 +334,45 @@
             pltpu.VMEM((2, TOK, D), BF16),
             pltpu.SemaphoreType.DMA((4,)),
         ],
-        compiler_params=pltpu.CompilerParams(vmem_limit_bytes=40 * MB),
+        cost_estimate=cost(9),
+        compiler_params=pltpu.CompilerParams(vmem_limit_bytes=60 * MB),
     )
 
     theirs = lax.ppermute(send, "core", [(0, 1), (1, 0)])
     pair_sum = (keep.astype(F32) + theirs.astype(F32)).astype(BF16)
+    added = pair_sum[0, 0, :, :128]
     plane = exchange(pair_sum, ("x", "y"))
     plane_sum = jnp.sum(plane.astype(F32), axis=0).astype(BF16)
     column = exchange(plane_sum, "z")
     whole = jnp.sum(column.astype(F32), axis=0).astype(BF16)
     sums = exchange(jnp.broadcast_to(whole[None], (OWNERS, PROWS, PCOLS)), TABLE)
-    squares = call(square_kernel, [((NZ, 8, 128), F32)], (sums,))
-    squares = exchange(squares, "z")
-    mix_grad, out_grad = call(
-        scale_kernel, [((TOK, 4 * AW), F32), ((64, D), F32)], (sums, squares)
-    )
-
     received = exchange(grad_slots.reshape(OWNERS, SLOTS, D), TABLE)
     packed = call(
-        pack_kernel, [((GROWS, D), BF16)], (received.reshape(OWNERS * SLOTS, D), asked)
+        pack_kernel,
+        [((GROWS, D), BF16)],
+        (received.reshape(OWNERS * SLOTS, D), asked, added),
+        specs=[vmem(), vmem(), anywhere],
+        cost_estimate=cost(2),
+        compiler_params=pltpu.CompilerParams(vmem_limit_bytes=16 * MB),
     )
     gathered = lax.all_gather(packed, "z", axis=0, tiled=True).reshape(NZ, GROWS, D)
     table_grad = call(
         table_kernel,
         [((256, D), F32)],
         (gathered,),
-        compiler_params=pltpu.CompilerParams(vmem_limit_bytes=40 * MB),
-    )
+        cost_estimate=cost(2),
+        compiler_params=pltpu.CompilerParams(vmem_limit_bytes=60 * MB),
+    )
+    squares = call(square_kernel, [((NZ, 8, 128), F32)], (sums,))
+    squares = exchange(squares, "z")
+    mix_grad, out_grad = call(
+        scale_kernel,
+        [((TOK, 4 * AW), F32), ((64, D), F32)],
+        (sums, squares, table_grad),
+        specs=[vmem(), vmem(), anywhere],
+        cost_estimate=cost(2),
+    )
+
     return (layer_out, table_grad, mix_grad, out_grad)
 
 

time: 189 us -> 181 us (0.958)
  blocking collectives: 128 us -> 100 us
  starting transfers between devices: 0.43 us -> 10.9 us
  waiting for transfers between devices: 11.5 us -> 21 us
  local copies, waits for them, and re-layouts: 11 us -> 7.55 us
  Pallas kernels: 19.2 us -> 22.5 us
    all_to_all x7 -> x5, blocking collectives: 128 us -> 100 us  [exchange(): return lax.all_to_all(array, axes, split_axis=0, concat_axis=0, tiled=True)]
    all_to_all x0 -> x2, starting transfers between devices: none -> 10.4 us  [exchange(): return lax.all_to_all(array, axes, split_axis=0, concat_axis=0, tiled=True)]
    all_to_all x0 -> x2, waiting for transfers between devices: none -> 9.27 us  [exchange(): return lax.all_to_all(array, axes, split_axis=0, concat_axis=0, tiled=True)]
    unnamed x20 -> x6, local copies, waits for them, and re-layouts: 5.64 us -> 2.21 us
    pallas_call x6, Pallas kernels: 19.2 us -> 22.5 us  [call(): pl.pallas_call(body, out_shape=shapes[0] if one else shapes, in_specs=spe...]
  transfers between devices with their start and end apart: 3 -> 5, of which waited for: 1 -> 3; matrix products, arithmetic and copies ran while one was open for 4% -> 5% of each run, Pallas kernels for 4% -> 4%
where the time goes in v2:
time: 181 us
  blocking collectives  100 us (55%)
  Pallas kernels  22.5 us (12%)
  waiting for transfers between devices  21 us (12%)
  between operations  14.2 us (8%)
  starting transfers between devices  10.9 us (6%)
  local copies, waits for them, and re-layouts  7.55 us (4%)
  other arithmetic  4.48 us (2%)
    all_to_all x5, blocking collectives, exchange(): return lax.all_to_all(array, axes, split_axis=0, concat_axis=0, tiled=True)  100 us
    pallas_call x6, Pallas kernels, call(): pl.pallas_call(body, out_shape=shapes[0] if one else shapes, in_specs=spe...  22.5 us
    all_gather x1, waiting for transfers between devices, shards(): lax.all_gather(share, ('core', 'z'), axis=0, tiled=True)  11.6 us
    all_to_all x2, starting transfers between devices, exchange(): return lax.all_to_all(array, axes, split_axis=0, concat_axis=0, tiled=True)  10.4 us
    all_to_all x2, waiting for transfers between devices, exchange(): return lax.all_to_all(array, axes, split_axis=0, concat_axis=0, tiled=True)  9.27 us
    gather x1, local copies, waits for them, and re-layouts, shards(): found = item_table.at[wanted].get(mode='promise_in_bounds')  4.29 us
  transfers between devices with their start and end apart: 5, of which 3 were waited for; matrix products, arithmetic and copies ran while one was open for 5% of the time, Pallas kernels for 4%

profile of v2, /device:TPU:1, one launch (start us, length us, event | category | flops | bytes accessed | tf_op | source)
XLA Modules:
  0.0 180.8 jit_solution(5658508586461623641)
XLA Ops:
  7.2 0.9 constant_dynamic-slice_fusion
  8.3 0.7 pad_maximum_fusion
  9.0 1.7 shard_map.120
  10.8 15.5 %all_to_all.41 = s32[32,1,128]{2,1,0:T(1,128)S(1)} all-to-all(s32[32,1,128]{2,1,0:T(1,128)} %bitcast.26), channel_id=1, replica_groups=mesh['x'=4,'y'=4,'core'=2,'z'=8] {'x','y','core'}, dimensions={0} | all-to-all | bytes 32768 | tf_op jit(solution)/shard_map/all_to_all | solution.py:289
  26.3 4.3 %gather_fusion = bf16[256,1024]{1,0:T(8,128)(2,1)S(1)} fusion(bf16[2048,1024]{1,0:T(8,128)(2,1)} %param.9, s32[1024]{0:T(1024)S(1)} %pad_clamp_fusion), kind=kCustom, calls=%fused_computation | custom fusion | bytes 1049600 | tf_op jit(solution)/shard_map/gather | solution.py:312
  30.6 15.7 %all_to_all.42 = bf16[32,8,1024]{2,1,0:T(8,128)(2,1)} all-to-all(bf16[32,8,1024]{2,1,0:T(8,128)(2,1)S(1)} %bitcast.24), channel_id=1, replica_groups=mesh['x'=4,'y'=4,'core'=2,'z'=8] {'x','y','core'}, dimensions={0} | all-to-all | bytes 1048576 | tf_op jit(solution)/shard_map/all_to_all | solution.py:289
  46.3 11.6 %all-gather.3.cloned.1.call-done = bf16[2560,1024]{1,0:T(8,128)(2,1)} async-done(((bf16[160,1024]{1,0:T(8,128)(2,1)}), bf16[2560,1024]{1,0:T(8,128)(2,1)}) %all-gather.3.cloned.1.call-update) | async-done | bytes 5242896 | tf_op jit(solution)/shard_map/all_gather | solution.py:303
  58.0 11.0 %shard_map.121 = (bf16[128,1024]{1,0:T(8,128)(2,1)}, bf16[256,1024]{1,0:T(8,128)(2,1)}, bf16[16,8,16,640]{3,2,1,0:T(8,128)(2,1)}, bf16[16,8,16,640]{3,2,1,0:T(8,128)(2,1)}) custom-call(s32[1,8]{1,0:T(1,128)} %lens_ref.1, bf16[256,1024]{1,0:T(8,128)(2,1)} %bitcast.23, s32[128,128]{1,0:T(8,128)} %get-tuple-element.13.tgt_ref, ...), custom_call_target="tpu_custom_call" | custom-call | bytes 27000000 | tf_op jit(solution)/shard_map/pallas_call | solution.py:275
  69.0 0.3 collective-permute-start
  69.4 7.1 %all-to-all-start.2 = ((bf16[32,8,1024]{2,1,0:T(8,128)(2,1)}), bf16[32,8,1024]{2,1,0:T(8,128)(2,1)S(1)}, u32[]{:S(2)}, u32[]{:S(2)}) async-start(bf16[32,8,1024]{2,1,0:T(8,128)(2,1)} %bitcast.25), calls=%async_computation.2 | async-start | bytes 1048576 | tf_op jit(solution)/shard_map/all_to_all | solution.py:289
  76.5 3.3 %add_convert_fusion = bf16[16,8,16,640]{3,2,1,0:T(8,128)(2,1)S(1)} fusion(bf16[16,8,16,640]{3,2,1,0:T(8,128)(2,1)} %collective-permute-done, bf16[16,8,16,640]{3,2,1,0:T(8,128)(2,1)} %get-tuple-element.16), kind=kLoop, calls=%fused_computation.1 | loop fusion | flops 5242880 | bytes 7864320 | tf_op jit(solution)/shard_map/convert_element_type | solution.py:342
  79.9 1.5 copy-done.1
  81.4 6.7 %all-to-all-done.2 = bf16[32,8,1024]{2,1,0:T(8,128)(2,1)S(1)} async-done(((bf16[32,8,1024]{2,1,0:T(8,128)(2,1)}), bf16[32,8,1024]{2,1,0:T(8,128)(2,1)S(1)}, u32[]{:S(2)}, u32[]{:S(2)}) %all-to-all-start.2) | async-done | bytes 524320 | tf_op jit(solution)/shard_map/all_to_all | solution.py:289
  88.1 1.3 shard_map.122
  89.4 37.8 %all_to_all.43 = bf16[16,8,16,640]{3,2,1,0:T(8,128)(2,1)S(1)} all-to-all(bf16[16,8,16,640]{3,2,1,0:T(8,128)(2,1)} %copy-done.1), channel_id=1, replica_groups=mesh['x'=4,'y'=4,'core'=2,'z'=8] {'x','y'}, dimensions={0} | all-to-all | bytes 5242880 | tf_op jit(solution)/shard_map/all_to_all | solution.py:289
  127.2 0.4 reduce_sum.24
  127.6 12.0 %all_to_all.44 = bf16[8,16,640]{2,1,0:T(8,128)(2,1)S(1)} all-to-all(bf16[8,16,640]{2,1,0:T(8,128)(2,1)S(1)} %reduce_sum.24), channel_id=1, replica_groups=mesh['x'=4,'y'=4,'core'=2,'z'=8] {'z'}, dimensions={0} | all-to-all | bytes 327680 | tf_op jit(solution)/shard_map/all_to_all | solution.py:289
  139.6 19.3 %all_to_all.45.sums_ref = bf16[32,16,640]{2,1,0:T(8,128)(2,1)} all-to-all(bf16[32,16,640]{2,1,0:T(8,128)(2,1)S(1)} %broadcast_in_dim.2), channel_id=1, replica_groups=mesh['x'=4,'y'=4,'core'=2,'z'=8] {'x','y','core'}, dimensions={0} | all-to-all | bytes 1310720 | tf_op jit(solution)/shard_map/all_to_all | solution.py:289
  158.9 2.1 %shard_map.124 = f32[8,8,128]{2,1,0:T(8,128)} custom-call(bf16[32,16,640]{2,1,0:T(8,128)(2,1)} %all_to_all.45.sums_ref), custom_call_target="tpu_custom_call" | custom-call | tf_op jit(solution)/shard_map/pallas_call | solution.py:275
  161.0 3.3 %all-to-all-start.6 = ((f32[8,8,128]{2,1,0:T(8,128)}), f32[8,8,128]{2,1,0:T(8,128)S(1)}, u32[]{:S(2)}, u32[]{:S(2)}) async-start(f32[8,8,128]{2,1,0:T(8,128)} %shard_map.124), calls=%async_computation.6 | async-start | bytes 65536 | tf_op jit(solution)/shard_map/all_to_all | solution.py:289
  164.4 4.2 %shard_map.123.after_ref = f32[256,1024]{1,0:T(8,128)} custom-call(bf16[8,208,1024]{2,1,0:T(8,128)(2,1)} %bitcast.22), custom_call_target="tpu_custom_call" | custom-call | bytes 6000000 | tf_op jit(solution)/shard_map/pallas_call | solution.py:275
  168.6 2.5 %all-to-all-done.6.squares_ref = f32[8,8,128]{2,1,0:T(8,128)S(1)} async-done(((f32[8,8,128]{2,1,0:T(8,128)}), f32[8,8,128]{2,1,0:T(8,128)S(1)}, u32[]{:S(2)}, u32[]{:S(2)}) %all-to-all-start.6) | async-done | bytes 32800 | tf_op jit(solution)/shard_map/all_to_all | solution.py:289
  171.1 0.6 copy-done.2
  171.7 2.3 %shard_map.125 = (f32[128,2048]{1,0:T(8,128)}, f32[64,1024]{1,0:T(8,128)}) custom-call(bf16[32,16,640]{2,1,0:T(8,128)(2,1)} %all_to_all.45.sums_ref, f32[8,8,128]{2,1,0:T(8,128)} %copy-done.2, f32[256,1024]{1,0:T(8,128)} %shard_map.123.after_ref), custom_call_target="tpu_custom_call" | custom-call | bytes 6000000 | tf_op jit(solution)/shard_map/pallas_call | solution.py:275
  (17 shorter events, 0.5 us)
Async XLA Ops:
  7.2 1.1 copy-start
  7.2 50.8 %all-gather.3.cloned.1.call-start = ((), (), s32[]{:S(2)}) async-start(), calls=%async_computation.7 | async-start | bytes 5570560 | tf_op jit(solution)/shard_map/all_gather | solution.py:303
  69.0 7.5 %collective-permute-start = (bf16[16,8,16,640]{3,2,1,0:T(8,128)(2,1)}, bf16[16,8,16,640]{3,2,1,0:T(8,128)(2,1)}, u32[]{:S(2)}, u32[]{:S(2)}) collective-permute-start(bf16[16,8,16,640]{3,2,1,0:T(8,128)(2,1)} %get-tuple-element.17), channel_id=1, source_target_pairs={{0,8},{8,0},{1,9},{9,1},{2,10},{10,2},{3,11},{11,3},{4,12},{12,4},... | collective-permute-start | bytes 7864328 | tf_op jit(solution)/shard_map/ppermute | solution.py:341
  69.4 18.7 %all-to-all-start.2 = ((bf16[32,8,1024]{2,1,0:T(8,128)(2,1)}), bf16[32,8,1024]{2,1,0:T(8,128)(2,1)S(1)}, u32[]{:S(2)}, u32[]{:S(2)}) async-start(bf16[32,8,1024]{2,1,0:T(8,128)(2,1)} %bitcast.25), calls=%async_computation.2 | async-start | bytes 1048576 | tf_op jit(solution)/shard_map/all_to_all | solution.py:289
  76.5 87.9 %all-gather.5.cloned.1.call-start = ((), (), s32[]{:S(2)}) async-start(), calls=%async_computation.8 | async-start | bytes 3833856 | tf_op jit(solution)/shard_map/all_gather | solution.py:358
  79.9 1.5 copy-start.1
  161.0 10.1 %all-to-all-start.6 = ((f32[8,8,128]{2,1,0:T(8,128)}), f32[8,8,128]{2,1,0:T(8,128)S(1)}, u32[]{:S(2)}, u32[]{:S(2)}) async-start(f32[8,8,128]{2,1,0:T(8,128)} %shard_map.124), calls=%async_computation.6 | async-start | bytes 65536 | tf_op jit(solution)/shard_map/all_to_all | solution.py:289
  171.1 0.6 copy-start.2
Sparse Core Ops, SparseCore 0:
  10.4 47.5 all-gather.2
  89.5 42.1 all-gather.4

commit v3 on v2

--- a/solution.py
+++ b/solution.py
@@ -19,6 +19,8 @@
 XY = 16
 PROWS = 16
 PCOLS = 640
+PEER = 96
+FACT = 4224
 GROWS = OWNERS * CAP + 16
 TABLE = ("x", "y", "core")
 ALL = ("x", "y", "core", "z")
@@ -43,7 +45,7 @@
     return lax.broadcasted_iota(jnp.int32, shape, dim)
 
 
-def plan_kernel(owner_ref, row_ref, req_ref, tgt_ref):
+def plan_kernel(owner_ref, row_ref, req_ref, tgt_ref, num_ref):
     square = (TOK, TOK)
     lane = iota(square, 1)
 
@@ -60,6 +62,7 @@
     before = mm(earlier, onehot_b)
     slot = jnp.sum(before * onehot_f, axis=1, keepdims=True)
     tgt_ref[...] = (owner * SLOTS + slot).astype(jnp.int32)
+    num_ref[...] = jnp.where(lane == 0, low, jnp.where(lane == 1, high, 0.0)).astype(BF16)
     here = slot == lane.astype(F32)
     low = jnp.where(here, low, 0.0).astype(BF16)
     high = jnp.where(here, high, 0.0).astype(BF16)
@@ -68,8 +71,8 @@
 
 
 def layer_kernel(
-    lens_ref, got_ref, tgt_ref, weights_ref, gin_ref, gat_ref, ct_ref,
-    out_ref, slots_ref, keep_ref, send_ref,
+    lens_ref, got_ref, tgt_ref, num_ref, weights_ref, gin_ref, gat_ref, ct_ref,
+    out_ref, keep_ref, send_ref,
     wm, wo, dmx, sems,
 ):
     core = lax.axis_index("core")
@@ -183,41 +186,108 @@
         )
         + ct.astype(F32)
     ).astype(BF16)
-    slots_ref[...] = mm_tn(pick, d_emb).astype(BF16)
-
+    lane = iota((TOK, TOK), 1)
+    rows = jnp.concatenate([d_emb, num_ref[...]], axis=1)
     for side, dst in ((1 - core, send_ref), (core, keep_ref)):
-        d_mix = dmx[side]
-        ct_half = ct_ref[:, pl.ds(pl.multiple_of(side * AW, AW), AW)]
+        dst[:, 0:1024] = normed
+        dst[:, 1024:2048] = dmx[side]
+        dst[:, 2048:2560] = gated
+        dst[:, 2560:3072] = ct_ref[:, pl.ds(pl.multiple_of(side * AW, AW), AW)]
+        slot = ((lane >> 3) * 2 + side) * SLOTS + (lane & 7)
+        chosen = (tgt_ref[...] == slot).astype(F32).astype(BF16)
+        dst[:, 3072:FACT] = mm_tn(chosen, rows).astype(BF16)
+
+
+def grads_kernel(keep_ref, theirs_ref, out_ref, buf, sems):
+    def both(first, last):
+        return jnp.concatenate([keep_ref[:, first:last], theirs_ref[:, first:last]], axis=0)
+
+    copies = []
+
+    def send(first, count):
+        block = pl.ds(first, count)
+        copies.append(
+            pltpu.make_async_copy(buf.at[:, block, :], out_ref.at[:, block, :], sems.at[len(copies)])
+        )
+        copies[-1].start()
+
+    d_mix = both(1024, 2048)
+    for pair in range(NZ // 2):
+        one, two = (
+            mm_tn(both(z * TOK, (z + 1) * TOK), d_mix) for z in (2 * pair, 2 * pair + 1)
+        )
+        for p in range(XY):
+            buf[p, 16 * pair : 16 * pair + 16, :] = jnp.concatenate(
+                [one[8 * p : 8 * p + 8], two[8 * p : 8 * p + 8]], axis=0
+            ).astype(BF16)
+        send(16 * pair, 16)
+
+    grad = mm_tn(both(2048, 2560), both(2560, 3072))
+    for p in range(XY):
+        r, c = (p // 2) * 8, (p % 2) * 256
+        halves = [
+            jnp.concatenate(
+                [grad[z * 64 + r : z * 64 + r + 8, c : c + 256] for z in range(first, first + 4)],
+                axis=1,
+            )
+            for first in (0, 4)
+        ]
+        buf[p, 64:80, :] = jnp.concatenate(halves, axis=0).astype(BF16)
+    send(64, 16)
+
+    r, k = iota((256, 256), 0), iota((256, 256), 1)
+    j = r & 15
+    source = jnp.where(j < CAP, 0, 128) + (r >> 4) * SLOTS + jnp.where(j < CAP, j, j - CAP)
+    take = ((k == source) & (j < 2 * CAP)).astype(F32).astype(BF16)
+    rows = mm(take, both(3072, 4096))
+    names = mm(take, both(4096, FACT)).T
+    place = iota((256, 256), 0) & 15
+    names = jnp.where(
+        place == 2 * CAP, names[0:1], jnp.where(place == 2 * CAP + 1, names[1:2], 0.0)
+    )
+    rows = jnp.concatenate([rows[:, :256] + names, rows[:, 256:]], axis=1).astype(BF16)
+    for p in range(XY):
+        buf[p, 80:PEER, :] = rows[16 * p : 16 * p + 16]
+    send(80, 16)
+    for copy in copies:
+        copy.wait()
+
+
+def plane_kernel(block_ref, out_ref):
+    step = pl.program_id(0)
+    total = jnp.sum(block_ref[...].astype(F32), axis=0)
+
+    @pl.when(step < 4)
+    def _():
+        for sub in range(2):
+            part = total[8 * sub : 8 * sub + 8]
+            out_ref[step * 2 + sub, :, 0:512] = jnp.concatenate(
+                [part[:, :512], part[:, 512:]], axis=0
+            ).astype(BF16)
+
+    @pl.when(step == 4)
+    def _():
         for z in range(NZ):
-            grad = mm_tn(normed[:, z * TOK : (z + 1) * TOK], d_mix).astype(BF16)
-            for g in range(8):
-                for c in range(2):
-                    dst[g * 2 + c, z, :, 0:512] = grad[
-                        g * PROWS : (g + 1) * PROWS, c * 512 : (c + 1) * 512
-                    ]
-        for pair in range(NZ // 2):
-            grad = mm_tn(gated[:, pair * TOK : (pair + 1) * TOK], ct_half).astype(BF16)
-            for sub in range(2):
-                for r in range(4):
-                    for c in range(4):
-                        dst[r * 4 + c, pair * 2 + sub, :, 512:PCOLS] = grad[
-                            sub * 64 + r * PROWS : sub * 64 + (r + 1) * PROWS,
-                            c * 128 : (c + 1) * 128,
-                        ]
-
-
-def pack_kernel(rows_ref, asked_ref, after_ref, out_ref):
+            part = total[(z // 4) * 8 : (z // 4) * 8 + 8, (z % 4) * 256 : (z % 4) * 256 + 256]
+            out_ref[z, :, 512:PCOLS] = jnp.concatenate(
+                [part[:, :128], part[:, 128:]], axis=0
+            ).astype(BF16)
+
+
+def pack_kernel(rows_ref, out_ref):
     used = OWNERS * CAP
-    r, k = iota((used, OWNERS * SLOTS), 0), iota((used, OWNERS * SLOTS), 1)
-    take = (r // CAP == k // SLOTS) & (r % CAP == k % SLOTS)
-    out_ref[:used] = mm(take.astype(F32).astype(BF16), rows_ref[...]).astype(BF16)
-    asked = asked_ref[...]
-    owner = (iota((256, OWNERS), 0) // CAP == iota((256, OWNERS), 1)).astype(F32).astype(BF16)
-    slot = iota((256, 128), 0) % CAP == iota((256, 128), 1)
+    me = lax.axis_index("x") * 4 + lax.axis_index("y")
+    rows = rows_ref[...].reshape(256, D)
+    r, k = iota((used, 256), 0), iota((used, 256), 1)
+    src, j = r // (2 * CAP), r % (2 * CAP)
+    out_ref[:used] = mm((k == src * 16 + j).astype(F32).astype(BF16), rows).astype(BF16)
+    r, k = iota((256, 256), 0), iota((256, 256), 1)
+    src, j = r // (2 * CAP), r % (2 * CAP)
+    mine = k == me * 16 + j
     parts = []
-    for part in (asked & 127, asked >> 7):
-        spread = mm(owner, part.astype(F32).astype(BF16))
-        column = jnp.sum(jnp.where(slot, spread, 0.0), axis=1, keepdims=True)
+    for place in (2 * CAP, 2 * CAP + 1):
+        take = (k == src * 16 + place).astype(F32).astype(BF16)
+        column = jnp.sum(jnp.where(mine, mm(take, rows[:, :256]), 0.0), axis=1, keepdims=True)
         parts.append(jnp.broadcast_to(column, (256, 128)).T[:PROWS])
     which = iota((PROWS, 256), 0)
     numbers = jnp.where(which == 0, parts[0], jnp.where(which == 1, parts[1], 0.0))
@@ -229,40 +299,46 @@
 def table_kernel(rows_ref, out_ref):
     used = OWNERS * CAP
     first = lax.axis_index("z") * 256
-    total = jnp.zeros((256, D), F32)
-    for z in range(NZ):
-        low = rows_ref[z, used : used + PROWS, :256].astype(F32)
-        number = (low[0:1] + 128.0 * low[1:2]).astype(jnp.int32)[:, :used] - first
-        here = (iota((256, used), 0) == number).astype(F32).astype(BF16)
-        total = total + mm(here, rows_ref[z, :used])
-    out_ref[...] = total
+    names = rows_ref[0, used : used + PROWS, :256].astype(F32)
+    number = (names[0:1] + 128.0 * names[1:2]).astype(jnp.int32)[:, :used] - first
+    here = (iota((256, used), 0) == number).astype(F32).astype(BF16)
+    part = mm(here, rows_ref[0, :used])
+
+    @pl.when(pl.program_id(0) == 0)
+    def _():
+        out_ref[...] = part
+
+    @pl.when(pl.program_id(0) > 0)
+    def _():
+        out_ref[...] += part
 
 
 def square_kernel(sums_ref, out_ref):
-    sums = sums_ref[...].astype(F32)
-    sq = sums * sums
-    mix = jnp.sum(sq[:, :, :512])
-    out = jnp.sum(sq[:, :, 512:])
+    total = jnp.zeros((PROWS, PCOLS), F32)
+    for i in range(OWNERS):
+        part = sums_ref[i].astype(F32)
+        total = total + part * part
+    mix = jnp.sum(total[:, :512])
+    out = jnp.sum(total[:, 512:])
     lane = iota((NZ, 8, 128), 2)
     out_ref[...] = jnp.where(lane == 0, mix, jnp.where(lane == 1, out, 0.0))
 
 
-def scale_kernel(sums_ref, squares_ref, after_ref, mix_ref, out_ref):
+def scale_kernel(sums_ref, squares_ref, mix_ref, out_ref):
     total = jnp.sum(squares_ref[...], axis=0)[0:1]
     mix_sq, out_sq = total[:, 0:1], total[:, 1:2]
     mix_scale = jnp.minimum(1.0, 1.0 / jnp.sqrt(mix_sq / float(D * 4 * AW) + 1e-06))
     out_scale = jnp.minimum(1.0, 1.0 / jnp.sqrt(out_sq / float(D * AW) + 1e-06))
-    for core in range(2):
-        for g in range(8):
-            for c in range(2):
-                mix_ref[
-                    g * PROWS : (g + 1) * PROWS, core * D + c * 512 : core * D + (c + 1) * 512
-                ] = sums_ref[(g * 2 + c) * 2 + core, :, 0:512].astype(F32) * mix_scale
-        for r in range(4):
-            for c in range(4):
-                out_ref[
-                    r * PROWS : (r + 1) * PROWS, core * AW + c * 128 : core * AW + (c + 1) * 128
-                ] = sums_ref[(r * 4 + c) * 2 + core, :, 512:PCOLS].astype(F32) * out_scale
+    for p in range(XY):
+        for core in range(2):
+            sums = sums_ref[p * 2 + core].astype(F32)
+            mix, out = sums[:, :512] * mix_scale, sums[:, 512:] * out_scale
+            r, c = p * 8, core * D
+            mix_ref[r : r + 8, c : c + 512] = mix[:8]
+            mix_ref[r : r + 8, c + 512 : c + 1024] = mix[8:]
+            r, c = (p // 2) * 8, core * AW + (p % 2) * 256
+            out_ref[r : r + 8, c : c + 128] = out[:8]
+            out_ref[r : r + 8, c + 128 : c + 256] = out[8:]
 
 
 def vmem():
@@ -302,9 +378,9 @@
     )
     weights = lax.all_gather(share, ("core", "z"), axis=0, tiled=True).reshape(2, NZ, 160, D)
 
-    requests, target = call(
+    requests, target, numbers = call(
         plan_kernel,
-        [((OWNERS, 128), jnp.int32), ((TOK, TOK), jnp.int32)],
+        [((OWNERS, 128), jnp.int32), ((TOK, TOK), jnp.int32), ((TOK, TOK), BF16)],
         (item_owner.reshape(1, TOK), item_row.reshape(1, TOK)),
     )
     asked = exchange(requests, TABLE)
@@ -314,20 +390,20 @@
 
     smem = pl.BlockSpec(memory_space=pltpu.SMEM)
     anywhere = pl.BlockSpec(memory_space=pl.ANY)
-    piece = (XY, NZ, PROWS, PCOLS)
-    layer_out, grad_slots, keep, send = call(
+    layer_out, keep, send = call(
         layer_kernel,
-        [((TOK, D), BF16), ((OWNERS * SLOTS, D), BF16), (piece, BF16), (piece, BF16)],
+        [((TOK, D), BF16), ((TOK, FACT), BF16), ((TOK, FACT), BF16)],
         (
             user_lengths,
             got.reshape(OWNERS * SLOTS, D),
             target,
+            numbers,
             weights,
             gain_in.reshape(1, D),
             gain_attn.reshape(1, AW),
             cotangent,
         ),
-        specs=[smem, vmem(), vmem(), anywhere, vmem(), vmem(), vmem()],
+        specs=[smem, vmem(), vmem(), vmem(), anywhere, vmem(), vmem(), vmem()],
         scratch_shapes=[
             pltpu.VMEM((2, NZ, TOK, D), BF16),
             pltpu.VMEM((NZ, 2, 32, D), BF16),
@@ -339,40 +415,67 @@
     )
 
     theirs = lax.ppermute(send, "core", [(0, 1), (1, 0)])
-    pair_sum = (keep.astype(F32) + theirs.astype(F32)).astype(BF16)
-    added = pair_sum[0, 0, :, :128]
-    plane = exchange(pair_sum, ("x", "y"))
-    plane_sum = jnp.sum(plane.astype(F32), axis=0).astype(BF16)
+    grads = pl.pallas_call(
+        grads_kernel,
+        out_shape=jax.ShapeDtypeStruct((XY, PEER, D), BF16),
+        in_specs=[vmem(), vmem()],
+        out_specs=anywhere,
+        scratch_shapes=[
+            pltpu.VMEM((XY, PEER, D), BF16),
+            pltpu.SemaphoreType.DMA((6,)),
+        ],
+        cost_estimate=cost(3),
+        compiler_params=pltpu.CompilerParams(vmem_limit_bytes=30 * MB),
+    )(keep, theirs)
+    plane = exchange(grads, ("x", "y"))
+
+    packed = pl.pallas_call(
+        pack_kernel,
+        grid=(1,),
+        out_shape=jax.ShapeDtypeStruct((GROWS, D), BF16),
+        in_specs=[pl.BlockSpec((XY, 16, D), lambda i: (0, 5, 0))],
+        out_specs=pl.BlockSpec((GROWS, D), lambda i: (0, 0)),
+        cost_estimate=cost(2),
+        compiler_params=pltpu.CompilerParams(vmem_limit_bytes=60 * MB),
+    )(plane)
+    gathered = lax.all_gather(packed, "z", axis=0, tiled=True).reshape(NZ, GROWS, D)
+    table_grad = pl.pallas_call(
+        table_kernel,
+        grid=(NZ,),
+        out_shape=jax.ShapeDtypeStruct((256, D), F32),
+        in_specs=[pl.BlockSpec((1, GROWS, D), lambda i: (i, 0, 0))],
+        out_specs=pl.BlockSpec((256, D), lambda i: (0, 0)),
+        cost_estimate=cost(3),
+        compiler_params=pltpu.CompilerParams(vmem_limit_bytes=60 * MB),
+    )(gathered)
+
+    plane_sum = pl.pallas_call(
+        plane_kernel,
+        grid=(5,),
+        out_shape=jax.ShapeDtypeStruct((NZ, PROWS, PCOLS), BF16),
+        in_specs=[pl.BlockSpec((XY, 16, D), lambda i: (0, i, 0))],
+        out_specs=pl.BlockSpec((NZ, PROWS, PCOLS), lambda i: (0, 0, 0)),
+        cost_estimate=cost(2),
+        compiler_params=pltpu.CompilerParams(vmem_limit_bytes=60 * MB),
+    )(plane)
     column = exchange(plane_sum, "z")
     whole = jnp.sum(column.astype(F32), axis=0).astype(BF16)
     sums = exchange(jnp.broadcast_to(whole[None], (OWNERS, PROWS, PCOLS)), TABLE)
-    received = exchange(grad_slots.reshape(OWNERS, SLOTS, D), TABLE)
-    packed = call(
-        pack_kernel,
-        [((GROWS, D), BF16)],
-        (received.reshape(OWNERS * SLOTS, D), asked, added),
-        specs=[vmem(), vmem(), anywhere],
-        cost_estimate=cost(2),
+    squares = call(
+        square_kernel,
+        [((NZ, 8, 128), F32)],
+        (sums,),
+        cost_estimate=cost(1),
         compiler_params=pltpu.CompilerParams(vmem_limit_bytes=16 * MB),
     )
-    gathered = lax.all_gather(packed, "z", axis=0, tiled=True).reshape(NZ, GROWS, D)
-    table_grad = call(
-        table_kernel,
-        [((256, D), F32)],
-        (gathered,),
-        cost_estimate=cost(2),
-        compiler_params=pltpu.CompilerParams(vmem_limit_bytes=60 * MB),
-    )
-    squares = call(square_kernel, [((NZ, 8, 128), F32)], (sums,))
     squares = exchange(squares, "z")
     mix_grad, out_grad = call(
         scale_kernel,
         [((TOK, 4 * AW), F32), ((64, D), F32)],
-        (sums, squares, table_grad),
-        specs=[vmem(), vmem(), anywhere],
+        (sums, squares),
         cost_estimate=cost(2),
-    )
-
+        compiler_params=pltpu.CompilerParams(vmem_limit_bytes=16 * MB),
+    )
     return (layer_out, table_grad, mix_grad, out_grad)
 
 

time: 181 us -> 185 us (1.022)
  blocking collectives: 100 us -> 120 us
  starting transfers between devices: 10.9 us -> 0.42 us
  waiting for transfers between devices: 21 us -> 14.3 us
  Pallas kernels: 22.5 us -> 28.5 us
  other arithmetic: 4.48 us -> 0.79 us
    all_to_all x5 -> x6, blocking collectives: 100 us -> 120 us  [exchange(): return lax.all_to_all(array, axes, split_axis=0, concat_axis=0, tiled=True)]
    pallas_call x0 -> x4, Pallas kernels: none -> 15.8 us  [the longest x1 7.01 us: shards(): pl.pallas_call(table_kernel, grid=(NZ,), out_shape=jax.ShapeDtypeStruct((...]
    all_to_all x2 -> x0, starting transfers between devices: 10.4 us -> none  [exchange(): return lax.all_to_all(array, axes, split_axis=0, concat_axis=0, tiled=True)]
    pallas_call x6 -> x4, Pallas kernels: 22.5 us -> 12.6 us  [call(): pl.pallas_call(body, out_shape=shapes[0] if one else shapes, in_specs=spe...]
    all_to_all x2 -> x0, waiting for transfers between devices: 9.27 us -> none  [exchange(): return lax.all_to_all(array, axes, split_axis=0, concat_axis=0, tiled=True)]
    convert_element_type x1 -> x0, other arithmetic: 3.32 us -> none  [shards(): pair_sum = (keep.astype(F32) + theirs.astype(F32)).astype(BF16)]
    ppermute x1, waiting for transfers between devices: 0.01 us -> 2.66 us  [shards(): theirs = lax.ppermute(send, 'core', [(0, 1), (1, 0)])]
  transfers between devices with their start and end apart: 5 -> 3, of which waited for: 3 -> 2; matrix products, arithmetic and copies ran while one was open for 5% -> 2% of each run, Pallas kernels for 4% -> 4%
where the time goes in v3:
time: 185 us; the launch traced here: 184 us
  blocking collectives  120 us (65%)
  Pallas kernels  28.5 us (15%)
  waiting for transfers between devices  14.3 us (8%)
  between operations  14.1 us (8%)
  local copies, waits for them, and re-layouts  6.7 us (4%)
    all_to_all x6, blocking collectives, exchange(): return lax.all_to_all(array, axes, split_axis=0, concat_axis=0, tiled=True)  120 us
    pallas_call x4, Pallas kernels, call(): pl.pallas_call(body, out_shape=shapes[0] if one else shapes, in_specs=spe...  12.6 us
    all_gather x1, waiting for transfers between devices, shards(): lax.all_gather(share, ('core', 'z'), axis=0, tiled=True)  11.6 us
    pallas_call x1, Pallas kernels, shards(): pl.pallas_call(table_kernel, grid=(NZ,), out_shape=jax.ShapeDtypeStruct((...  7.01 us
    gather x1, local copies, waits for them, and re-layouts, shards(): found = item_table.at[wanted].get(mode='promise_in_bounds')  4.29 us
    pallas_call x1, Pallas kernels, shards(): pl.pallas_call(plane_kernel, grid=(5,), out_shape=jax.ShapeDtypeStruct((N...  4.16 us
  transfers between devices with their start and end apart: 3, of which 2 were waited for; matrix products, arithmetic and copies ran while one was open for 2% of the time, Pallas kernels for 4%

profile of v3, /device:TPU:1, one launch (start us, length us, event | category | flops | bytes accessed | tf_op | source)
XLA Modules:
  0.0 184.5 jit_solution(7612087656969428020)
XLA Ops:
  7.2 0.9 constant_dynamic-slice_fusion
  8.1 0.1 copy-done
  8.3 0.7 pad_maximum_fusion
  9.1 1.7 shard_map.120
  10.8 15.5 %all_to_all.37 = s32[32,1,128]{2,1,0:T(1,128)S(1)} all-to-all(s32[32,1,128]{2,1,0:T(1,128)} %bitcast.19), channel_id=1, replica_groups=mesh['x'=4,'y'=4,'core'=2,'z'=8] {'x','y','core'}, dimensions={0} | all-to-all | bytes 32768 | tf_op jit(solution)/shard_map/all_to_all | solution.py:365
  26.3 0.1 reshape.68
  26.4 4.3 %gather_fusion = bf16[256,1024]{1,0:T(8,128)(2,1)S(1)} fusion(bf16[2048,1024]{1,0:T(8,128)(2,1)} %param.9, s32[1024]{0:T(1024)S(1)} %pad_clamp_fusion), kind=kCustom, calls=%fused_computation | custom fusion | bytes 1049600 | tf_op jit(solution)/shard_map/gather | solution.py:388
  30.7 15.7 %all_to_all.38 = bf16[32,8,1024]{2,1,0:T(8,128)(2,1)} all-to-all(bf16[32,8,1024]{2,1,0:T(8,128)(2,1)S(1)} %bitcast.17), channel_id=1, replica_groups=mesh['x'=4,'y'=4,'core'=2,'z'=8] {'x','y','core'}, dimensions={0} | all-to-all | bytes 1048576 | tf_op jit(solution)/shard_map/all_to_all | solution.py:365
  46.4 11.6 %all-gather.3.cloned.1.call-done = bf16[2560,1024]{1,0:T(8,128)(2,1)} async-done(((bf16[160,1024]{1,0:T(8,128)(2,1)}), bf16[2560,1024]{1,0:T(8,128)(2,1)}) %all-gather.3.cloned.1.call-update) | async-done | bytes 5242896 | tf_op jit(solution)/shard_map/all_gather | solution.py:379
  58.0 9.5 %shard_map.121 = (bf16[128,1024]{1,0:T(8,128)(2,1)}, bf16[128,4224]{1,0:T(8,128)(2,1)}, bf16[128,4224]{1,0:T(8,128)(2,1)}) custom-call(s32[1,8]{1,0:T(1,128)} %lens_ref.1, bf16[256,1024]{1,0:T(8,128)(2,1)} %bitcast.16, s32[128,128]{1,0:T(8,128)} %get-tuple-element.13.tgt_ref, bf16[128,128]{1,0:T(8,128)(2,1)} %get-tuple-element.14.num_ref, ...), custom_call_target="tpu_custom_call" | custom-call | bytes 27000000 | tf_op jit(solution)/shard_map/pallas_call | solution.py:351
  67.5 0.3 collective-permute-start
  67.8 2.7 %collective-permute-done.theirs_ref = bf16[128,4224]{1,0:T(8,128)(2,1)S(1)} collective-permute-done((bf16[128,4224]{1,0:T(8,128)(2,1)}, bf16[128,4224]{1,0:T(8,128)(2,1)S(1)}, u32[]{:S(2)}, u32[]{:S(2)}) %collective-permute-start) | collective-permute-done | bytes 1081376 | tf_op jit(solution)/shard_map/ppermute | solution.py:417
  70.5 1.2 copy-done.1
  71.7 2.4 %shard_map.122 = bf16[16,96,1024]{2,1,0:T(8,128)(2,1)S(1)} custom-call(bf16[128,4224]{1,0:T(8,128)(2,1)S(1)} %copy-done.1, bf16[128,4224]{1,0:T(8,128)(2,1)S(1)} %collective-permute-done.theirs_ref), custom_call_target="tpu_custom_call" | custom-call | bytes 9000000 | tf_op jit(solution)/shard_map/pallas_call | solution.py:418
  74.1 44.7 %all_to_all.39.rows_ref.block_ref = bf16[16,96,1024]{2,1,0:T(8,128)(2,1)} all-to-all(bf16[16,96,1024]{2,1,0:T(8,128)(2,1)S(1)} %shard_map.122), channel_id=1, replica_groups=mesh['x'=4,'y'=4,'core'=2,'z'=8] {'x','y'}, dimensions={0} | all-to-all | bytes 6291456 | tf_op jit(solution)/shard_map/all_to_all | solution.py:365
  118.9 2.3 %shard_map.123 = bf16[208,1024]{1,0:T(8,128)(2,1)} custom-call(bf16[16,96,1024]{2,1,0:T(8,128)(2,1)} %all_to_all.39.rows_ref.block_ref), custom_call_target="tpu_custom_call" | custom-call | bytes 6000000 | tf_op jit(solution)/shard_map/pallas_call | solution.py:432
  121.2 4.2 %shard_map.125 = bf16[8,16,640]{2,1,0:T(8,128)(2,1)} custom-call(bf16[16,96,1024]{2,1,0:T(8,128)(2,1)} %all_to_all.39.rows_ref.block_ref), custom_call_target="tpu_custom_call" | custom-call | bytes 6000000 | tf_op jit(solution)/shard_map/pallas_call | solution.py:452
  125.3 14.1 %all_to_all.40 = bf16[8,16,640]{2,1,0:T(8,128)(2,1)S(1)} all-to-all(bf16[8,16,640]{2,1,0:T(8,128)(2,1)} %shard_map.125), channel_id=1, replica_groups=mesh['x'=4,'y'=4,'core'=2,'z'=8] {'z'}, dimensions={0} | all-to-all | bytes 327680 | tf_op jit(solution)/shard_map/all_to_all | solution.py:365
  139.4 0.1 broadcast_in_dim.2
  139.5 19.9 %all_to_all.41.sums_ref = bf16[32,16,640]{2,1,0:T(8,128)(2,1)S(1)} all-to-all(bf16[32,16,640]{2,1,0:T(8,128)(2,1)S(1)} %broadcast_in_dim.2), channel_id=1, replica_groups=mesh['x'=4,'y'=4,'core'=2,'z'=8] {'x','y','core'}, dimensions={0} | all-to-all | bytes 1310720 | tf_op jit(solution)/shard_map/all_to_all | solution.py:365
  159.4 0.2 shard_map.126
  159.6 9.9 %all_to_all.42.squares_ref = f32[8,8,128]{2,1,0:T(8,128)S(1)} all-to-all(f32[8,8,128]{2,1,0:T(8,128)S(1)} %shard_map.126), channel_id=1, replica_groups=mesh['x'=4,'y'=4,'core'=2,'z'=8] {'z'}, dimensions={0} | all-to-all | bytes 65536 | tf_op jit(solution)/shard_map/all_to_all | solution.py:365
  169.4 1.2 shard_map.127
  170.6 7.0 %shard_map.124 = f32[256,1024]{1,0:T(8,128)} custom-call(bf16[8,208,1024]{2,1,0:T(8,128)(2,1)} %bitcast.15), custom_call_target="tpu_custom_call" | custom-call | bytes 9000000 | tf_op jit(solution)/shard_map/pallas_call | solution.py:442
  (11 shorter events, 0.2 us)
Async XLA Ops:
  7.2 1.1 copy-start
  7.2 50.8 %all-gather.3.cloned.1.call-start = ((), (), s32[]{:S(2)}) async-start(), calls=%async_computation.6 | async-start | bytes 5570560 | tf_op jit(solution)/shard_map/all_gather | solution.py:379
  9.0 161.6 %all-gather.5.cloned.1.call-start = ((), (), s32[]{:S(2)}) async-start(), calls=%async_computation.7 | async-start | bytes 3833856 | tf_op jit(solution)/shard_map/all_gather | solution.py:441
  67.5 3.0 %collective-permute-start = (bf16[128,4224]{1,0:T(8,128)(2,1)}, bf16[128,4224]{1,0:T(8,128)(2,1)S(1)}, u32[]{:S(2)}, u32[]{:S(2)}) collective-permute-start(bf16[128,4224]{1,0:T(8,128)(2,1)} %get-tuple-element.17), channel_id=1, source_target_pairs={{0,8},{8,0},{1,9},{9,1},{2,10},{10,2},{3,11},{11,3},{4,12},{12,4},... | collective-permute-start | bytes 3244040 | tf_op jit(solution)/shard_map/ppermute | solution.py:417
  70.5 1.2 copy-start.1
Sparse Core Ops, SparseCore 0:
  10.4 47.5 all-gather.2
  121.3 48.5 all-gather.4

commit v4 on v2

--- a/solution.py
+++ b/solution.py
@@ -19,6 +19,7 @@
 XY = 16
 PROWS = 16
 PCOLS = 640
+FACT = 3072
 GROWS = OWNERS * CAP + 16
 TABLE = ("x", "y", "core")
 ALL = ("x", "y", "core", "z")
@@ -184,29 +185,42 @@
         + ct.astype(F32)
     ).astype(BF16)
     slots_ref[...] = mm_tn(pick, d_emb).astype(BF16)
-
     for side, dst in ((1 - core, send_ref), (core, keep_ref)):
-        d_mix = dmx[side]
-        ct_half = ct_ref[:, pl.ds(pl.multiple_of(side * AW, AW), AW)]
-        for z in range(NZ):
-            grad = mm_tn(normed[:, z * TOK : (z + 1) * TOK], d_mix).astype(BF16)
-            for g in range(8):
-                for c in range(2):
-                    dst[g * 2 + c, z, :, 0:512] = grad[
-                        g * PROWS : (g + 1) * PROWS, c * 512 : (c + 1) * 512
-                    ]
-        for pair in range(NZ // 2):
-            grad = mm_tn(gated[:, pair * TOK : (pair + 1) * TOK], ct_half).astype(BF16)
-            for sub in range(2):
-                for r in range(4):
-                    for c in range(4):
-                        dst[r * 4 + c, pair * 2 + sub, :, 512:PCOLS] = grad[
-                            sub * 64 + r * PROWS : sub * 64 + (r + 1) * PROWS,
-                            c * 128 : (c + 1) * 128,
-                        ]
-
-
-def pack_kernel(rows_ref, asked_ref, after_ref, out_ref):
+        dst[:, 0:1024] = normed
+        dst[:, 1024:2048] = dmx[side]
+        dst[:, 2048:2560] = gated
+        dst[:, 2560:FACT] = ct_ref[:, pl.ds(pl.multiple_of(side * AW, AW), AW)]
+
+
+def grads_kernel(keep_ref, theirs_ref, out_ref, buf, sems):
+    def both(first, last):
+        return jnp.concatenate([keep_ref[:, first:last], theirs_ref[:, first:last]], axis=0)
+
+    grad = mm_tn(both(2048, 2560), both(2560, FACT))
+    for z in range(NZ):
+        for p in range(XY):
+            r, c = z * 64 + (p // 2) * 8, (p % 2) * 256
+            part = grad[r : r + 8, c : c + 256]
+            buf[p, z, :, 512:PCOLS] = jnp.concatenate(
+                [part[:, :128], part[:, 128:]], axis=0
+            ).astype(BF16)
+
+    copies = []
+    d_mix = both(1024, 2048)
+    for z in range(NZ):
+        grad = mm_tn(both(z * TOK, (z + 1) * TOK), d_mix)
+        for p in range(XY):
+            part = grad[8 * p : 8 * p + 8]
+            buf[p, z, :, 0:512] = jnp.concatenate(
+                [part[:, :512], part[:, 512:]], axis=0
+            ).astype(BF16)
+        copies.append(pltpu.make_async_copy(buf.at[:, z], out_ref.at[:, z], sems.at[z]))
+        copies[-1].start()
+    for copy in copies:
+        copy.wait()
+
+
+def pack_kernel(rows_ref, asked_ref, out_ref):
     used = OWNERS * CAP
     r, k = iota((used, OWNERS * SLOTS), 0), iota((used, OWNERS * SLOTS), 1)
     take = (r // CAP == k // SLOTS) & (r % CAP == k % SLOTS)
@@ -226,43 +240,50 @@
     )
 
 
-def table_kernel(rows_ref, out_ref):
+def table_kernel(rows_ref, out_ref, buf, sems):
     used = OWNERS * CAP
     first = lax.axis_index("z") * 256
+    copies = [
+        pltpu.make_async_copy(rows_ref.at[z], buf.at[z], sems.at[z]) for z in range(NZ)
+    ]
+    for copy in copies:
+        copy.start()
     total = jnp.zeros((256, D), F32)
     for z in range(NZ):
-        low = rows_ref[z, used : used + PROWS, :256].astype(F32)
-        number = (low[0:1] + 128.0 * low[1:2]).astype(jnp.int32)[:, :used] - first
+        copies[z].wait()
+        names = buf[z, used : used + PROWS, :256].astype(F32)
+        number = (names[0:1] + 128.0 * names[1:2]).astype(jnp.int32)[:, :used] - first
         here = (iota((256, used), 0) == number).astype(F32).astype(BF16)
-        total = total + mm(here, rows_ref[z, :used])
+        total = total + mm(here, buf[z, :used])
     out_ref[...] = total
 
 
 def square_kernel(sums_ref, out_ref):
-    sums = sums_ref[...].astype(F32)
-    sq = sums * sums
-    mix = jnp.sum(sq[:, :, :512])
-    out = jnp.sum(sq[:, :, 512:])
+    total = jnp.zeros((PROWS, PCOLS), F32)
+    for i in range(OWNERS):
+        part = sums_ref[i].astype(F32)
+        total = total + part * part
+    mix = jnp.sum(total[:, :512])
+    out = jnp.sum(total[:, 512:])
     lane = iota((NZ, 8, 128), 2)
     out_ref[...] = jnp.where(lane == 0, mix, jnp.where(lane == 1, out, 0.0))
 
 
-def scale_kernel(sums_ref, squares_ref, after_ref, mix_ref, out_ref):
+def scale_kernel(sums_ref, squares_ref, mix_ref, out_ref):
     total = jnp.sum(squares_ref[...], axis=0)[0:1]
     mix_sq, out_sq = total[:, 0:1], total[:, 1:2]
     mix_scale = jnp.minimum(1.0, 1.0 / jnp.sqrt(mix_sq / float(D * 4 * AW) + 1e-06))
     out_scale = jnp.minimum(1.0, 1.0 / jnp.sqrt(out_sq / float(D * AW) + 1e-06))
-    for core in range(2):
-        for g in range(8):
-            for c in range(2):
-                mix_ref[
-                    g * PROWS : (g + 1) * PROWS, core * D + c * 512 : core * D + (c + 1) * 512
-                ] = sums_ref[(g * 2 + c) * 2 + core, :, 0:512].astype(F32) * mix_scale
-        for r in range(4):
-            for c in range(4):
-                out_ref[
-                    r * PROWS : (r + 1) * PROWS, core * AW + c * 128 : core * AW + (c + 1) * 128
-                ] = sums_ref[(r * 4 + c) * 2 + core, :, 512:PCOLS].astype(F32) * out_scale
+    for p in range(XY):
+        for core in range(2):
+            sums = sums_ref[p * 2 + core].astype(F32)
+            mix, out = sums[:, :512] * mix_scale, sums[:, 512:] * out_scale
+            r, c = p * 8, core * D
+            mix_ref[r : r + 8, c : c + 512] = mix[:8]
+            mix_ref[r : r + 8, c + 512 : c + 1024] = mix[8:]
+            r, c = (p // 2) * 8, core * AW + (p % 2) * 256
+            out_ref[r : r + 8, c : c + 128] = out[:8]
+            out_ref[r : r + 8, c + 128 : c + 256] = out[8:]
 
 
 def vmem():
@@ -314,10 +335,14 @@
 
     smem = pl.BlockSpec(memory_space=pltpu.SMEM)
     anywhere = pl.BlockSpec(memory_space=pl.ANY)
-    piece = (XY, NZ, PROWS, PCOLS)
     layer_out, grad_slots, keep, send = call(
         layer_kernel,
-        [((TOK, D), BF16), ((OWNERS * SLOTS, D), BF16), (piece, BF16), (piece, BF16)],
+        [
+            ((TOK, D), BF16),
+            ((OWNERS * SLOTS, D), BF16),
+            ((TOK, FACT), BF16),
+            ((TOK, FACT), BF16),
+        ],
         (
             user_lengths,
             got.reshape(OWNERS * SLOTS, D),
@@ -339,19 +364,30 @@
     )
 
     theirs = lax.ppermute(send, "core", [(0, 1), (1, 0)])
-    pair_sum = (keep.astype(F32) + theirs.astype(F32)).astype(BF16)
-    added = pair_sum[0, 0, :, :128]
-    plane = exchange(pair_sum, ("x", "y"))
-    plane_sum = jnp.sum(plane.astype(F32), axis=0).astype(BF16)
-    column = exchange(plane_sum, "z")
+    grads = pl.pallas_call(
+        grads_kernel,
+        out_shape=jax.ShapeDtypeStruct((XY, NZ, PROWS, PCOLS), BF16),
+        in_specs=[vmem(), vmem()],
+        out_specs=anywhere,
+        scratch_shapes=[
+            pltpu.VMEM((XY, NZ, PROWS, PCOLS), BF16),
+            pltpu.SemaphoreType.DMA((NZ,)),
+        ],
+        cost_estimate=cost(3),
+        compiler_params=pltpu.CompilerParams(vmem_limit_bytes=30 * MB),
+    )(keep, theirs)
+    row_sum = lax.psum_scatter(
+        grads.reshape(XY * NZ * PROWS, PCOLS), "x", scatter_dimension=0, tiled=True
+    )
+    column = exchange(row_sum.reshape(4 * NZ, PROWS, PCOLS), ("y", "z"))
     whole = jnp.sum(column.astype(F32), axis=0).astype(BF16)
     sums = exchange(jnp.broadcast_to(whole[None], (OWNERS, PROWS, PCOLS)), TABLE)
+
     received = exchange(grad_slots.reshape(OWNERS, SLOTS, D), TABLE)
     packed = call(
         pack_kernel,
         [((GROWS, D), BF16)],
-        (received.reshape(OWNERS * SLOTS, D), asked, added),
-        specs=[vmem(), vmem(), anywhere],
+        (received.reshape(OWNERS * SLOTS, D), asked),
         cost_estimate=cost(2),
         compiler_params=pltpu.CompilerParams(vmem_limit_bytes=16 * MB),
     )
@@ -360,19 +396,27 @@
         table_kernel,
         [((256, D), F32)],
         (gathered,),
-        cost_estimate=cost(2),
+        specs=[anywhere],
+        scratch_shapes=[pltpu.VMEM((NZ, GROWS, D), BF16), pltpu.SemaphoreType.DMA((NZ,))],
+        cost_estimate=cost(3),
         compiler_params=pltpu.CompilerParams(vmem_limit_bytes=60 * MB),
     )
-    squares = call(square_kernel, [((NZ, 8, 128), F32)], (sums,))
+
+    squares = call(
+        square_kernel,
+        [((NZ, 8, 128), F32)],
+        (sums,),
+        cost_estimate=cost(1),
+        compiler_params=pltpu.CompilerParams(vmem_limit_bytes=16 * MB),
+    )
     squares = exchange(squares, "z")
     mix_grad, out_grad = call(
         scale_kernel,
         [((TOK, 4 * AW), F32), ((64, D), F32)],
-        (sums, squares, table_grad),
-        specs=[vmem(), vmem(), anywhere],
+        (sums, squares),
         cost_estimate=cost(2),
-    )
-
+        compiler_params=pltpu.CompilerParams(vmem_limit_bytes=16 * MB),
+    )
     return (layer_out, table_grad, mix_grad, out_grad)
 
 

time: 181 us -> 181 us (level)
  waiting for transfers between devices: 21 us -> 33.1 us
  starting transfers between devices: 10.9 us -> 4.9 us
  other arithmetic: 4.48 us -> 0.86 us
  Pallas kernels: 22.5 us -> 20 us
    reduce_scatter x0 -> x1, waiting for transfers between devices: none -> 15.8 us  [shards(): lax.psum_scatter(grads.reshape(XY * NZ * PROWS, PCOLS), 'x', scatter_dime...]
    all_to_all x2 -> x1, waiting for transfers between devices: 9.27 us -> 0.01 us  [exchange(): return lax.all_to_all(array, axes, split_axis=0, concat_axis=0, tiled=True)]
    all_to_all x2 -> x1, starting transfers between devices: 10.4 us -> 4.42 us  [exchange(): return lax.all_to_all(array, axes, split_axis=0, concat_axis=0, tiled=True)]
    pallas_call x6, Pallas kernels: 22.5 us -> 18 us  [call(): pl.pallas_call(body, out_shape=shapes[0] if one else shapes, in_specs=spe...]
    all_gather x1, waiting for transfers between devices: 0.02 us -> 3.43 us  [shards(): lax.all_gather(packed, 'z', axis=0, tiled=True).reshape(NZ, GROWS, D)]
    convert_element_type x1 -> x0, other arithmetic: 3.32 us -> none  [shards(): pair_sum = (keep.astype(F32) + theirs.astype(F32)).astype(BF16)]
    ppermute x1, waiting for transfers between devices: 0.01 us -> 2.22 us  [shards(): theirs = lax.ppermute(send, 'core', [(0, 1), (1, 0)])]
    pallas_call x0 -> x1, Pallas kernels: none -> 1.98 us  [shards(): pl.pallas_call(grads_kernel, out_shape=jax.ShapeDtypeStruct((XY, NZ, PROW...]
  transfers between devices with their start and end apart: 5 -> 5, of which waited for: 3 -> 4; matrix products, arithmetic and copies ran while one was open for 5% -> 3% of each run, Pallas kernels for 4% -> 4%
where the time goes in v4:
time: 181 us
  blocking collectives  101 us (56%)
  waiting for transfers between devices  33.1 us (18%)
  Pallas kernels  20 us (11%)
  between operations  13.8 us (8%)
  local copies, waits for them, and re-layouts  6.6 us (4%)
  starting transfers between devices  4.9 us (3%)
    all_to_all x5, blocking collectives, exchange(): return lax.all_to_all(array, axes, split_axis=0, concat_axis=0, tiled=True)  101 us
    pallas_call x6, Pallas kernels, call(): pl.pallas_call(body, out_shape=shapes[0] if one else shapes, in_specs=spe...  18 us
    reduce_scatter x1, waiting for transfers between devices, shards(): lax.psum_scatter(grads.reshape(XY * NZ * PROWS, PCOLS), 'x', scatter_dime...  15.8 us
    all_gather x1, waiting for transfers between devices, shards(): lax.all_gather(share, ('core', 'z'), axis=0, tiled=True)  11.6 us
    all_to_all x1, starting transfers between devices, exchange(): return lax.all_to_all(array, axes, split_axis=0, concat_axis=0, tiled=True)  4.42 us
    gather x1, local copies, waits for them, and re-layouts, shards(): found = item_table.at[wanted].get(mode='promise_in_bounds')  4.29 us
  transfers between devices with their start and end apart: 5, of which 4 were waited for; matrix products, arithmetic and copies ran while one was open for 3% of the time, Pallas kernels for 4%

profile of v4, /device:TPU:1, one launch (start us, length us, event | category | flops | bytes accessed | tf_op | source)
XLA Modules:
  0.0 180.6 jit_solution(15479128060227456972)
XLA Ops:
  7.2 0.9 constant_dynamic-slice_fusion
  8.1 0.1 copy-done
  8.3 0.7 pad_maximum_fusion
  9.1 1.7 shard_map.120
  10.8 15.5 %all_to_all.36 = s32[32,1,128]{2,1,0:T(1,128)S(1)} all-to-all(s32[32,1,128]{2,1,0:T(1,128)} %bitcast.27), channel_id=1, replica_groups=mesh['x'=4,'y'=4,'core'=2,'z'=8] {'x','y','core'}, dimensions={0} | all-to-all | bytes 32768 | tf_op jit(solution)/shard_map/all_to_all | solution.py:310
  26.4 4.3 %gather_fusion = bf16[256,1024]{1,0:T(8,128)(2,1)S(1)} fusion(bf16[2048,1024]{1,0:T(8,128)(2,1)} %param.9, s32[1024]{0:T(1024)S(1)} %pad_clamp_fusion), kind=kCustom, calls=%fused_computation | custom fusion | bytes 1049600 | tf_op jit(solution)/shard_map/gather | solution.py:333
  30.7 15.7 %all_to_all.37 = bf16[32,8,1024]{2,1,0:T(8,128)(2,1)} all-to-all(bf16[32,8,1024]{2,1,0:T(8,128)(2,1)S(1)} %bitcast.24), channel_id=1, replica_groups=mesh['x'=4,'y'=4,'core'=2,'z'=8] {'x','y','core'}, dimensions={0} | all-to-all | bytes 1048576 | tf_op jit(solution)/shard_map/all_to_all | solution.py:310
  46.4 11.6 %all-gather.3.cloned.1.call-done = bf16[2560,1024]{1,0:T(8,128)(2,1)} async-done(((bf16[160,1024]{1,0:T(8,128)(2,1)}), bf16[2560,1024]{1,0:T(8,128)(2,1)}) %all-gather.3.cloned.1.call-update) | async-done | bytes 5242896 | tf_op jit(solution)/shard_map/all_gather | solution.py:324
  58.0 9.3 %shard_map.121 = (bf16[128,1024]{1,0:T(8,128)(2,1)}, bf16[256,1024]{1,0:T(8,128)(2,1)}, bf16[128,3072]{1,0:T(8,128)(2,1)}, bf16[128,3072]{1,0:T(8,128)(2,1)}) custom-call(s32[1,8]{1,0:T(1,128)} %lens_ref.1, bf16[256,1024]{1,0:T(8,128)(2,1)} %bitcast.23, s32[128,128]{1,0:T(8,128)} %get-tuple-element.13.tgt_ref, bf16[2,8,160,1024]{3,2,1,0:T(8,128)(2,1)} %bitcast.21, ...), custom_call_target="tpu_custom_call" | custom-call | bytes 27000000 | tf_op jit(solution)/shard_map/pallas_call | solution.py:296
  67.3 0.4 collective-permute-start
  67.7 2.2 %collective-permute-done.theirs_ref = bf16[128,3072]{1,0:T(8,128)(2,1)S(1)} collective-permute-done((bf16[128,3072]{1,0:T(8,128)(2,1)}, bf16[128,3072]{1,0:T(8,128)(2,1)S(1)}, u32[]{:S(2)}, u32[]{:S(2)}) %collective-permute-start) | collective-permute-done | bytes 786464 | tf_op jit(solution)/shard_map/ppermute | solution.py:366
  69.9 1.1 copy-done.1
  71.0 2.0 %shard_map.124 = bf16[16,8,16,640]{3,2,1,0:T(8,128)(2,1)} custom-call(bf16[128,3072]{1,0:T(8,128)(2,1)S(1)} %copy-done.1, bf16[128,3072]{1,0:T(8,128)(2,1)S(1)} %collective-permute-done.theirs_ref), custom_call_target="tpu_custom_call" | custom-call | bytes 9000000 | tf_op jit(solution)/shard_map/pallas_call | solution.py:367
  73.1 21.6 %all_to_all.38 = bf16[32,8,1024]{2,1,0:T(8,128)(2,1)S(1)} all-to-all(bf16[32,8,1024]{2,1,0:T(8,128)(2,1)S(1)} %bitcast.26), channel_id=1, replica_groups=mesh['x'=4,'y'=4,'core'=2,'z'=8] {'x','y','core'}, dimensions={0} | all-to-all | bytes 1048576 | tf_op jit(solution)/shard_map/all_to_all | solution.py:310
  94.7 1.3 shard_map.122
  96.0 15.8 %reduce-scatter.2.cloned.1.call-done = bf16[512,640]{1,0:T(8,128)(2,1)} async-done(((bf16[2048,640]{1,0:T(8,128)(2,1)}), bf16[512,640]{1,0:T(8,128)(2,1)}) %reduce-scatter.2.cloned.1.call-update) | async-done | bytes 655376 | tf_op jit(solution)/shard_map/reduce_scatter | solution.py:379
  111.8 26.8 %all_to_all.39 = bf16[32,16,640]{2,1,0:T(8,128)(2,1)S(1)} all-to-all(bf16[32,16,640]{2,1,0:T(8,128)(2,1)} %bitcast.25), channel_id=1, replica_groups=mesh['x'=4,'y'=4,'core'=2,'z'=8] {'y','z'}, dimensions={0} | all-to-all | bytes 1310720 | tf_op jit(solution)/shard_map/all_to_all | solution.py:310
  138.6 0.1 reduce_sum.12
  138.8 21.7 %all_to_all.40.sums_ref = bf16[32,16,640]{2,1,0:T(8,128)(2,1)S(1)} all-to-all(bf16[32,16,640]{2,1,0:T(8,128)(2,1)S(1)} %broadcast_in_dim.2), channel_id=1, replica_groups=mesh['x'=4,'y'=4,'core'=2,'z'=8] {'x','y','core'}, dimensions={0} | all-to-all | bytes 1310720 | tf_op jit(solution)/shard_map/all_to_all | solution.py:310
  160.5 0.8 shard_map.125
  161.3 4.4 %all-to-all-start.5 = ((f32[8,8,128]{2,1,0:T(8,128)}), f32[8,8,128]{2,1,0:T(8,128)S(1)}, u32[]{:S(2)}, u32[]{:S(2)}) async-start(f32[8,8,128]{2,1,0:T(8,128)} %shard_map.125), calls=%async_computation.6 | async-start | bytes 65536 | tf_op jit(solution)/shard_map/all_to_all | solution.py:310
  165.7 3.4 %all-gather.5.cloned.1.call-done = bf16[1664,1024]{1,0:T(8,128)(2,1)} async-done(((bf16[208,1024]{1,0:T(8,128)(2,1)}), bf16[1664,1024]{1,0:T(8,128)(2,1)}) %all-gather.5.cloned.1.call-update) | async-done | bytes 3407888 | tf_op jit(solution)/shard_map/all_gather | solution.py:394
  169.1 3.7 %shard_map.123 = f32[256,1024]{1,0:T(8,128)} custom-call(bf16[8,208,1024]{2,1,0:T(8,128)(2,1)} %bitcast.22), custom_call_target="tpu_custom_call" | custom-call | bytes 9000000 | tf_op jit(solution)/shard_map/pallas_call | solution.py:296
  172.8 1.2 shard_map.126
  (16 shorter events, 0.4 us)
Async XLA Ops:
  7.2 1.1 copy-start
  7.2 50.8 %all-gather.3.cloned.1.call-start = ((), (), s32[]{:S(2)}) async-start(), calls=%async_computation.7 | async-start | bytes 5570560 | tf_op jit(solution)/shard_map/all_gather | solution.py:324
  9.0 102.8 %reduce-scatter.2.cloned.1.call-start = ((), (), s32[]{:S(2)}) async-start(), calls=%async_computation.9 | async-start | bytes 3276800 | tf_op jit(solution)/shard_map/reduce_scatter | solution.py:379
  67.3 2.6 %collective-permute-start = (bf16[128,3072]{1,0:T(8,128)(2,1)}, bf16[128,3072]{1,0:T(8,128)(2,1)S(1)}, u32[]{:S(2)}, u32[]{:S(2)}) collective-permute-start(bf16[128,3072]{1,0:T(8,128)(2,1)} %get-tuple-element.17), channel_id=1, source_target_pairs={{0,8},{8,0},{1,9},{9,1},{2,10},{10,2},{3,11},{11,3},{4,12},{12,4},... | collective-permute-start | bytes 2359304 | tf_op jit(solution)/shard_map/ppermute | solution.py:366
  69.9 1.1 copy-start.1
  71.0 2.1 %copy-start.2 = (bf16[256,1024]{1,0:T(8,128)(2,1)S(1)}, bf16[256,1024]{1,0:T(8,128)(2,1)}, u32[]{:S(2)}) copy-start(bf16[256,1024]{1,0:T(8,128)(2,1)} %get-tuple-element.15) | copy-start | bytes 1572868
  73.1 96.1 %all-gather.5.cloned.1.call-start = ((), (), s32[]{:S(2)}) async-start(), calls=%async_computation.8 | async-start | bytes 3833856 | tf_op jit(solution)/shard_map/all_gather | solution.py:394
  161.3 11.5 %all-to-all-start.5 = ((f32[8,8,128]{2,1,0:T(8,128)}), f32[8,8,128]{2,1,0:T(8,128)S(1)}, u32[]{:S(2)}, u32[]{:S(2)}) async-start(f32[8,8,128]{2,1,0:T(8,128)} %shard_map.125), calls=%async_computation.6 | async-start | bytes 65536 | tf_op jit(solution)/shard_map/all_to_all | solution.py:310
Sparse Core Ops, SparseCore 0:
  10.4 47.5 all-gather.2
  73.2 38.5 reduce-scatter.1
  114.2 54.9 all-gather.4

commit v5 on v4

--- a/solution.py
+++ b/solution.py
@@ -44,6 +44,26 @@
     return lax.broadcasted_iota(jnp.int32, shape, dim)
 
 
+def share_kernel(mix_ref, out_ref, share_ref, sems):
+    core = lax.axis_index("core")
+    copies = [
+        pltpu.make_async_copy(
+            mix_ref.at[:, pl.ds(pl.multiple_of(core * D, D), D)],
+            share_ref.at[pl.ds(0, TOK), :],
+            sems.at[0],
+        ),
+        pltpu.make_async_copy(
+            out_ref.at[pl.ds(pl.multiple_of(core * 32, 32), 32), :],
+            share_ref.at[pl.ds(TOK, 32), :],
+            sems.at[1],
+        ),
+    ]
+    for copy in copies:
+        copy.start()
+    for copy in copies:
+        copy.wait()
+
+
 def plan_kernel(owner_ref, row_ref, req_ref, tgt_ref):
     square = (TOK, TOK)
     lane = iota(square, 1)
@@ -76,15 +96,19 @@
     core = lax.axis_index("core")
     copies = []
     for half in range(2):
-        copies.append(
-            pltpu.make_async_copy(
-                weights_ref.at[half, :, pl.ds(0, TOK), :], wm.at[half], sems.at[half]
+        for part in range(4):
+            z = pl.ds(2 * part, 2)
+            copies.append(
+                pltpu.make_async_copy(
+                    weights_ref.at[half, z, pl.ds(0, TOK), :],
+                    wm.at[half, z],
+                    sems.at[len(copies)],
+                )
             )
-        )
     for half in range(2):
         copies.append(
             pltpu.make_async_copy(
-                weights_ref.at[half, :, pl.ds(TOK, 32), :], wo.at[:, half], sems.at[2 + half]
+                weights_ref.at[half, :, pl.ds(TOK, 32), :], wo.at[:, half], sems.at[len(copies)]
             )
         )
     for copy in copies:
@@ -109,12 +133,16 @@
         seg_col = seg_col + (other >= end).astype(jnp.int32)
     allowed = (seg_row == seg_col) & (other <= position)
 
-    copies[0].wait()
-    wm0 = wm[0].reshape(D, D)
-    mix0 = mm(normed, wm0)
-    copies[1].wait()
-    wm1 = wm[1].reshape(D, D)
-    mix1 = mm(normed, wm1)
+    mixtures = []
+    for half in range(2):
+        mixture = jnp.zeros((TOK, D), F32)
+        for part in range(4):
+            copies[4 * half + part].wait()
+            rows = wm[half, 2 * part : 2 * part + 2].reshape(2 * TOK, D)
+            mixture = mixture + mm(normed[:, 256 * part : 256 * part + 256], rows)
+        mixtures.append(mixture)
+    mix0, mix1 = mixtures
+    wm0, wm1 = wm[0].reshape(D, D), wm[1].reshape(D, D)
 
     sig0, sig1 = jax.nn.sigmoid(mix0), jax.nn.sigmoid(mix1)
     act0, act1 = (mix0 * sig0).astype(BF16), (mix1 * sig1).astype(BF16)
@@ -143,8 +171,8 @@
     scaled = ahat * gat
     gated = (scaled * gate_u).astype(BF16)
 
-    copies[2].wait()
-    copies[3].wait()
+    copies[8].wait()
+    copies[9].wait()
     w_out = wo[...].reshape(AW, D)
     ct = ct_ref[...]
     out_ref[...] = (emb + mm(gated, w_out)).astype(BF16)
@@ -201,7 +229,7 @@
         for p in range(XY):
             r, c = z * 64 + (p // 2) * 8, (p % 2) * 256
             part = grad[r : r + 8, c : c + 256]
-            buf[p, z, :, 512:PCOLS] = jnp.concatenate(
+            buf[z, p, :, 512:PCOLS] = jnp.concatenate(
                 [part[:, :128], part[:, 128:]], axis=0
             ).astype(BF16)
 
@@ -211,10 +239,10 @@
         grad = mm_tn(both(z * TOK, (z + 1) * TOK), d_mix)
         for p in range(XY):
             part = grad[8 * p : 8 * p + 8]
-            buf[p, z, :, 0:512] = jnp.concatenate(
+            buf[z, p, :, 0:512] = jnp.concatenate(
                 [part[:, :512], part[:, 512:]], axis=0
             ).astype(BF16)
-        copies.append(pltpu.make_async_copy(buf.at[:, z], out_ref.at[:, z], sems.at[z]))
+        copies.append(pltpu.make_async_copy(buf.at[z], out_ref.at[z], sems.at[z]))
         copies[-1].start()
     for copy in copies:
         copy.wait()
@@ -240,7 +268,7 @@
     )
 
 
-def table_kernel(rows_ref, out_ref, buf, sems):
+def table_kernel(rows_ref, out_ref, buf, total, sems, out_sems):
     used = OWNERS * CAP
     first = lax.axis_index("z") * 256
     copies = [
@@ -248,14 +276,26 @@
     ]
     for copy in copies:
         copy.start()
-    total = jnp.zeros((256, D), F32)
+    picks = []
     for z in range(NZ):
         copies[z].wait()
         names = buf[z, used : used + PROWS, :256].astype(F32)
         number = (names[0:1] + 128.0 * names[1:2]).astype(jnp.int32)[:, :used] - first
-        here = (iota((256, used), 0) == number).astype(F32).astype(BF16)
-        total = total + mm(here, buf[z, :used])
-    out_ref[...] = total
+        picks.append((iota((256, used), 0) == number).astype(F32).astype(BF16))
+    outs = []
+    for n in range(4):
+        cols = slice(256 * n, 256 * n + 256)
+        part = mm(picks[0], buf[0, :used, cols])
+        for z in range(1, NZ):
+            part = part + mm(picks[z], buf[z, :used, cols])
+        total[:, cols] = part
+        block = pl.ds(256 * n, 256)
+        outs.append(
+            pltpu.make_async_copy(total.at[:, block], out_ref.at[:, block], out_sems.at[n])
+        )
+        outs[-1].start()
+    for copy in outs:
+        copy.wait()
 
 
 def square_kernel(sums_ref, out_ref):
@@ -290,14 +330,14 @@
     return pl.BlockSpec(memory_space=pltpu.VMEM)
 
 
-def call(body, outs, args, specs=None, **kwargs):
+def call(body, outs, args, specs=None, outs_specs=None, **kwargs):
     shapes = [jax.ShapeDtypeStruct(s, t) for s, t in outs]
     one = len(shapes) == 1
     return pl.pallas_call(
         body,
         out_shape=shapes[0] if one else shapes,
         in_specs=specs or [vmem()] * len(args),
-        out_specs=vmem() if one else [vmem()] * len(shapes),
+        out_specs=outs_specs or (vmem() if one else [vmem()] * len(shapes)),
         **kwargs,
     )(*args)
 
@@ -313,13 +353,15 @@
 def shards(
     item_table, item_row, item_owner, user_lengths, w_mix, w_out, gain_in, gain_attn, cotangent
 ):
-    core = lax.axis_index("core")
-    share = jnp.concatenate(
-        [
-            lax.dynamic_slice(w_mix, (0, core * D), (TOK, D)),
-            lax.dynamic_slice(w_out, (core * 32, 0), (32, D)),
-        ],
-        axis=0,
+    anywhere = pl.BlockSpec(memory_space=pl.ANY)
+    share = call(
+        share_kernel,
+        [((TOK + 32, D), BF16)],
+        (w_mix, w_out),
+        specs=[anywhere, anywhere],
+        outs_specs=anywhere,
+        scratch_shapes=[pltpu.SemaphoreType.DMA((2,))],
+        compiler_params=pltpu.CompilerParams(vmem_limit_bytes=60 * MB),
     )
     weights = lax.all_gather(share, ("core", "z"), axis=0, tiled=True).reshape(2, NZ, 160, D)
 
@@ -334,7 +376,6 @@
     got = exchange(found.reshape(OWNERS, SLOTS, D), TABLE)
 
     smem = pl.BlockSpec(memory_space=pltpu.SMEM)
-    anywhere = pl.BlockSpec(memory_space=pl.ANY)
     layer_out, grad_slots, keep, send = call(
         layer_kernel,
         [
@@ -357,7 +398,7 @@
             pltpu.VMEM((2, NZ, TOK, D), BF16),
             pltpu.VMEM((NZ, 2, 32, D), BF16),
             pltpu.VMEM((2, TOK, D), BF16),
-            pltpu.SemaphoreType.DMA((4,)),
+            pltpu.SemaphoreType.DMA((10,)),
         ],
         cost_estimate=cost(9),
         compiler_params=pltpu.CompilerParams(vmem_limit_bytes=60 * MB),
@@ -366,21 +407,21 @@
     theirs = lax.ppermute(send, "core", [(0, 1), (1, 0)])
     grads = pl.pallas_call(
         grads_kernel,
-        out_shape=jax.ShapeDtypeStruct((XY, NZ, PROWS, PCOLS), BF16),
+        out_shape=jax.ShapeDtypeStruct((NZ, XY, PROWS, PCOLS), BF16),
         in_specs=[vmem(), vmem()],
         out_specs=anywhere,
         scratch_shapes=[
-            pltpu.VMEM((XY, NZ, PROWS, PCOLS), BF16),
+            pltpu.VMEM((NZ, XY, PROWS, PCOLS), BF16),
             pltpu.SemaphoreType.DMA((NZ,)),
         ],
         cost_estimate=cost(3),
         compiler_params=pltpu.CompilerParams(vmem_limit_bytes=30 * MB),
     )(keep, theirs)
-    row_sum = lax.psum_scatter(
-        grads.reshape(XY * NZ * PROWS, PCOLS), "x", scatter_dimension=0, tiled=True
-    )
-    column = exchange(row_sum.reshape(4 * NZ, PROWS, PCOLS), ("y", "z"))
-    whole = jnp.sum(column.astype(F32), axis=0).astype(BF16)
+    column = lax.psum_scatter(
+        grads.reshape(NZ * XY * PROWS, PCOLS), "z", scatter_dimension=0, tiled=True
+    )
+    plane = exchange(column.reshape(XY, PROWS, PCOLS), ("x", "y"))
+    whole = jnp.sum(plane.astype(F32), axis=0).astype(BF16)
     sums = exchange(jnp.broadcast_to(whole[None], (OWNERS, PROWS, PCOLS)), TABLE)
 
     received = exchange(grad_slots.reshape(OWNERS, SLOTS, D), TABLE)
@@ -397,7 +438,13 @@
         [((256, D), F32)],
         (gathered,),
         specs=[anywhere],
-        scratch_shapes=[pltpu.VMEM((NZ, GROWS, D), BF16), pltpu.SemaphoreType.DMA((NZ,))],
+        outs_specs=anywhere,
+        scratch_shapes=[
+            pltpu.VMEM((NZ, GROWS, D), BF16),
+            pltpu.VMEM((256, D), F32),
+            pltpu.SemaphoreType.DMA((NZ,)),
+            pltpu.SemaphoreType.DMA((4,)),
+        ],
         cost_estimate=cost(3),
         compiler_params=pltpu.CompilerParams(vmem_limit_bytes=60 * MB),
     )

time: 181 us -> 186 us (1.028)
  blocking collectives: 101 us -> 86.2 us
  Pallas kernels: 20 us -> 31.4 us
  waiting for transfers between devices: 33.1 us -> 42.9 us
    all_to_all x5, blocking collectives: 101 us -> 86.2 us  [exchange(): return lax.all_to_all(array, axes, split_axis=0, concat_axis=0, tiled=True)]
    pallas_call x6 -> x7, Pallas kernels: 18 us -> 29.5 us  [call(): pl.pallas_call(body, out_shape=shapes[0] if one else shapes, in_specs=spe...]
    all_gather x1, waiting for transfers between devices: 3.43 us -> 11.4 us  [shards(): lax.all_gather(packed, 'z', axis=0, tiled=True).reshape(NZ, GROWS, D)]
    reduce_scatter x1, waiting for transfers between devices: 15.8 us -> 18.6 us  [shards(): lax.psum_scatter(grads.reshape(NZ * XY * PROWS, PCOLS), 'z', scatter_dime...]
  transfers between devices with their start and end apart: 5 -> 5, of which waited for: 4 -> 4; matrix products, arithmetic and copies ran while one was open for 3% -> 2% of each run, Pallas kernels for 4% -> 4%
where the time goes in v5:
time: 186 us; the launch traced here: 185 us
  blocking collectives  86.2 us (46%)
  waiting for transfers between devices  42.9 us (23%)
  Pallas kernels  31.4 us (17%)
  between operations  13.8 us (7%)
  local copies, waits for them, and re-layouts  5.56 us (3%)
  starting transfers between devices  5.25 us (3%)
    all_to_all x5, blocking collectives, exchange(): return lax.all_to_all(array, axes, split_axis=0, concat_axis=0, tiled=True)  86.2 us
    pallas_call x7, Pallas kernels, call(): pl.pallas_call(body, out_shape=shapes[0] if one else shapes, in_specs=spe...  29.5 us
    reduce_scatter x1, waiting for transfers between devices, shards(): lax.psum_scatter(grads.reshape(NZ * XY * PROWS, PCOLS), 'z', scatter_dime...  18.6 us
    all_gather x1, waiting for transfers between devices, shards(): lax.all_gather(packed, 'z', axis=0, tiled=True).reshape(NZ, GROWS, D)  11.4 us
    all_gather x1, waiting for transfers between devices, shards(): lax.all_gather(share, ('core', 'z'), axis=0, tiled=True)  10.6 us
    all_to_all x1, starting transfers between devices, exchange(): return lax.all_to_all(array, axes, split_axis=0, concat_axis=0, tiled=True)  4.78 us
    gather x1, local copies, waits for them, and re-layouts, shards(): found = item_table.at[wanted].get(mode='promise_in_bounds')  4.29 us
  transfers between devices with their start and end apart: 5, of which 4 were waited for; matrix products, arithmetic and copies ran while one was open for 2% of the time, Pallas kernels for 4%

profile of v5, /device:TPU:1, one launch (start us, length us, event | category | flops | bytes accessed | tf_op | source)
XLA Modules:
  0.0 185.3 jit_solution(9259020946149593067)
XLA Ops:
  7.2 11.1 %shard_map.121 = bf16[160,1024]{1,0:T(8,128)(2,1)} custom-call(bf16[128,2048]{1,0:T(8,128)(2,1)} %mix_ref.1, bf16[64,1024]{1,0:T(8,128)(2,1)} %out_ref.1), custom_call_target="tpu_custom_call" | custom-call | tf_op jit(solution)/shard_map/pallas_call | solution.py:336
  18.4 1.7 shard_map.120
  20.1 15.5 %all_to_all.36 = s32[32,1,128]{2,1,0:T(1,128)S(1)} all-to-all(s32[32,1,128]{2,1,0:T(1,128)} %bitcast.27), channel_id=1, replica_groups=mesh['x'=4,'y'=4,'core'=2,'z'=8] {'x','y','core'}, dimensions={0} | all-to-all | bytes 32768 | tf_op jit(solution)/shard_map/all_to_all | solution.py:350
  35.5 0.1 reshape.80
  35.6 4.3 %gather_fusion = bf16[256,1024]{1,0:T(8,128)(2,1)S(1)} fusion(bf16[2048,1024]{1,0:T(8,128)(2,1)} %param.9, s32[1024]{0:T(1024)S(1)} %pad_clamp_fusion), kind=kCustom, calls=%fused_computation | custom fusion | bytes 1049600 | tf_op jit(solution)/shard_map/gather | solution.py:375
  39.9 15.7 %all_to_all.37 = bf16[32,8,1024]{2,1,0:T(8,128)(2,1)} all-to-all(bf16[32,8,1024]{2,1,0:T(8,128)(2,1)S(1)} %bitcast.24), channel_id=1, replica_groups=mesh['x'=4,'y'=4,'core'=2,'z'=8] {'x','y','core'}, dimensions={0} | all-to-all | bytes 1048576 | tf_op jit(solution)/shard_map/all_to_all | solution.py:350
  55.6 10.6 %all-gather.3.cloned.1.call-done = bf16[2560,1024]{1,0:T(8,128)(2,1)} async-done(((bf16[160,1024]{1,0:T(8,128)(2,1)}), bf16[2560,1024]{1,0:T(8,128)(2,1)}) %all-gather.3.cloned.1.call-update) | async-done | bytes 5242896 | tf_op jit(solution)/shard_map/all_gather | solution.py:366
  66.2 9.4 %shard_map.122 = (bf16[128,1024]{1,0:T(8,128)(2,1)}, bf16[256,1024]{1,0:T(8,128)(2,1)}, bf16[128,3072]{1,0:T(8,128)(2,1)}, bf16[128,3072]{1,0:T(8,128)(2,1)}) custom-call(s32[1,8]{1,0:T(1,128)} %lens_ref.1, bf16[256,1024]{1,0:T(8,128)(2,1)} %bitcast.23, s32[128,128]{1,0:T(8,128)} %get-tuple-element.13.tgt_ref, bf16[2,8,160,1024]{3,2,1,0:T(8,128)(2,1)} %bitcast.21, ...), custom_call_target="tpu_custom_call" | custom-call | bytes 27000000 | tf_op jit(solution)/shard_map/pallas_call | solution.py:336
  75.6 0.3 collective-permute-start
  76.0 2.2 %collective-permute-done.theirs_ref = bf16[128,3072]{1,0:T(8,128)(2,1)S(1)} collective-permute-done((bf16[128,3072]{1,0:T(8,128)(2,1)}, bf16[128,3072]{1,0:T(8,128)(2,1)S(1)}, u32[]{:S(2)}, u32[]{:S(2)}) %collective-permute-start) | collective-permute-done | bytes 786464 | tf_op jit(solution)/shard_map/ppermute | solution.py:407
  78.2 1.1 copy-done
  79.3 2.0 %shard_map.125 = bf16[8,16,16,640]{3,2,1,0:T(8,128)(2,1)} custom-call(bf16[128,3072]{1,0:T(8,128)(2,1)S(1)} %copy-done, bf16[128,3072]{1,0:T(8,128)(2,1)S(1)} %collective-permute-done.theirs_ref), custom_call_target="tpu_custom_call" | custom-call | bytes 9000000 | tf_op jit(solution)/shard_map/pallas_call | solution.py:408
  81.4 18.2 %all_to_all.38 = bf16[32,8,1024]{2,1,0:T(8,128)(2,1)S(1)} all-to-all(bf16[32,8,1024]{2,1,0:T(8,128)(2,1)S(1)} %bitcast.25), channel_id=1, replica_groups=mesh['x'=4,'y'=4,'core'=2,'z'=8] {'x','y','core'}, dimensions={0} | all-to-all | bytes 1048576 | tf_op jit(solution)/shard_map/all_to_all | solution.py:350
  99.6 1.3 shard_map.123
  100.9 18.6 %reduce-scatter.2.cloned.1.call-done = bf16[256,640]{1,0:T(8,128)(2,1)} async-done(((bf16[2048,640]{1,0:T(8,128)(2,1)}), bf16[256,640]{1,0:T(8,128)(2,1)}) %reduce-scatter.2.cloned.1.call-update) | async-done | bytes 327696 | tf_op jit(solution)/shard_map/reduce_scatter | solution.py:420
  119.5 14.3 %all_to_all.39 = bf16[16,16,640]{2,1,0:T(8,128)(2,1)S(1)} all-to-all(bf16[16,16,640]{2,1,0:T(8,128)(2,1)} %bitcast.26), channel_id=1, replica_groups=mesh['x'=4,'y'=4,'core'=2,'z'=8] {'x','y'}, dimensions={0} | all-to-all | bytes 655360 | tf_op jit(solution)/shard_map/all_to_all | solution.py:350
  133.8 0.1 reduce_sum.12
  133.9 0.1 broadcast_in_dim.2
  133.9 22.6 %all_to_all.40.sums_ref = bf16[32,16,640]{2,1,0:T(8,128)(2,1)S(1)} all-to-all(bf16[32,16,640]{2,1,0:T(8,128)(2,1)S(1)} %broadcast_in_dim.2), channel_id=1, replica_groups=mesh['x'=4,'y'=4,'core'=2,'z'=8] {'x','y','core'}, dimensions={0} | all-to-all | bytes 1310720 | tf_op jit(solution)/shard_map/all_to_all | solution.py:350
  156.5 0.8 shard_map.126
  157.3 4.8 %all-to-all-start.5 = ((f32[8,8,128]{2,1,0:T(8,128)}), f32[8,8,128]{2,1,0:T(8,128)S(1)}, u32[]{:S(2)}, u32[]{:S(2)}) async-start(f32[8,8,128]{2,1,0:T(8,128)} %shard_map.126), calls=%async_computation.6 | async-start | bytes 65536 | tf_op jit(solution)/shard_map/all_to_all | solution.py:350
  162.1 11.4 %all-gather.5.cloned.1.call-done = bf16[1664,1024]{1,0:T(8,128)(2,1)} async-done(((bf16[208,1024]{1,0:T(8,128)(2,1)}), bf16[1664,1024]{1,0:T(8,128)(2,1)}) %all-gather.5.cloned.1.call-update) | async-done | bytes 3407888 | tf_op jit(solution)/shard_map/all_gather | solution.py:435
  173.5 4.0 %shard_map.124 = f32[256,1024]{1,0:T(8,128)} custom-call(bf16[8,208,1024]{2,1,0:T(8,128)(2,1)} %bitcast.22), custom_call_target="tpu_custom_call" | custom-call | bytes 9000000 | tf_op jit(solution)/shard_map/pallas_call | solution.py:336
  177.6 1.2 shard_map.127
  (12 shorter events, 0.2 us)
Async XLA Ops:
  7.2 59.1 %all-gather.3.cloned.1.call-start = ((), (), s32[]{:S(2)}) async-start(), calls=%async_computation.7 | async-start | bytes 5570560 | tf_op jit(solution)/shard_map/all_gather | solution.py:366
  18.3 101.2 %reduce-scatter.2.cloned.1.call-start = ((), (), s32[]{:S(2)}) async-start(), calls=%async_computation.9 | async-start | bytes 2949120 | tf_op jit(solution)/shard_map/reduce_scatter | solution.py:420
  75.6 2.6 %collective-permute-start = (bf16[128,3072]{1,0:T(8,128)(2,1)}, bf16[128,3072]{1,0:T(8,128)(2,1)S(1)}, u32[]{:S(2)}, u32[]{:S(2)}) collective-permute-start(bf16[128,3072]{1,0:T(8,128)(2,1)} %get-tuple-element.17), channel_id=1, source_target_pairs={{0,8},{8,0},{1,9},{9,1},{2,10},{10,2},{3,11},{11,3},{4,12},{12,4},... | collective-permute-start | bytes 2359304 | tf_op jit(solution)/shard_map/ppermute | solution.py:407
  78.2 1.1 copy-start
  79.3 2.1 %copy-start.1 = (bf16[256,1024]{1,0:T(8,128)(2,1)S(1)}, bf16[256,1024]{1,0:T(8,128)(2,1)}, u32[]{:S(2)}) copy-start(bf16[256,1024]{1,0:T(8,128)(2,1)} %get-tuple-element.15) | copy-start | bytes 1572868
  81.3 92.2 %all-gather.5.cloned.1.call-start = ((), (), s32[]{:S(2)}) async-start(), calls=%async_computation.8 | async-start | bytes 3833856 | tf_op jit(solution)/shard_map/all_gather | solution.py:435
  157.3 20.3 %all-to-all-start.5 = ((f32[8,8,128]{2,1,0:T(8,128)}), f32[8,8,128]{2,1,0:T(8,128)S(1)}, u32[]{:S(2)}, u32[]{:S(2)}) async-start(f32[8,8,128]{2,1,0:T(8,128)} %shard_map.126), calls=%async_computation.6 | async-start | bytes 65536 | tf_op jit(solution)/shard_map/all_to_all | solution.py:350
Sparse Core Ops, SparseCore 0:
  18.4 47.7 all-gather.2
  81.5 38.0 reduce-scatter.1
  121.9 51.5 all-gather.4

commit v6 on v5

--- a/solution.py
+++ b/solution.py
@@ -20,7 +20,7 @@
 PROWS = 16
 PCOLS = 640
 FACT = 3072
-GROWS = OWNERS * CAP + 16
+GROWS = OWNERS * CAP
 TABLE = ("x", "y", "core")
 ALL = ("x", "y", "core", "z")
 F32 = jnp.float32
@@ -44,24 +44,10 @@
     return lax.broadcasted_iota(jnp.int32, shape, dim)
 
 
-def share_kernel(mix_ref, out_ref, share_ref, sems):
+def share_kernel(mix_ref, out_ref, share_ref):
     core = lax.axis_index("core")
-    copies = [
-        pltpu.make_async_copy(
-            mix_ref.at[:, pl.ds(pl.multiple_of(core * D, D), D)],
-            share_ref.at[pl.ds(0, TOK), :],
-            sems.at[0],
-        ),
-        pltpu.make_async_copy(
-            out_ref.at[pl.ds(pl.multiple_of(core * 32, 32), 32), :],
-            share_ref.at[pl.ds(TOK, 32), :],
-            sems.at[1],
-        ),
-    ]
-    for copy in copies:
-        copy.start()
-    for copy in copies:
-        copy.wait()
+    share_ref[:TOK] = mix_ref[:, pl.ds(pl.multiple_of(core * D, D), D)]
+    share_ref[TOK:] = out_ref[pl.ds(pl.multiple_of(core * 32, 32), 32), :]
 
 
 def plan_kernel(owner_ref, row_ref, req_ref, tgt_ref):
@@ -89,7 +75,7 @@
 
 
 def layer_kernel(
-    lens_ref, got_ref, tgt_ref, weights_ref, gin_ref, gat_ref, ct_ref,
+    lens_ref, got_ref, tgt_ref, weights_ref, gin_ref, gat_ref, ct_ref, after_ref,
     out_ref, slots_ref, keep_ref, send_ref,
     wm, wo, dmx, sems,
 ):
@@ -248,54 +234,59 @@
         copy.wait()
 
 
-def pack_kernel(rows_ref, asked_ref, out_ref):
-    used = OWNERS * CAP
-    r, k = iota((used, OWNERS * SLOTS), 0), iota((used, OWNERS * SLOTS), 1)
-    take = (r // CAP == k // SLOTS) & (r % CAP == k % SLOTS)
-    out_ref[:used] = mm(take.astype(F32).astype(BF16), rows_ref[...]).astype(BF16)
-    asked = asked_ref[...]
-    owner = (iota((256, OWNERS), 0) // CAP == iota((256, OWNERS), 1)).astype(F32).astype(BF16)
-    slot = iota((256, 128), 0) % CAP == iota((256, 128), 1)
-    parts = []
-    for part in (asked & 127, asked >> 7):
-        spread = mm(owner, part.astype(F32).astype(BF16))
-        column = jnp.sum(jnp.where(slot, spread, 0.0), axis=1, keepdims=True)
-        parts.append(jnp.broadcast_to(column, (256, 128)).T[:PROWS])
-    which = iota((PROWS, 256), 0)
-    numbers = jnp.where(which == 0, parts[0], jnp.where(which == 1, parts[1], 0.0))
-    out_ref[used:] = jnp.concatenate(
-        [numbers.astype(BF16), jnp.zeros((PROWS, D - 256), BF16)], axis=1
-    )
-
-
-def table_kernel(rows_ref, out_ref, buf, total, sems, out_sems):
-    used = OWNERS * CAP
+def pack_kernel(rows_ref, out_ref):
+    r, k = iota((GROWS, OWNERS * SLOTS), 0), iota((GROWS, OWNERS * SLOTS), 1)
+    take = (r // CAP) * SLOTS + r % CAP == k
+    out_ref[...] = mm(take.astype(F32).astype(BF16), rows_ref[...]).astype(BF16)
+
+
+def names_kernel(asked_ref, out_ref):
     first = lax.axis_index("z") * 256
+    count = NZ * GROWS
+    asked = asked_ref[...].reshape(NZ * OWNERS, 128)
+    row, col = iota((count, NZ * OWNERS), 0), iota((count, NZ * OWNERS), 1)
+    owner = (row // CAP == col).astype(F32).astype(BF16)
+    lane = iota((count, 128), 1)
+    spread = mm(owner, (asked & 127).astype(F32).astype(BF16)) + 128.0 * mm(
+        owner, (asked >> 7).astype(F32).astype(BF16)
+    )
+    column = jnp.sum(
+        jnp.where(iota((count, 128), 0) % CAP == lane, spread, 0.0), axis=1, keepdims=True
+    )
+    names = jnp.zeros((128, 128), F32)
+    for line in range(count // 128):
+        names = jnp.where(
+            iota((128, 128), 1) == line, column[128 * line : 128 * line + 128], names
+        )
+    out_ref[...] = names.T[:PROWS].astype(jnp.int32) - first
+
+
+def table_kernel(rows_ref, names_ref, after_ref, out_ref, buf, sems):
+    half = NZ * GROWS // 2
     copies = [
-        pltpu.make_async_copy(rows_ref.at[z], buf.at[z], sems.at[z]) for z in range(NZ)
+        pltpu.make_async_copy(
+            rows_ref.at[pl.ds(part * half, half), :], buf.at[part], sems.at[part]
+        )
+        for part in range(2)
     ]
     for copy in copies:
         copy.start()
-    picks = []
-    for z in range(NZ):
-        copies[z].wait()
-        names = buf[z, used : used + PROWS, :256].astype(F32)
-        number = (names[0:1] + 128.0 * names[1:2]).astype(jnp.int32)[:, :used] - first
-        picks.append((iota((256, used), 0) == number).astype(F32).astype(BF16))
-    outs = []
-    for n in range(4):
-        cols = slice(256 * n, 256 * n + 256)
-        part = mm(picks[0], buf[0, :used, cols])
-        for z in range(1, NZ):
-            part = part + mm(picks[z], buf[z, :used, cols])
-        total[:, cols] = part
-        block = pl.ds(256 * n, 256)
-        outs.append(
-            pltpu.make_async_copy(total.at[:, block], out_ref.at[:, block], out_sems.at[n])
-        )
-        outs[-1].start()
-    for copy in outs:
-        copy.wait()
+    place = iota((256, 128), 0)
+    lines = half // 128
+    for part in range(2):
+        pick = jnp.concatenate(
+            [
+                (place == names_ref[line : line + 1, :]).astype(F32).astype(BF16)
+                for line in range(part * lines, (part + 1) * lines)
+            ],
+            axis=1,
+        )
+        copies[part].wait()
+        total = mm(pick, buf[part])
+        if part == 0:
+            out_ref[...] = total
+        else:
+            out_ref[...] += total
 
 
 def square_kernel(sums_ref, out_ref):
@@ -354,15 +345,8 @@
     item_table, item_row, item_owner, user_lengths, w_mix, w_out, gain_in, gain_attn, cotangent
 ):
     anywhere = pl.BlockSpec(memory_space=pl.ANY)
-    share = call(
-        share_kernel,
-        [((TOK + 32, D), BF16)],
-        (w_mix, w_out),
-        specs=[anywhere, anywhere],
-        outs_specs=anywhere,
-        scratch_shapes=[pltpu.SemaphoreType.DMA((2,))],
-        compiler_params=pltpu.CompilerParams(vmem_limit_bytes=60 * MB),
-    )
+    pinned = pl.BlockSpec(memory_space=pltpu.HBM)
+    share = call(share_kernel, [((TOK + 32, D), BF16)], (w_mix, w_out))
     weights = lax.all_gather(share, ("core", "z"), axis=0, tiled=True).reshape(2, NZ, 160, D)
 
     requests, target = call(
@@ -371,6 +355,12 @@
         (item_owner.reshape(1, TOK), item_row.reshape(1, TOK)),
     )
     asked = exchange(requests, TABLE)
+    names = call(
+        names_kernel,
+        [((PROWS, 128), jnp.int32)],
+        (exchange(jnp.broadcast_to(asked[None], (NZ, OWNERS, 128)), "z"),),
+        cost_estimate=cost(1),
+    )
     wanted = asked[:, :SLOTS].reshape(OWNERS * SLOTS)
     found = item_table.at[wanted].get(mode="promise_in_bounds")
     got = exchange(found.reshape(OWNERS, SLOTS, D), TABLE)
@@ -392,8 +382,9 @@
             gain_in.reshape(1, D),
             gain_attn.reshape(1, AW),
             cotangent,
+            names,
         ),
-        specs=[smem, vmem(), vmem(), anywhere, vmem(), vmem(), vmem()],
+        specs=[smem, vmem(), vmem(), pinned, vmem(), vmem(), vmem(), anywhere],
         scratch_shapes=[
             pltpu.VMEM((2, NZ, TOK, D), BF16),
             pltpu.VMEM((NZ, 2, 32, D), BF16),
@@ -401,7 +392,7 @@
             pltpu.SemaphoreType.DMA((10,)),
         ],
         cost_estimate=cost(9),
-        compiler_params=pltpu.CompilerParams(vmem_limit_bytes=60 * MB),
+        compiler_params=pltpu.CompilerParams(vmem_limit_bytes=32 * MB),
     )
 
     theirs = lax.ppermute(send, "core", [(0, 1), (1, 0)])
@@ -428,27 +419,11 @@
     packed = call(
         pack_kernel,
         [((GROWS, D), BF16)],
-        (received.reshape(OWNERS * SLOTS, D), asked),
+        (received.reshape(OWNERS * SLOTS, D),),
         cost_estimate=cost(2),
         compiler_params=pltpu.CompilerParams(vmem_limit_bytes=16 * MB),
     )
-    gathered = lax.all_gather(packed, "z", axis=0, tiled=True).reshape(NZ, GROWS, D)
-    table_grad = call(
-        table_kernel,
-        [((256, D), F32)],
-        (gathered,),
-        specs=[anywhere],
-        outs_specs=anywhere,
-        scratch_shapes=[
-            pltpu.VMEM((NZ, GROWS, D), BF16),
-            pltpu.VMEM((256, D), F32),
-            pltpu.SemaphoreType.DMA((NZ,)),
-            pltpu.SemaphoreType.DMA((4,)),
-        ],
-        cost_estimate=cost(3),
-        compiler_params=pltpu.CompilerParams(vmem_limit_bytes=60 * MB),
-    )
-
+    gathered = lax.all_gather(packed, "z", axis=0, tiled=True)
     squares = call(
         square_kernel,
         [((NZ, 8, 128), F32)],
@@ -463,6 +438,18 @@
         (sums, squares),
         cost_estimate=cost(2),
         compiler_params=pltpu.CompilerParams(vmem_limit_bytes=16 * MB),
+    )
+    table_grad = call(
+        table_kernel,
+        [((256, D), F32)],
+        (gathered, names, out_grad),
+        specs=[pinned, vmem(), anywhere],
+        scratch_shapes=[
+            pltpu.VMEM((2, NZ * GROWS // 2, D), BF16),
+            pltpu.SemaphoreType.DMA((2,)),
+        ],
+        cost_estimate=cost(3),
+        compiler_params=pltpu.CompilerParams(vmem_limit_bytes=60 * MB),
     )
     return (layer_out, table_grad, mix_grad, out_grad)
 

time: 186 us -> 177 us (0.952)
  Pallas kernels: 31.4 us -> 21.7 us
  starting transfers between devices: 5.25 us -> 14.2 us
  waiting for transfers between devices: 42.9 us -> 35.8 us
  blocking collectives: 86.2 us -> 81.2 us
  local copies, waits for them, and re-layouts: 5.56 us -> 9.15 us
    all_to_all x1 -> x2, waiting for transfers between devices: 0.01 us -> 13.8 us  [exchange(): return lax.all_to_all(array, axes, split_axis=0, concat_axis=0, tiled=True)]
    all_gather x1, waiting for transfers between devices: 11.4 us -> 0.83 us  [shards(): gathered = lax.all_gather(packed, 'z', axis=0, tiled=True)]
    all_gather x1, waiting for transfers between devices: 10.6 us -> 0.01 us  [shards(): lax.all_gather(share, ('core', 'z'), axis=0, tiled=True)]
    pallas_call x7 -> x8, Pallas kernels: 29.5 us -> 19.7 us  [call(): pl.pallas_call(body, out_shape=shapes[0] if one else shapes, in_specs=spe...]
    all_to_all x1 -> x2, starting transfers between devices: 4.78 us -> 14 us  [exchange(): return lax.all_to_all(array, axes, split_axis=0, concat_axis=0, tiled=True)]
    all_to_all x5, blocking collectives: 86.2 us -> 81.2 us  [exchange(): return lax.all_to_all(array, axes, split_axis=0, concat_axis=0, tiled=True)]
    unnamed x4 -> x16, local copies, waits for them, and re-layouts: 1.14 us -> 3.2 us
  transfers between devices with their start and end apart: 5 -> 6, of which waited for: 4 -> 5; matrix products, arithmetic and copies ran while one was open for 2% -> 3% of each run, Pallas kernels for 4% -> 4%
where the time goes in v6:
time: 177 us; the launch traced here: 176 us
  blocking collectives  81.2 us (46%)
  waiting for transfers between devices  35.8 us (20%)
  Pallas kernels  21.7 us (12%)
  starting transfers between devices  14.2 us (8%)
  between operations  13.9 us (8%)
  local copies, waits for them, and re-layouts  9.15 us (5%)
    all_to_all x5, blocking collectives, exchange(): return lax.all_to_all(array, axes, split_axis=0, concat_axis=0, tiled=True)  81.2 us
    pallas_call x8, Pallas kernels, call(): pl.pallas_call(body, out_shape=shapes[0] if one else shapes, in_specs=spe...  19.7 us
    reduce_scatter x1, waiting for transfers between devices, shards(): lax.psum_scatter(grads.reshape(NZ * XY * PROWS, PCOLS), 'z', scatter_dime...  18.8 us
    all_to_all x2, starting transfers between devices, exchange(): return lax.all_to_all(array, axes, split_axis=0, concat_axis=0, tiled=True)  14 us
    all_to_all x2, waiting for transfers between devices, exchange(): return lax.all_to_all(array, axes, split_axis=0, concat_axis=0, tiled=True)  13.8 us
    gather x1, local copies, waits for them, and re-layouts, shards(): found = item_table.at[wanted].get(mode='promise_in_bounds')  5.14 us
  transfers between devices with their start and end apart: 6, of which 5 were waited for; matrix products, arithmetic and copies ran while one was open for 3% of the time, Pallas kernels for 4%

profile of v6, /device:TPU:1, one launch (start us, length us, event | category | flops | bytes accessed | tf_op | source)
XLA Modules:
  0.0 176.1 jit_solution(8911307582866048234)
XLA Ops:
  7.3 1.8 %shard_map.121 = bf16[160,1024]{1,0:T(8,128)(2,1)} custom-call(bf16[128,2048]{1,0:T(8,128)(2,1)} %mix_ref.1, bf16[64,1024]{1,0:T(8,128)(2,1)} %out_ref.1), custom_call_target="tpu_custom_call" | custom-call | tf_op jit(solution)/shard_map/pallas_call | solution.py:327
  9.1 1.7 shard_map.120
  10.9 15.6 %all_to_all.42 = s32[32,1,128]{2,1,0:T(1,128)S(1)} all-to-all(s32[32,1,128]{2,1,0:T(1,128)} %bitcast.26), channel_id=1, replica_groups=mesh['x'=4,'y'=4,'core'=2,'z'=8] {'x','y','core'}, dimensions={0} | all-to-all | bytes 32768 | tf_op jit(solution)/shard_map/all_to_all | solution.py:341
  26.5 0.7 broadcast_in_dim.4
  27.2 8.2 %all-to-all-start.2 = ((s32[8,32,128]{2,1,0:T(8,128)}), s32[8,32,128]{2,1,0:T(8,128)S(1)}, u32[]{:S(2)}, u32[]{:S(2)}) async-start(s32[8,32,128]{2,1,0:T(8,128)} %broadcast_in_dim.4), calls=%async_computation.2 | async-start | bytes 262144 | tf_op jit(solution)/shard_map/all_to_all | solution.py:341
  35.4 5.1 %gather_fusion = bf16[256,1024]{1,0:T(8,128)(2,1)} fusion(bf16[2048,1024]{1,0:T(8,128)(2,1)} %param.9, s32[1024]{0:T(1024)S(1)} %pad_clamp_fusion), kind=kCustom, calls=%fused_computation | custom fusion | bytes 1049600 | tf_op jit(solution)/shard_map/gather | solution.py:365
  40.6 4.4 %all-to-all-done.2.asked_ref = s32[8,32,128]{2,1,0:T(8,128)S(1)} async-done(((s32[8,32,128]{2,1,0:T(8,128)}), s32[8,32,128]{2,1,0:T(8,128)S(1)}, u32[]{:S(2)}, u32[]{:S(2)}) %all-to-all-start.2) | async-done | bytes 131104 | tf_op jit(solution)/shard_map/all_to_all | solution.py:341
  44.9 5.8 %all-to-all-start.1 = ((bf16[32,8,1024]{2,1,0:T(8,128)(2,1)}), bf16[32,8,1024]{2,1,0:T(8,128)(2,1)S(1)}, u32[]{:S(2)}, u32[]{:S(2)}) async-start(bf16[32,8,1024]{2,1,0:T(8,128)(2,1)} %bitcast.6), calls=%async_computation.1 | async-start | bytes 1048576 | tf_op jit(solution)/shard_map/all_to_all | solution.py:341
  50.8 2.3 %shard_map.122.after_ref.names_ref = s32[16,128]{1,0:T(8,128)} custom-call(s32[8,32,128]{2,1,0:T(8,128)} %copy-done.7), custom_call_target="tpu_custom_call" | custom-call | bytes 3000000 | tf_op jit(solution)/shard_map/pallas_call | solution.py:327
  53.1 9.4 %all-to-all-done.1 = bf16[32,8,1024]{2,1,0:T(8,128)(2,1)S(1)} async-done(((bf16[32,8,1024]{2,1,0:T(8,128)(2,1)}), bf16[32,8,1024]{2,1,0:T(8,128)(2,1)S(1)}, u32[]{:S(2)}, u32[]{:S(2)}) %all-to-all-start.1) | async-done | bytes 524320 | tf_op jit(solution)/shard_map/all_to_all | solution.py:341
  62.6 2.5 %copy-done = bf16[2560,1024]{1,0:T(8,128)(2,1)S(1)} copy-done((bf16[2560,1024]{1,0:T(8,128)(2,1)S(1)}, bf16[2560,1024]{1,0:T(8,128)(2,1)}, u32[]{:S(2)}) %copy-start) | copy-done | bytes 5242904
  65.0 0.7 copy-done.2
  65.7 7.2 %shard_map.123 = (bf16[128,1024]{1,0:T(8,128)(2,1)}, bf16[256,1024]{1,0:T(8,128)(2,1)S(1)}, bf16[128,3072]{1,0:T(8,128)(2,1)S(1)}, bf16[128,3072]{1,0:T(8,128)(2,1)S(1)}) custom-call(s32[1,8]{1,0:T(1,128)S(1)} %copy-done.6, bf16[256,1024]{1,0:T(8,128)(2,1)S(1)} %bitcast.18, s32[128,128]{1,0:T(8,128)S(1)} %copy-done.3, ...), custom_call_target="tpu_custom_call" | custom-call | bytes 27000000 | tf_op jit(solution)/shard_map/pallas_call | solution.py:327
  73.1 2.3 %collective-permute-done.theirs_ref = bf16[128,3072]{1,0:T(8,128)(2,1)S(1)} collective-permute-done((bf16[128,3072]{1,0:T(8,128)(2,1)S(1)}, bf16[128,3072]{1,0:T(8,128)(2,1)S(1)}, u32[]{:S(2)}, u32[]{:S(2)}) %collective-permute-start) | collective-permute-done | bytes 786464 | tf_op jit(solution)/shard_map/ppermute | solution.py:398
  75.3 2.0 %shard_map.125 = bf16[8,16,16,640]{3,2,1,0:T(8,128)(2,1)} custom-call(bf16[128,3072]{1,0:T(8,128)(2,1)S(1)} %get-tuple-element.16.keep_ref, bf16[128,3072]{1,0:T(8,128)(2,1)S(1)} %collective-permute-done.theirs_ref), custom_call_target="tpu_custom_call" | custom-call | bytes 9000000 | tf_op jit(solution)/shard_map/pallas_call | solution.py:399
  77.4 16.7 %all_to_all.43 = bf16[32,8,1024]{2,1,0:T(8,128)(2,1)S(1)} all-to-all(bf16[32,8,1024]{2,1,0:T(8,128)(2,1)S(1)} %bitcast.20), channel_id=1, replica_groups=mesh['x'=4,'y'=4,'core'=2,'z'=8] {'x','y','core'}, dimensions={0} | all-to-all | bytes 1048576 | tf_op jit(solution)/shard_map/all_to_all | solution.py:341
  94.2 1.0 shard_map.124
  95.2 18.8 %reduce-scatter.2.cloned.1.call-done = bf16[256,640]{1,0:T(8,128)(2,1)} async-done(((bf16[2048,640]{1,0:T(8,128)(2,1)}), bf16[256,640]{1,0:T(8,128)(2,1)}) %reduce-scatter.2.cloned.1.call-update) | async-done | bytes 327696 | tf_op jit(solution)/shard_map/reduce_scatter | solution.py:411
  114.1 14.2 %all_to_all.44 = bf16[16,16,640]{2,1,0:T(8,128)(2,1)S(1)} all-to-all(bf16[16,16,640]{2,1,0:T(8,128)(2,1)} %bitcast.23), channel_id=1, replica_groups=mesh['x'=4,'y'=4,'core'=2,'z'=8] {'x','y'}, dimensions={0} | all-to-all | bytes 655360 | tf_op jit(solution)/shard_map/all_to_all | solution.py:341
  128.4 22.6 %all_to_all.45.sums_ref = bf16[32,16,640]{2,1,0:T(8,128)(2,1)S(1)} all-to-all(bf16[32,16,640]{2,1,0:T(8,128)(2,1)S(1)} %broadcast_in_dim.5), channel_id=1, replica_groups=mesh['x'=4,'y'=4,'core'=2,'z'=8] {'x','y','core'}, dimensions={0} | all-to-all | bytes 1310720 | tf_op jit(solution)/shard_map/all_to_all | solution.py:341
  151.1 12.1 %all_to_all.46.squares_ref = f32[8,8,128]{2,1,0:T(8,128)S(1)} all-to-all(f32[8,8,128]{2,1,0:T(8,128)S(1)} %shard_map.126), channel_id=1, replica_groups=mesh['x'=4,'y'=4,'core'=2,'z'=8] {'z'}, dimensions={0} | all-to-all | bytes 65536 | tf_op jit(solution)/shard_map/all_to_all | solution.py:341
  163.3 1.2 shard_map.127
  164.5 0.8 all-gather.5.cloned.1.call-done.rows_ref
  165.3 4.2 %shard_map.128 = f32[256,1024]{1,0:T(8,128)} custom-call(bf16[1536,1024]{1,0:T(8,128)(2,1)} %all-gather.5.cloned.1.call-done.rows_ref, s32[16,128]{1,0:T(8,128)} %shard_map.122.after_ref.names_ref, f32[64,1024]{1,0:T(8,128)} %get-tuple-element.11.after_ref), custom_call_target="tpu_custom_call" | custom-call | bytes 9000000 | tf_op jit(solution)/shard_map/pallas_call | solution.py:327
  (28 shorter events, 0.7 us)
Async XLA Ops:
  7.2 55.4 %copy-start.1 = (bf16[128,1024]{1,0:T(8,128)(2,1)S(1)}, bf16[128,1024]{1,0:T(8,128)(2,1)}, u32[]{:S(2)}) copy-start(bf16[128,1024]{1,0:T(8,128)(2,1)} %ct_ref.1) | copy-start | bytes 786436
  7.2 55.4 %copy-start.5 = (f32[512]{0:T(512)S(1)}, f32[512]{0:T(512)}, u32[]{:S(2)}) copy-start(f32[512]{0:T(512)} %param.16) | copy-start | bytes 6148
  7.2 55.3 %copy-start.4 = (f32[1024]{0:T(1024)S(1)}, f32[1024]{0:T(1024)}, u32[]{:S(2)}) copy-start(f32[1024]{0:T(1024)} %param.15) | copy-start | bytes 12292
  7.2 55.3 %copy-start.6 = (s32[1,8]{1,0:T(1,128)S(1)}, s32[1,8]{1,0:T(1,128)}, u32[]{:S(2)}) copy-start(s32[1,8]{1,0:T(1,128)} %lens_ref.1) | copy-start | bytes 100
  7.2 55.3 %all-gather.3.cloned.1.call-start = ((), (), s32[]{:S(2)}) async-start(), calls=%async_computation.8 | async-start | bytes 5570560 | tf_op jit(solution)/shard_map/all_gather | solution.py:350
  10.9 51.7 %copy-start.3 = (s32[128,128]{1,0:T(8,128)S(1)}, s32[128,128]{1,0:T(8,128)}, u32[]{:S(2)}) copy-start(s32[128,128]{1,0:T(8,128)} %get-tuple-element.13.tgt_ref) | copy-start | bytes 196612
  27.2 17.7 %all-to-all-start.2 = ((s32[8,32,128]{2,1,0:T(8,128)}), s32[8,32,128]{2,1,0:T(8,128)S(1)}, u32[]{:S(2)}, u32[]{:S(2)}) async-start(s32[8,32,128]{2,1,0:T(8,128)} %broadcast_in_dim.4), calls=%async_computation.2 | async-start | bytes 262144 | tf_op jit(solution)/shard_map/all_to_all | solution.py:341
  44.9 5.9 %copy-start.7 = (s32[8,32,128]{2,1,0:T(8,128)}, s32[8,32,128]{2,1,0:T(8,128)S(1)}, u32[]{:S(2)}) copy-start(s32[8,32,128]{2,1,0:T(8,128)S(1)} %all-to-all-done.2.asked_ref) | copy-start | bytes 393220
  44.9 17.6 %all-to-all-start.1 = ((bf16[32,8,1024]{2,1,0:T(8,128)(2,1)}), bf16[32,8,1024]{2,1,0:T(8,128)(2,1)S(1)}, u32[]{:S(2)}, u32[]{:S(2)}) async-start(bf16[32,8,1024]{2,1,0:T(8,128)(2,1)} %bitcast.6), calls=%async_computation.1 | async-start | bytes 1048576 | tf_op jit(solution)/shard_map/all_to_all | solution.py:341
  50.8 63.3 %reduce-scatter.2.cloned.1.call-start = ((), (), s32[]{:S(2)}) async-start(), calls=%async_computation.10 | async-start | bytes 2949120 | tf_op jit(solution)/shard_map/reduce_scatter | solution.py:411
  62.6 2.5 %copy-start = (bf16[2560,1024]{1,0:T(8,128)(2,1)S(1)}, bf16[2560,1024]{1,0:T(8,128)(2,1)}, u32[]{:S(2)}) copy-start(bf16[2560,1024]{1,0:T(8,128)(2,1)} %all-gather.3.cloned.1.call-done) | copy-start | bytes 15728644
  65.0 0.7 copy-start.2
  73.0 2.4 %collective-permute-start = (bf16[128,3072]{1,0:T(8,128)(2,1)S(1)}, bf16[128,3072]{1,0:T(8,128)(2,1)S(1)}, u32[]{:S(2)}, u32[]{:S(2)}) collective-permute-start(bf16[128,3072]{1,0:T(8,128)(2,1)S(1)} %get-tuple-element.17), channel_id=1, source_target_pairs={{0,8},{8,0},{1,9},{9,1},{2,10},{10,2},{3,11},{11,3},{4,12},{12,4},... | collective-permute-start | bytes 2359304 | tf_op jit(solution)/shard_map/ppermute | solution.py:398
  77.4 87.9 %all-gather.5.cloned.1.call-start = ((), (), s32[]{:S(2)}) async-start(), calls=%async_computation.9 | async-start | bytes 3538944 | tf_op jit(solution)/shard_map/all_gather | solution.py:426
Sparse Core Ops, SparseCore 0:
  10.4 50.4 all-gather.2
  77.5 36.5 reduce-scatter.1
  116.4 48.8 all-gather.4

commit v7 on v6

--- a/solution.py
+++ b/solution.py
@@ -20,7 +20,9 @@
 PROWS = 16
 PCOLS = 640
 FACT = 3072
-GROWS = OWNERS * CAP
+USED = OWNERS * CAP
+LATE = 160
+EARLY = USED - LATE
 TABLE = ("x", "y", "core")
 ALL = ("x", "y", "core", "z")
 F32 = jnp.float32
@@ -75,7 +77,7 @@
 
 
 def layer_kernel(
-    lens_ref, got_ref, tgt_ref, weights_ref, gin_ref, gat_ref, ct_ref, after_ref,
+    lens_ref, got_ref, tgt_ref, weights_ref, gin_ref, gat_ref, ct_ref,
     out_ref, slots_ref, keep_ref, send_ref,
     wm, wo, dmx, sems,
 ):
@@ -234,24 +236,41 @@
         copy.wait()
 
 
-def pack_kernel(rows_ref, out_ref):
-    r, k = iota((GROWS, OWNERS * SLOTS), 0), iota((GROWS, OWNERS * SLOTS), 1)
-    take = (r // CAP) * SLOTS + r % CAP == k
-    out_ref[...] = mm(take.astype(F32).astype(BF16), rows_ref[...]).astype(BF16)
-
-
-def names_kernel(asked_ref, out_ref):
+def pack_kernel(rows_ref, asked_ref, late_ref, early_ref):
+    r, k = iota((USED, OWNERS * SLOTS), 0), iota((USED, OWNERS * SLOTS), 1)
+    take = ((r // CAP) * SLOTS + r % CAP == k).astype(F32).astype(BF16)
+    rows = mm(take, rows_ref[...]).astype(BF16)
+    late_ref[...] = rows[:LATE]
+    early_ref[:EARLY] = rows[LATE:]
+    asked = asked_ref[...]
+    owner = (iota((256, OWNERS), 0) // CAP == iota((256, OWNERS), 1)).astype(F32).astype(BF16)
+    slot = iota((256, 128), 0) % CAP == iota((256, 128), 1)
+    parts = []
+    for part in (asked & 127, asked >> 7):
+        spread = mm(owner, part.astype(F32).astype(BF16))
+        column = jnp.sum(jnp.where(slot, spread, 0.0), axis=1, keepdims=True)
+        parts.append(jnp.broadcast_to(column, (256, 128)).T[:PROWS])
+    which = iota((PROWS, 256), 0)
+    numbers = jnp.where(which == 0, parts[0], jnp.where(which == 1, parts[1], 0.0))
+    early_ref[EARLY:] = jnp.concatenate(
+        [numbers.astype(BF16), jnp.zeros((PROWS, D - 256), BF16)], axis=1
+    )
+
+
+def names_kernel(early_ref, out_ref):
     first = lax.axis_index("z") * 256
-    count = NZ * GROWS
-    asked = asked_ref[...].reshape(NZ * OWNERS, 128)
-    row, col = iota((count, NZ * OWNERS), 0), iota((count, NZ * OWNERS), 1)
-    owner = (row // CAP == col).astype(F32).astype(BF16)
-    lane = iota((count, 128), 1)
-    spread = mm(owner, (asked & 127).astype(F32).astype(BF16)) + 128.0 * mm(
-        owner, (asked >> 7).astype(F32).astype(BF16)
-    )
+    count = NZ * USED
+    parts = early_ref[:, EARLY:, :256].reshape(NZ * PROWS, 256)
+    k, col = iota((count, 128), 0), iota((count, 128), 1)
+    late = k < NZ * LATE
+    source = jnp.where(late, k // LATE, (k - NZ * LATE) // EARLY)
+    low, high = (
+        mm((col == source * PROWS + i).astype(F32).astype(BF16), parts) for i in range(2)
+    )
+    k = iota((count, 256), 0)
+    place = jnp.where(k < NZ * LATE, k % LATE, LATE + (k - NZ * LATE) % EARLY)
     column = jnp.sum(
-        jnp.where(iota((count, 128), 0) % CAP == lane, spread, 0.0), axis=1, keepdims=True
+        jnp.where(iota((count, 256), 1) == place, low + 128.0 * high, 0.0), axis=1, keepdims=True
     )
     names = jnp.zeros((128, 128), F32)
     for line in range(count // 128):
@@ -261,60 +280,80 @@
     out_ref[...] = names.T[:PROWS].astype(jnp.int32) - first
 
 
-def table_kernel(rows_ref, names_ref, after_ref, out_ref, buf, sems):
-    half = NZ * GROWS // 2
+def table_kernel(late_ref, early_ref, names_ref, after_ref, out_ref, buf, early, total, sems):
+    half = NZ * LATE // 2
     copies = [
         pltpu.make_async_copy(
-            rows_ref.at[pl.ds(part * half, half), :], buf.at[part], sems.at[part]
+            late_ref.at[pl.ds(part * half, half), :], buf.at[part], sems.at[part]
         )
         for part in range(2)
     ]
-    for copy in copies:
+    copies.append(
+        pltpu.make_async_copy(early_ref.at[:, pl.ds(0, EARLY), :], early, sems.at[2])
+    )
+    for copy in copies[::-1]:
         copy.start()
     place = iota((256, 128), 0)
-    lines = half // 128
-    for part in range(2):
-        pick = jnp.concatenate(
+
+    def picks(first, last):
+        return jnp.concatenate(
             [
                 (place == names_ref[line : line + 1, :]).astype(F32).astype(BF16)
-                for line in range(part * lines, (part + 1) * lines)
+                for line in range(first, last)
             ],
             axis=1,
         )
-        copies[part].wait()
-        total = mm(pick, buf[part])
-        if part == 0:
-            out_ref[...] = total
-        else:
-            out_ref[...] += total
-
-
-def square_kernel(sums_ref, out_ref):
+
+    lines = half // 128
+    late_picks = [picks(part * lines, (part + 1) * lines) for part in range(2)]
+    early_picks = picks(2 * lines, 2 * lines + NZ * EARLY // 128)
+    copies[2].wait()
+    total[...] = mm(early_picks, early[...].reshape(NZ * EARLY, D))
+    copies[0].wait()
+    total[...] += mm(late_picks[0], buf[0])
+    copies[1].wait()
+    outs = []
+    for n in range(4):
+        cols = slice(256 * n, 256 * n + 256)
+        total[:, cols] += mm(late_picks[1], buf[1, :, cols])
+        block = pl.ds(256 * n, 256)
+        outs.append(
+            pltpu.make_async_copy(total.at[:, block], out_ref.at[:, block], sems.at[3 + n])
+        )
+        outs[-1].start()
+    for copy in outs:
+        copy.wait()
+
+
+def square_kernel(mine_ref, other_ref, out_ref):
     total = jnp.zeros((PROWS, PCOLS), F32)
-    for i in range(OWNERS):
-        part = sums_ref[i].astype(F32)
-        total = total + part * part
+    for sums_ref in (mine_ref, other_ref):
+        for i in range(XY):
+            part = sums_ref[i].astype(F32)
+            total = total + part * part
     mix = jnp.sum(total[:, :512])
     out = jnp.sum(total[:, 512:])
     lane = iota((NZ, 8, 128), 2)
     out_ref[...] = jnp.where(lane == 0, mix, jnp.where(lane == 1, out, 0.0))
 
 
-def scale_kernel(sums_ref, squares_ref, mix_ref, out_ref):
+def scale_kernel(mine_ref, other_ref, squares_ref, mix_ref, out_ref):
     total = jnp.sum(squares_ref[...], axis=0)[0:1]
     mix_sq, out_sq = total[:, 0:1], total[:, 1:2]
     mix_scale = jnp.minimum(1.0, 1.0 / jnp.sqrt(mix_sq / float(D * 4 * AW) + 1e-06))
     out_scale = jnp.minimum(1.0, 1.0 / jnp.sqrt(out_sq / float(D * AW) + 1e-06))
-    for p in range(XY):
-        for core in range(2):
-            sums = sums_ref[p * 2 + core].astype(F32)
+    core = lax.axis_index("core")
+    for side, sums_ref in ((core, mine_ref), (1 - core, other_ref)):
+        for p in range(XY):
+            sums = sums_ref[p].astype(F32)
             mix, out = sums[:, :512] * mix_scale, sums[:, 512:] * out_scale
-            r, c = p * 8, core * D
-            mix_ref[r : r + 8, c : c + 512] = mix[:8]
-            mix_ref[r : r + 8, c + 512 : c + 1024] = mix[8:]
-            r, c = (p // 2) * 8, core * AW + (p % 2) * 256
-            out_ref[r : r + 8, c : c + 128] = out[:8]
-            out_ref[r : r + 8, c + 128 : c + 256] = out[8:]
+            for part in range(2):
+                r = p * 8
+                c = pl.multiple_of(side * D + part * 512, 512)
+                mix_ref[r : r + 8, pl.ds(c, 512)] = mix[8 * part : 8 * part + 8]
+                r = (p // 2) * 8
+                c = pl.multiple_of(side * AW + (p % 2) * 256 + part * 128, 128)
+                out_ref[r : r + 8, pl.ds(c, 128)] = out[8 * part : 8 * part + 8]
 
 
 def vmem():
@@ -355,12 +394,6 @@
         (item_owner.reshape(1, TOK), item_row.reshape(1, TOK)),
     )
     asked = exchange(requests, TABLE)
-    names = call(
-        names_kernel,
-        [((PROWS, 128), jnp.int32)],
-        (exchange(jnp.broadcast_to(asked[None], (NZ, OWNERS, 128)), "z"),),
-        cost_estimate=cost(1),
-    )
     wanted = asked[:, :SLOTS].reshape(OWNERS * SLOTS)
     found = item_table.at[wanted].get(mode="promise_in_bounds")
     got = exchange(found.reshape(OWNERS, SLOTS, D), TABLE)
@@ -382,9 +415,8 @@
             gain_in.reshape(1, D),
             gain_attn.reshape(1, AW),
             cotangent,
-            names,
         ),
-        specs=[smem, vmem(), vmem(), pinned, vmem(), vmem(), vmem(), anywhere],
+        specs=[smem, vmem(), vmem(), pinned, vmem(), vmem(), vmem()],
         scratch_shapes=[
             pltpu.VMEM((2, NZ, TOK, D), BF16),
             pltpu.VMEM((NZ, 2, 32, D), BF16),
@@ -411,23 +443,33 @@
     column = lax.psum_scatter(
         grads.reshape(NZ * XY * PROWS, PCOLS), "z", scatter_dimension=0, tiled=True
     )
+    received = exchange(grad_slots.reshape(OWNERS, SLOTS, D), TABLE)
+    late, early = call(
+        pack_kernel,
+        [((LATE, D), BF16), ((EARLY + PROWS, D), BF16)],
+        (received.reshape(OWNERS * SLOTS, D), asked),
+        cost_estimate=cost(2),
+        compiler_params=pltpu.CompilerParams(vmem_limit_bytes=16 * MB),
+    )
+    late = lax.all_gather(late, "z", axis=0, tiled=True)
+    early = exchange(jnp.broadcast_to(early[None], (NZ, EARLY + PROWS, D)), "z")
+    column, early = lax.optimization_barrier((column, early))
+    names = call(
+        names_kernel,
+        [((PROWS, 128), jnp.int32)],
+        (early,),
+        cost_estimate=cost(2),
+        compiler_params=pltpu.CompilerParams(vmem_limit_bytes=16 * MB),
+    )
     plane = exchange(column.reshape(XY, PROWS, PCOLS), ("x", "y"))
     whole = jnp.sum(plane.astype(F32), axis=0).astype(BF16)
-    sums = exchange(jnp.broadcast_to(whole[None], (OWNERS, PROWS, PCOLS)), TABLE)
-
-    received = exchange(grad_slots.reshape(OWNERS, SLOTS, D), TABLE)
-    packed = call(
-        pack_kernel,
-        [((GROWS, D), BF16)],
-        (received.reshape(OWNERS * SLOTS, D),),
-        cost_estimate=cost(2),
-        compiler_params=pltpu.CompilerParams(vmem_limit_bytes=16 * MB),
-    )
-    gathered = lax.all_gather(packed, "z", axis=0, tiled=True)
+    mine = exchange(jnp.broadcast_to(whole[None], (XY, PROWS, PCOLS)), ("x", "y"))
+    other = lax.ppermute(mine, "core", [(0, 1), (1, 0)])
+
     squares = call(
         square_kernel,
         [((NZ, 8, 128), F32)],
-        (sums,),
+        (mine, other),
         cost_estimate=cost(1),
         compiler_params=pltpu.CompilerParams(vmem_limit_bytes=16 * MB),
     )
@@ -435,18 +477,21 @@
     mix_grad, out_grad = call(
         scale_kernel,
         [((TOK, 4 * AW), F32), ((64, D), F32)],
-        (sums, squares),
+        (mine, other, squares),
         cost_estimate=cost(2),
         compiler_params=pltpu.CompilerParams(vmem_limit_bytes=16 * MB),
     )
     table_grad = call(
         table_kernel,
         [((256, D), F32)],
-        (gathered, names, out_grad),
-        specs=[pinned, vmem(), anywhere],
+        (late, early, names, out_grad),
+        specs=[pinned, pinned, vmem(), anywhere],
+        outs_specs=anywhere,
         scratch_shapes=[
-            pltpu.VMEM((2, NZ * GROWS // 2, D), BF16),
-            pltpu.SemaphoreType.DMA((2,)),
+            pltpu.VMEM((2, NZ * LATE // 2, D), BF16),
+            pltpu.VMEM((NZ, EARLY, D), BF16),
+            pltpu.VMEM((256, D), F32),
+            pltpu.SemaphoreType.DMA((7,)),
         ],
         cost_estimate=cost(3),
         compiler_params=pltpu.CompilerParams(vmem_limit_bytes=60 * MB),

time: 177 us -> 185 us (1.045)
  blocking collectives: 81.2 us -> 110 us
  waiting for transfers between devices: 35.8 us -> 21.2 us
  starting transfers between devices: 14.2 us -> 10.8 us
    all_to_all x5 -> x6, blocking collectives: 81.2 us -> 110 us  [exchange(): return lax.all_to_all(array, axes, split_axis=0, concat_axis=0, tiled=True)]
    reduce_scatter x1, waiting for transfers between devices: 18.8 us -> 0.56 us  [shards(): lax.psum_scatter(grads.reshape(NZ * XY * PROWS, PCOLS), 'z', scatter_dime...]
    all_gather x1, waiting for transfers between devices: 0.01 us -> 11.8 us  [shards(): lax.all_gather(share, ('core', 'z'), axis=0, tiled=True)]
    all_to_all x2 -> x1, starting transfers between devices: 14 us -> 5.32 us  [exchange(): return lax.all_to_all(array, axes, split_axis=0, concat_axis=0, tiled=True)]
    all_to_all x2 -> x1, waiting for transfers between devices: 13.8 us -> 5.51 us  [exchange(): return lax.all_to_all(array, axes, split_axis=0, concat_axis=0, tiled=True)]
    ppermute x0 -> x1, starting transfers between devices: none -> 5 us  [shards(): other = lax.ppermute(mine, 'core', [(0, 1), (1, 0)])]
  transfers between devices with their start and end apart: 6 -> 6, of which waited for: 5 -> 5; matrix products, arithmetic and copies ran while one was open for 3% -> 2% of each run, Pallas kernels for 4% -> 3%
where the time goes in v7:
time: 185 us
  blocking collectives  110 us (59%)
  waiting for transfers between devices  21.2 us (11%)
  Pallas kernels  21.1 us (11%)
  between operations  13.9 us (8%)
  starting transfers between devices  10.8 us (6%)
  local copies, waits for them, and re-layouts  7.59 us (4%)
    all_to_all x6, blocking collectives, exchange(): return lax.all_to_all(array, axes, split_axis=0, concat_axis=0, tiled=True)  110 us
    pallas_call x8, Pallas kernels, call(): pl.pallas_call(body, out_shape=shapes[0] if one else shapes, in_specs=spe...  19.1 us
    all_gather x1, waiting for transfers between devices, shards(): lax.all_gather(share, ('core', 'z'), axis=0, tiled=True)  11.8 us
    all_to_all x1, waiting for transfers between devices, exchange(): return lax.all_to_all(array, axes, split_axis=0, concat_axis=0, tiled=True)  5.51 us
    all_to_all x1, starting transfers between devices, exchange(): return lax.all_to_all(array, axes, split_axis=0, concat_axis=0, tiled=True)  5.32 us
    ppermute x1, starting transfers between devices, shards(): other = lax.ppermute(mine, 'core', [(0, 1), (1, 0)])  5 us
    gather x1, local copies, waits for them, and re-layouts, shards(): found = item_table.at[wanted].get(mode='promise_in_bounds')  4.29 us
  transfers between devices with their start and end apart: 6, of which 5 were waited for; matrix products, arithmetic and copies ran while one was open for 2% of the time, Pallas kernels for 3%

profile of v7, /device:TPU:1, one launch (start us, length us, event | category | flops | bytes accessed | tf_op | source)
XLA Modules:
  0.0 184.7 jit_solution(1276974811147576443)
XLA Ops:
  7.3 1.8 shard_map.121
  9.2 1.7 shard_map.120
  10.9 15.6 %all_to_all.41 = s32[32,1,128]{2,1,0:T(1,128)S(1)} all-to-all(s32[32,1,128]{2,1,0:T(1,128)} %bitcast.27), channel_id=1, replica_groups=mesh['x'=4,'y'=4,'core'=2,'z'=8] {'x','y','core'}, dimensions={0} | all-to-all | bytes 32768 | tf_op jit(solution)/shard_map/all_to_all | solution.py:380
  26.6 4.3 %gather_fusion = bf16[256,1024]{1,0:T(8,128)(2,1)S(1)} fusion(bf16[2048,1024]{1,0:T(8,128)(2,1)} %param.9, s32[1024]{0:T(1024)S(1)} %pad_clamp_fusion), kind=kCustom, calls=%fused_computation | custom fusion | bytes 1049600 | tf_op jit(solution)/shard_map/gather | solution.py:398
  30.9 15.3 %all_to_all.42 = bf16[32,8,1024]{2,1,0:T(8,128)(2,1)S(1)} all-to-all(bf16[32,8,1024]{2,1,0:T(8,128)(2,1)S(1)} %bitcast.25), channel_id=1, replica_groups=mesh['x'=4,'y'=4,'core'=2,'z'=8] {'x','y','core'}, dimensions={0} | all-to-all | bytes 1048576 | tf_op jit(solution)/shard_map/all_to_all | solution.py:380
  46.2 11.8 %all-gather.3.cloned.1.call-done = bf16[2560,1024]{1,0:T(8,128)(2,1)} async-done(((bf16[160,1024]{1,0:T(8,128)(2,1)}), bf16[2560,1024]{1,0:T(8,128)(2,1)}) %all-gather.3.cloned.1.call-update) | async-done | bytes 5242896 | tf_op jit(solution)/shard_map/all_gather | solution.py:389
  58.1 2.5 %copy-done.1 = bf16[2560,1024]{1,0:T(8,128)(2,1)S(1)} copy-done((bf16[2560,1024]{1,0:T(8,128)(2,1)S(1)}, bf16[2560,1024]{1,0:T(8,128)(2,1)}, u32[]{:S(2)}) %copy-start.1) | copy-done | bytes 5242904
  60.5 7.2 %shard_map.122 = (bf16[128,1024]{1,0:T(8,128)(2,1)}, bf16[256,1024]{1,0:T(8,128)(2,1)S(1)}, bf16[128,3072]{1,0:T(8,128)(2,1)S(1)}, bf16[128,3072]{1,0:T(8,128)(2,1)S(1)}) custom-call(s32[1,8]{1,0:T(1,128)S(1)} %copy-done.7, bf16[256,1024]{1,0:T(8,128)(2,1)S(1)} %bitcast.18, s32[128,128]{1,0:T(8,128)S(1)} %copy-done.3, ...), custom_call_target="tpu_custom_call" | custom-call | bytes 27000000 | tf_op jit(solution)/shard_map/pallas_call | solution.py:366
  68.1 2.0 %collective-permute-done.theirs_ref = bf16[128,3072]{1,0:T(8,128)(2,1)S(1)} collective-permute-done((bf16[128,3072]{1,0:T(8,128)(2,1)S(1)}, bf16[128,3072]{1,0:T(8,128)(2,1)S(1)}, u32[]{:S(2)}, u32[]{:S(2)}) %collective-permute-start) | collective-permute-done | bytes 786464 | tf_op jit(solution)/shard_map/ppermute | solution.py:430
  70.1 2.0 %shard_map.124 = bf16[8,16,16,640]{3,2,1,0:T(8,128)(2,1)} custom-call(bf16[128,3072]{1,0:T(8,128)(2,1)S(1)} %get-tuple-element.21.keep_ref, bf16[128,3072]{1,0:T(8,128)(2,1)S(1)} %collective-permute-done.theirs_ref), custom_call_target="tpu_custom_call" | custom-call | bytes 9000000 | tf_op jit(solution)/shard_map/pallas_call | solution.py:431
  72.2 18.5 %all_to_all.43 = bf16[32,8,1024]{2,1,0:T(8,128)(2,1)S(1)} all-to-all(bf16[32,8,1024]{2,1,0:T(8,128)(2,1)S(1)} %bitcast.20), channel_id=1, replica_groups=mesh['x'=4,'y'=4,'core'=2,'z'=8] {'x','y','core'}, dimensions={0} | all-to-all | bytes 1048576 | tf_op jit(solution)/shard_map/all_to_all | solution.py:380
  90.7 1.0 shard_map.123
  91.8 34.9 %all_to_all.44.early_ref = bf16[8,48,1024]{2,1,0:T(8,128)(2,1)S(1)} all-to-all(bf16[8,48,1024]{2,1,0:T(8,128)(2,1)S(1)} %broadcast_in_dim.4), channel_id=1, replica_groups=mesh['x'=4,'y'=4,'core'=2,'z'=8] {'z'}, dimensions={0} | all-to-all | bytes 1572864 | tf_op jit(solution)/shard_map/all_to_all | solution.py:380
  127.2 14.6 %all_to_all.45 = bf16[16,16,640]{2,1,0:T(8,128)(2,1)S(1)} all-to-all(bf16[16,16,640]{2,1,0:T(8,128)(2,1)} %bitcast.26), channel_id=1, replica_groups=mesh['x'=4,'y'=4,'core'=2,'z'=8] {'x','y'}, dimensions={0} | all-to-all | bytes 655360 | tf_op jit(solution)/shard_map/all_to_all | solution.py:380
  141.9 11.1 %all_to_all.46.mine_ref = bf16[16,16,640]{2,1,0:T(8,128)(2,1)S(1)} all-to-all(bf16[16,16,640]{2,1,0:T(8,128)(2,1)S(1)} %broadcast_in_dim.5), channel_id=1, replica_groups=mesh['x'=4,'y'=4,'core'=2,'z'=8] {'x','y'}, dimensions={0} | all-to-all | bytes 655360 | tf_op jit(solution)/shard_map/all_to_all | solution.py:380
  153.1 5.0 %collective-permute-start.1 = (bf16[16,16,640]{2,1,0:T(8,128)(2,1)S(1)}, bf16[16,16,640]{2,1,0:T(8,128)(2,1)S(1)}, u32[]{:S(2)}, u32[]{:S(2)}) collective-permute-start(bf16[16,16,640]{2,1,0:T(8,128)(2,1)S(1)} %all_to_all.46.mine_ref), channel_id=1, source_target_pairs={{0,8},{8,0},{1,9},{9,1},{2,10},{10,2},{3,11},{11,3},{4,12},{12,4},... | collective-permute-start | bytes 983048 | tf_op jit(solution)/shard_map/ppermute | solution.py:467
  158.1 1.3 collective-permute-done.1.other_ref
  159.3 0.8 shard_map.126
  160.1 5.3 %all-to-all-start.6 = ((f32[8,8,128]{2,1,0:T(8,128)}), f32[8,8,128]{2,1,0:T(8,128)S(1)}, u32[]{:S(2)}, u32[]{:S(2)}) async-start(f32[8,8,128]{2,1,0:T(8,128)} %shard_map.126), calls=%async_computation.7 | async-start | bytes 65536 | tf_op jit(solution)/shard_map/all_to_all | solution.py:380
  165.4 0.8 shard_map.125.names_ref
  166.3 0.6 copy-done.4
  166.9 5.5 %all-to-all-done.6.squares_ref = f32[8,8,128]{2,1,0:T(8,128)S(1)} async-done(((f32[8,8,128]{2,1,0:T(8,128)}), f32[8,8,128]{2,1,0:T(8,128)S(1)}, u32[]{:S(2)}, u32[]{:S(2)}) %all-to-all-start.6) | async-done | bytes 32800 | tf_op jit(solution)/shard_map/all_to_all | solution.py:380
  172.4 1.2 shard_map.127
  173.6 4.6 %shard_map.128 = f32[256,1024]{1,0:T(8,128)} custom-call(bf16[1280,1024]{1,0:T(8,128)(2,1)} %all-gather.5.cloned.1.call-done.late_ref, bf16[8,48,1024]{2,1,0:T(8,128)(2,1)} %copy-done, s32[16,128]{1,0:T(8,128)} %copy-done.4, f32[64,1024]{1,0:T(8,128)} %get-tuple-element.15.after_ref), custom_call_target="tpu_custom_call" | custom-call | bytes 9000000 | tf_op jit(solution)/shard_map/pallas_call | solution.py:366
  (29 shorter events, 1.4 us)
Async XLA Ops:
  7.2 50.9 %copy-start.2 = (bf16[128,1024]{1,0:T(8,128)(2,1)S(1)}, bf16[128,1024]{1,0:T(8,128)(2,1)}, u32[]{:S(2)}) copy-start(bf16[128,1024]{1,0:T(8,128)(2,1)} %ct_ref.1) | copy-start | bytes 786436
  7.2 50.9 %copy-start.6 = (f32[512]{0:T(512)S(1)}, f32[512]{0:T(512)}, u32[]{:S(2)}) copy-start(f32[512]{0:T(512)} %param.16) | copy-start | bytes 6148
  7.2 50.9 %copy-start.5 = (f32[1024]{0:T(1024)S(1)}, f32[1024]{0:T(1024)}, u32[]{:S(2)}) copy-start(f32[1024]{0:T(1024)} %param.15) | copy-start | bytes 12292
  7.2 50.8 %copy-start.7 = (s32[1,8]{1,0:T(1,128)S(1)}, s32[1,8]{1,0:T(1,128)}, u32[]{:S(2)}) copy-start(s32[1,8]{1,0:T(1,128)} %lens_ref.1) | copy-start | bytes 100
  7.2 50.8 %all-gather.3.cloned.1.call-start = ((), (), s32[]{:S(2)}) async-start(), calls=%async_computation.8 | async-start | bytes 5570560 | tf_op jit(solution)/shard_map/all_gather | solution.py:389
  9.1 118.1 %reduce-scatter.2.cloned.1.call-start = ((), (), s32[]{:S(2)}) async-start(), calls=%async_computation.10 | async-start | bytes 2949120 | tf_op jit(solution)/shard_map/reduce_scatter | solution.py:443
  10.9 47.1 %copy-start.3 = (s32[128,128]{1,0:T(8,128)S(1)}, s32[128,128]{1,0:T(8,128)}, u32[]{:S(2)}) copy-start(s32[128,128]{1,0:T(8,128)} %get-tuple-element.17.tgt_ref) | copy-start | bytes 196612
  58.1 2.5 %copy-start.1 = (bf16[2560,1024]{1,0:T(8,128)(2,1)S(1)}, bf16[2560,1024]{1,0:T(8,128)(2,1)}, u32[]{:S(2)}) copy-start(bf16[2560,1024]{1,0:T(8,128)(2,1)} %all-gather.3.cloned.1.call-done) | copy-start | bytes 15728644
  67.7 2.4 %collective-permute-start = (bf16[128,3072]{1,0:T(8,128)(2,1)S(1)}, bf16[128,3072]{1,0:T(8,128)(2,1)S(1)}, u32[]{:S(2)}, u32[]{:S(2)}) collective-permute-start(bf16[128,3072]{1,0:T(8,128)(2,1)S(1)} %get-tuple-element.22), channel_id=1, source_target_pairs={{0,8},{8,0},{1,9},{9,1},{2,10},{10,2},{3,11},{11,3},{4,12},{12,4},... | collective-permute-start | bytes 2359304 | tf_op jit(solution)/shard_map/ppermute | solution.py:430
  72.1 101.4 %all-gather.5.cloned.1.call-start = ((), (), s32[]{:S(2)}) async-start(), calls=%async_computation.9 | async-start | bytes 2949120 | tf_op jit(solution)/shard_map/all_gather | solution.py:454
  126.7 46.9 %copy-start = (bf16[8,48,1024]{2,1,0:T(8,128)(2,1)}, bf16[8,48,1024]{2,1,0:T(8,128)(2,1)S(1)}, u32[]{:S(2)}) copy-start(bf16[8,48,1024]{2,1,0:T(8,128)(2,1)S(1)} %all_to_all.44.early_ref) | copy-start | bytes 2359300
  153.1 6.3 %collective-permute-start.1 = (bf16[16,16,640]{2,1,0:T(8,128)(2,1)S(1)}, bf16[16,16,640]{2,1,0:T(8,128)(2,1)S(1)}, u32[]{:S(2)}, u32[]{:S(2)}) collective-permute-start(bf16[16,16,640]{2,1,0:T(8,128)(2,1)S(1)} %all_to_all.46.mine_ref), channel_id=1, source_target_pairs={{0,8},{8,0},{1,9},{9,1},{2,10},{10,2},{3,11},{11,3},{4,12},{12,4},... | collective-permute-start | bytes 983048 | tf_op jit(solution)/shard_map/ppermute | solution.py:467
  160.1 12.3 %all-to-all-start.6 = ((f32[8,8,128]{2,1,0:T(8,128)}), f32[8,8,128]{2,1,0:T(8,128)S(1)}, u32[]{:S(2)}, u32[]{:S(2)}) async-start(f32[8,8,128]{2,1,0:T(8,128)} %shard_map.126), calls=%async_computation.7 | async-start | bytes 65536 | tf_op jit(solution)/shard_map/all_to_all | solution.py:380
  166.3 0.6 copy-start.4
Sparse Core Ops, SparseCore 0:
  10.4 47.5 all-gather.2
  72.3 54.9 reduce-scatter.1
  129.6 42.0 all-gather.4

commit v8 on v7

--- a/solution.py
+++ b/solution.py
@@ -21,8 +21,6 @@
 PCOLS = 640
 FACT = 3072
 USED = OWNERS * CAP
-LATE = 160
-EARLY = USED - LATE
 TABLE = ("x", "y", "core")
 ALL = ("x", "y", "core", "z")
 F32 = jnp.float32
@@ -208,18 +206,9 @@
         dst[:, 2560:FACT] = ct_ref[:, pl.ds(pl.multiple_of(side * AW, AW), AW)]
 
 
-def grads_kernel(keep_ref, theirs_ref, out_ref, buf, sems):
+def grads_kernel(keep_ref, theirs_ref, mix_ref, out_ref, mix, out, sems):
     def both(first, last):
         return jnp.concatenate([keep_ref[:, first:last], theirs_ref[:, first:last]], axis=0)
-
-    grad = mm_tn(both(2048, 2560), both(2560, FACT))
-    for z in range(NZ):
-        for p in range(XY):
-            r, c = z * 64 + (p // 2) * 8, (p % 2) * 256
-            part = grad[r : r + 8, c : c + 256]
-            buf[z, p, :, 512:PCOLS] = jnp.concatenate(
-                [part[:, :128], part[:, 128:]], axis=0
-            ).astype(BF16)
 
     copies = []
     d_mix = both(1024, 2048)
@@ -227,50 +216,51 @@
         grad = mm_tn(both(z * TOK, (z + 1) * TOK), d_mix)
         for p in range(XY):
             part = grad[8 * p : 8 * p + 8]
-            buf[z, p, :, 0:512] = jnp.concatenate(
-                [part[:, :512], part[:, 512:]], axis=0
+            mix[z, p] = jnp.concatenate([part[:, :512], part[:, 512:]], axis=0).astype(BF16)
+        copies.append(pltpu.make_async_copy(mix.at[z], mix_ref.at[z], sems.at[z]))
+        copies[-1].start()
+
+    grad = mm_tn(both(2048, 2560), both(2560, FACT))
+    for z in range(NZ):
+        for p in range(XY):
+            r, c = z * 64 + (p // 2) * 8, (p % 2) * 256
+            part = grad[r : r + 8, c : c + 256]
+            out[p, z * PROWS : (z + 1) * PROWS] = jnp.concatenate(
+                [part[:, :128], part[:, 128:]], axis=0
             ).astype(BF16)
-        copies.append(pltpu.make_async_copy(buf.at[z], out_ref.at[z], sems.at[z]))
-        copies[-1].start()
+    copies.append(pltpu.make_async_copy(out, out_ref, sems.at[NZ]))
+    copies[-1].start()
     for copy in copies:
         copy.wait()
 
 
-def pack_kernel(rows_ref, asked_ref, late_ref, early_ref):
+def column_kernel(plane_ref, asked_ref, out_ref):
+    total = jnp.sum(plane_ref[...].astype(F32), axis=0).astype(BF16)
+    asked = asked_ref[...]
+    low, high = ((part).astype(F32).astype(BF16) for part in (asked & 127, asked >> 7))
+    for z in range(NZ):
+        out_ref[z, :PROWS] = total[z * PROWS : (z + 1) * PROWS]
+        out_ref[z, PROWS : PROWS + OWNERS] = low
+        out_ref[z, PROWS + OWNERS :] = high
+
+
+def pack_kernel(rows_ref, out_ref):
     r, k = iota((USED, OWNERS * SLOTS), 0), iota((USED, OWNERS * SLOTS), 1)
-    take = ((r // CAP) * SLOTS + r % CAP == k).astype(F32).astype(BF16)
-    rows = mm(take, rows_ref[...]).astype(BF16)
-    late_ref[...] = rows[:LATE]
-    early_ref[:EARLY] = rows[LATE:]
-    asked = asked_ref[...]
-    owner = (iota((256, OWNERS), 0) // CAP == iota((256, OWNERS), 1)).astype(F32).astype(BF16)
-    slot = iota((256, 128), 0) % CAP == iota((256, 128), 1)
-    parts = []
-    for part in (asked & 127, asked >> 7):
-        spread = mm(owner, part.astype(F32).astype(BF16))
-        column = jnp.sum(jnp.where(slot, spread, 0.0), axis=1, keepdims=True)
-        parts.append(jnp.broadcast_to(column, (256, 128)).T[:PROWS])
-    which = iota((PROWS, 256), 0)
-    numbers = jnp.where(which == 0, parts[0], jnp.where(which == 1, parts[1], 0.0))
-    early_ref[EARLY:] = jnp.concatenate(
-        [numbers.astype(BF16), jnp.zeros((PROWS, D - 256), BF16)], axis=1
-    )
-
-
-def names_kernel(early_ref, out_ref):
+    take = (r // CAP) * SLOTS + r % CAP == k
+    out_ref[...] = mm(take.astype(F32).astype(BF16), rows_ref[...]).astype(BF16)
+
+
+def names_kernel(column_ref, out_ref):
     first = lax.axis_index("z") * 256
     count = NZ * USED
-    parts = early_ref[:, EARLY:, :256].reshape(NZ * PROWS, 256)
-    k, col = iota((count, 128), 0), iota((count, 128), 1)
-    late = k < NZ * LATE
-    source = jnp.where(late, k // LATE, (k - NZ * LATE) // EARLY)
-    low, high = (
-        mm((col == source * PROWS + i).astype(F32).astype(BF16), parts) for i in range(2)
-    )
-    k = iota((count, 256), 0)
-    place = jnp.where(k < NZ * LATE, k % LATE, LATE + (k - NZ * LATE) % EARLY)
+    low = column_ref[:, PROWS : PROWS + OWNERS].reshape(NZ * OWNERS, 128)
+    high = column_ref[:, PROWS + OWNERS :].reshape(NZ * OWNERS, 128)
+    row, col = iota((count, NZ * OWNERS), 0), iota((count, NZ * OWNERS), 1)
+    owner = (row // CAP == col).astype(F32).astype(BF16)
+    lane = iota((count, 128), 1)
+    spread = mm(owner, low) + 128.0 * mm(owner, high)
     column = jnp.sum(
-        jnp.where(iota((count, 256), 1) == place, low + 128.0 * high, 0.0), axis=1, keepdims=True
+        jnp.where(iota((count, 128), 0) % CAP == lane, spread, 0.0), axis=1, keepdims=True
     )
     names = jnp.zeros((128, 128), F32)
     for line in range(count // 128):
@@ -280,45 +270,38 @@
     out_ref[...] = names.T[:PROWS].astype(jnp.int32) - first
 
 
-def table_kernel(late_ref, early_ref, names_ref, after_ref, out_ref, buf, early, total, sems):
-    half = NZ * LATE // 2
+def table_kernel(rows_ref, names_ref, after_ref, out_ref, buf, total, sems):
+    half = NZ * USED // 2
     copies = [
         pltpu.make_async_copy(
-            late_ref.at[pl.ds(part * half, half), :], buf.at[part], sems.at[part]
+            rows_ref.at[pl.ds(part * half, half), :], buf.at[part], sems.at[part]
         )
         for part in range(2)
     ]
-    copies.append(
-        pltpu.make_async_copy(early_ref.at[:, pl.ds(0, EARLY), :], early, sems.at[2])
-    )
-    for copy in copies[::-1]:
+    for copy in copies:
         copy.start()
     place = iota((256, 128), 0)
-
-    def picks(first, last):
-        return jnp.concatenate(
+    lines = half // 128
+    picks = [
+        jnp.concatenate(
             [
                 (place == names_ref[line : line + 1, :]).astype(F32).astype(BF16)
-                for line in range(first, last)
+                for line in range(part * lines, (part + 1) * lines)
             ],
             axis=1,
         )
-
-    lines = half // 128
-    late_picks = [picks(part * lines, (part + 1) * lines) for part in range(2)]
-    early_picks = picks(2 * lines, 2 * lines + NZ * EARLY // 128)
-    copies[2].wait()
-    total[...] = mm(early_picks, early[...].reshape(NZ * EARLY, D))
+        for part in range(2)
+    ]
     copies[0].wait()
-    total[...] += mm(late_picks[0], buf[0])
+    total[...] = mm(picks[0], buf[0])
     copies[1].wait()
     outs = []
     for n in range(4):
         cols = slice(256 * n, 256 * n + 256)
-        total[:, cols] += mm(late_picks[1], buf[1, :, cols])
+        total[:, cols] += mm(picks[1], buf[1, :, cols])
         block = pl.ds(256 * n, 256)
         outs.append(
-            pltpu.make_async_copy(total.at[:, block], out_ref.at[:, block], sems.at[3 + n])
+            pltpu.make_async_copy(total.at[:, block], out_ref.at[:, block], sems.at[2 + n])
         )
         outs[-1].start()
     for copy in outs:
@@ -428,41 +411,58 @@
     )
 
     theirs = lax.ppermute(send, "core", [(0, 1), (1, 0)])
-    grads = pl.pallas_call(
+    mix_part, out_part = call(
         grads_kernel,
-        out_shape=jax.ShapeDtypeStruct((NZ, XY, PROWS, PCOLS), BF16),
-        in_specs=[vmem(), vmem()],
-        out_specs=anywhere,
+        [((NZ, XY, PROWS, 512), BF16), ((XY, NZ * PROWS, 128), BF16)],
+        (keep, theirs),
+        outs_specs=[anywhere, anywhere],
         scratch_shapes=[
-            pltpu.VMEM((NZ, XY, PROWS, PCOLS), BF16),
-            pltpu.SemaphoreType.DMA((NZ,)),
+            pltpu.VMEM((NZ, XY, PROWS, 512), BF16),
+            pltpu.VMEM((XY, NZ * PROWS, 128), BF16),
+            pltpu.SemaphoreType.DMA((NZ + 1,)),
         ],
         cost_estimate=cost(3),
         compiler_params=pltpu.CompilerParams(vmem_limit_bytes=30 * MB),
-    )(keep, theirs)
-    column = lax.psum_scatter(
-        grads.reshape(NZ * XY * PROWS, PCOLS), "z", scatter_dimension=0, tiled=True
-    )
+    )
+    mix_column = lax.psum_scatter(
+        mix_part.reshape(NZ * XY * PROWS, 512), "z", scatter_dimension=0, tiled=True
+    )
+
     received = exchange(grad_slots.reshape(OWNERS, SLOTS, D), TABLE)
-    late, early = call(
+    packed = call(
         pack_kernel,
-        [((LATE, D), BF16), ((EARLY + PROWS, D), BF16)],
-        (received.reshape(OWNERS * SLOTS, D), asked),
+        [((USED, D), BF16)],
+        (received.reshape(OWNERS * SLOTS, D),),
         cost_estimate=cost(2),
         compiler_params=pltpu.CompilerParams(vmem_limit_bytes=16 * MB),
     )
-    late = lax.all_gather(late, "z", axis=0, tiled=True)
-    early = exchange(jnp.broadcast_to(early[None], (NZ, EARLY + PROWS, D)), "z")
-    column, early = lax.optimization_barrier((column, early))
+    out_part, packed = lax.optimization_barrier((out_part, packed))
+    gathered = lax.all_gather(packed, "z", axis=0, tiled=True)
+
+    out_column = call(
+        column_kernel,
+        [((NZ, PROWS + 2 * OWNERS, 128), BF16)],
+        (exchange(out_part, ("x", "y")), asked),
+        cost_estimate=cost(1),
+        compiler_params=pltpu.CompilerParams(vmem_limit_bytes=16 * MB),
+    )
+    out_column = exchange(out_column, "z")
+    mix_column, out_column = lax.optimization_barrier((mix_column, out_column))
     names = call(
         names_kernel,
         [((PROWS, 128), jnp.int32)],
-        (early,),
+        (out_column,),
         cost_estimate=cost(2),
         compiler_params=pltpu.CompilerParams(vmem_limit_bytes=16 * MB),
     )
-    plane = exchange(column.reshape(XY, PROWS, PCOLS), ("x", "y"))
-    whole = jnp.sum(plane.astype(F32), axis=0).astype(BF16)
+    mix_plane = exchange(mix_column.reshape(XY, PROWS, 512), ("x", "y"))
+    whole = jnp.concatenate(
+        [
+            jnp.sum(mix_plane.astype(F32), axis=0),
+            jnp.sum(out_column[:, :PROWS].astype(F32), axis=0),
+        ],
+        axis=1,
+    ).astype(BF16)
     mine = exchange(jnp.broadcast_to(whole[None], (XY, PROWS, PCOLS)), ("x", "y"))
     other = lax.ppermute(mine, "core", [(0, 1), (1, 0)])
 
@@ -484,14 +484,13 @@
     table_grad = call(
         table_kernel,
         [((256, D), F32)],
-        (late, early, names, out_grad),
-        specs=[pinned, pinned, vmem(), anywhere],
+        (gathered, names, out_grad),
+        specs=[pinned, vmem(), anywhere],
         outs_specs=anywhere,
         scratch_shapes=[
-            pltpu.VMEM((2, NZ * LATE // 2, D), BF16),
-            pltpu.VMEM((NZ, EARLY, D), BF16),
+            pltpu.VMEM((2, NZ * USED // 2, D), BF16),
             pltpu.VMEM((256, D), F32),
-            pltpu.SemaphoreType.DMA((7,)),
+            pltpu.SemaphoreType.DMA((6,)),
         ],
         cost_estimate=cost(3),
         compiler_params=pltpu.CompilerParams(vmem_limit_bytes=60 * MB),

time: 185 us -> 173 us (0.935)
  blocking collectives: 110 us -> 86 us
  waiting for transfers between devices: 21.2 us -> 31.2 us
  starting transfers between devices: 10.8 us -> 13.1 us
    all_to_all x6, blocking collectives: 110 us -> 86 us  [exchange(): return lax.all_to_all(array, axes, split_axis=0, concat_axis=0, tiled=True)]
    all_to_all x1 -> x2, waiting for transfers between devices: 5.51 us -> 13.1 us  [exchange(): return lax.all_to_all(array, axes, split_axis=0, concat_axis=0, tiled=True)]
    all_gather x1, waiting for transfers between devices: 0.01 us -> 2.96 us  [shards(): gathered = lax.all_gather(packed, 'z', axis=0, tiled=True)]
    all_to_all x1 -> x2, starting transfers between devices: 5.32 us -> 8.1 us  [exchange(): return lax.all_to_all(array, axes, split_axis=0, concat_axis=0, tiled=True)]
    pallas_call x1 -> x0, Pallas kernels: 2 us -> none  [shards(): pl.pallas_call(grads_kernel, out_shape=jax.ShapeDtypeStruct((NZ, XY, PROW...]
    pallas_call x8 -> x10, Pallas kernels: 19.1 us -> 20.4 us  [call(): pl.pallas_call(body, out_shape=shapes[0] if one else shapes, in_specs=spe...]
  transfers between devices with their start and end apart: 6 -> 7, of which waited for: 5 -> 6; matrix products, arithmetic and copies ran while one was open for 2% -> 3% of each run, Pallas kernels for 3% -> 3%
where the time goes in v8:
time: 173 us; the launch traced here: 172 us
  blocking collectives  86 us (50%)
  waiting for transfers between devices  31.2 us (18%)
  Pallas kernels  20.4 us (12%)
  between operations  13.9 us (8%)
  starting transfers between devices  13.1 us (8%)
  local copies, waits for them, and re-layouts  7.5 us (4%)
    all_to_all x6, blocking collectives, exchange(): return lax.all_to_all(array, axes, split_axis=0, concat_axis=0, tiled=True)  86 us
    pallas_call x10, Pallas kernels, call(): pl.pallas_call(body, out_shape=shapes[0] if one else shapes, in_specs=spe...  20.4 us
    all_to_all x2, waiting for transfers between devices, exchange(): return lax.all_to_all(array, axes, split_axis=0, concat_axis=0, tiled=True)  13.1 us
    all_gather x1, waiting for transfers between devices, shards(): lax.all_gather(share, ('core', 'z'), axis=0, tiled=True)  11.8 us
    all_to_all x2, starting transfers between devices, exchange(): return lax.all_to_all(array, axes, split_axis=0, concat_axis=0, tiled=True)  8.1 us
    ppermute x1, starting transfers between devices, shards(): other = lax.ppermute(mine, 'core', [(0, 1), (1, 0)])  4.55 us
    gather x1, local copies, waits for them, and re-layouts, shards(): found = item_table.at[wanted].get(mode='promise_in_bounds')  4.29 us
  transfers between devices with their start and end apart: 7, of which 6 were waited for; matrix products, arithmetic and copies ran while one was open for 3% of the time, Pallas kernels for 3%

profile of v8, /device:TPU:1, one launch (start us, length us, event | category | flops | bytes accessed | tf_op | source)
XLA Modules:
  0.0 172.2 jit_solution(10632995566740990015)
XLA Ops:
  7.3 1.8 %shard_map.121 = bf16[160,1024]{1,0:T(8,128)(2,1)} custom-call(bf16[128,2048]{1,0:T(8,128)(2,1)} %mix_ref.1, bf16[64,1024]{1,0:T(8,128)(2,1)} %out_ref.1), custom_call_target="tpu_custom_call" | custom-call | tf_op jit(solution)/shard_map/pallas_call | solution.py:349
  9.2 1.7 %shard_map.120 = (s32[32,128]{1,0:T(8,128)}, s32[128,128]{1,0:T(8,128)}) custom-call(s32[1,128]{1,0:T(1,128)} %bitcast.29, s32[1,128]{1,0:T(1,128)} %bitcast.30), custom_call_target="tpu_custom_call" | custom-call | tf_op jit(solution)/shard_map/pallas_call | solution.py:349
  10.9 15.6 %all_to_all.46 = s32[32,1,128]{2,1,0:T(1,128)S(1)} all-to-all(s32[32,1,128]{2,1,0:T(1,128)} %bitcast.27), channel_id=1, replica_groups=mesh['x'=4,'y'=4,'core'=2,'z'=8] {'x','y','core'}, dimensions={0} | all-to-all | bytes 32768 | tf_op jit(solution)/shard_map/all_to_all | solution.py:363
  26.6 4.3 %gather_fusion = bf16[256,1024]{1,0:T(8,128)(2,1)S(1)} fusion(bf16[2048,1024]{1,0:T(8,128)(2,1)} %param.9, s32[1024]{0:T(1024)S(1)} %pad_clamp_fusion), kind=kCustom, calls=%fused_computation | custom fusion | bytes 1049600 | tf_op jit(solution)/shard_map/gather | solution.py:381
  30.9 15.3 %all_to_all.47 = bf16[32,8,1024]{2,1,0:T(8,128)(2,1)S(1)} all-to-all(bf16[32,8,1024]{2,1,0:T(8,128)(2,1)S(1)} %bitcast.25), channel_id=1, replica_groups=mesh['x'=4,'y'=4,'core'=2,'z'=8] {'x','y','core'}, dimensions={0} | all-to-all | bytes 1048576 | tf_op jit(solution)/shard_map/all_to_all | solution.py:363
  46.2 11.8 %all-gather.3.cloned.1.call-done = bf16[2560,1024]{1,0:T(8,128)(2,1)} async-done(((bf16[160,1024]{1,0:T(8,128)(2,1)}), bf16[2560,1024]{1,0:T(8,128)(2,1)}) %all-gather.3.cloned.1.call-update) | async-done | bytes 5242896 | tf_op jit(solution)/shard_map/all_gather | solution.py:372
  58.1 2.5 %copy-done = bf16[2560,1024]{1,0:T(8,128)(2,1)S(1)} copy-done((bf16[2560,1024]{1,0:T(8,128)(2,1)S(1)}, bf16[2560,1024]{1,0:T(8,128)(2,1)}, u32[]{:S(2)}) %copy-start) | copy-done | bytes 5242904
  60.5 7.2 %shard_map.122 = (bf16[128,1024]{1,0:T(8,128)(2,1)}, bf16[256,1024]{1,0:T(8,128)(2,1)S(1)}, bf16[128,3072]{1,0:T(8,128)(2,1)S(1)}, bf16[128,3072]{1,0:T(8,128)(2,1)S(1)}) custom-call(s32[1,8]{1,0:T(1,128)S(1)} %copy-done.6, bf16[256,1024]{1,0:T(8,128)(2,1)S(1)} %bitcast.18, s32[128,128]{1,0:T(8,128)S(1)} %copy-done.2, ...), custom_call_target="tpu_custom_call" | custom-call | bytes 27000000 | tf_op jit(solution)/shard_map/pallas_call | solution.py:349
  68.1 2.0 %collective-permute-done.theirs_ref = bf16[128,3072]{1,0:T(8,128)(2,1)S(1)} collective-permute-done((bf16[128,3072]{1,0:T(8,128)(2,1)S(1)}, bf16[128,3072]{1,0:T(8,128)(2,1)S(1)}, u32[]{:S(2)}, u32[]{:S(2)}) %collective-permute-start) | collective-permute-done | bytes 786464 | tf_op jit(solution)/shard_map/ppermute | solution.py:413
  70.1 1.7 shard_map.123
  71.9 18.5 %all_to_all.48 = bf16[32,8,1024]{2,1,0:T(8,128)(2,1)S(1)} all-to-all(bf16[32,8,1024]{2,1,0:T(8,128)(2,1)S(1)} %bitcast.20), channel_id=1, replica_groups=mesh['x'=4,'y'=4,'core'=2,'z'=8] {'x','y','core'}, dimensions={0} | all-to-all | bytes 1048576 | tf_op jit(solution)/shard_map/all_to_all | solution.py:363
  90.4 1.0 shard_map.124
  91.5 13.2 %all_to_all.49.plane_ref = bf16[16,128,128]{2,1,0:T(8,128)(2,1)S(1)} all-to-all(bf16[16,128,128]{2,1,0:T(8,128)(2,1)S(1)} %get-tuple-element.27), channel_id=1, replica_groups=mesh['x'=4,'y'=4,'core'=2,'z'=8] {'x','y'}, dimensions={0} | all-to-all | bytes 1048576 | tf_op jit(solution)/shard_map/all_to_all | solution.py:363
  104.7 12.3 %all_to_all.50.column_ref = bf16[8,80,128]{2,1,0:T(8,128)(2,1)S(1)} all-to-all(bf16[8,80,128]{2,1,0:T(8,128)(2,1)S(1)} %shard_map.125), channel_id=1, replica_groups=mesh['x'=4,'y'=4,'core'=2,'z'=8] {'z'}, dimensions={0} | all-to-all | bytes 327680 | tf_op jit(solution)/shard_map/all_to_all | solution.py:363
  117.0 4.8 %all-to-all-start.5 = ((bf16[16,16,512]{2,1,0:T(8,128)(2,1)}), bf16[16,16,512]{2,1,0:T(8,128)(2,1)S(1)}, u32[]{:S(2)}, u32[]{:S(2)}) async-start(bf16[16,16,512]{2,1,0:T(8,128)(2,1)} %bitcast.26), calls=%async_computation.6 | async-start | bytes 524288 | tf_op jit(solution)/shard_map/all_to_all | solution.py:363
  121.8 7.3 %all-to-all-done.5 = bf16[16,16,512]{2,1,0:T(8,128)(2,1)S(1)} async-done(((bf16[16,16,512]{2,1,0:T(8,128)(2,1)}), bf16[16,16,512]{2,1,0:T(8,128)(2,1)S(1)}, u32[]{:S(2)}, u32[]{:S(2)}) %all-to-all-start.5) | async-done | bytes 262176 | tf_op jit(solution)/shard_map/all_to_all | solution.py:363
  129.2 11.1 %all_to_all.51.mine_ref = bf16[16,16,640]{2,1,0:T(8,128)(2,1)S(1)} all-to-all(bf16[16,16,640]{2,1,0:T(8,128)(2,1)S(1)} %broadcast_in_dim.2), channel_id=1, replica_groups=mesh['x'=4,'y'=4,'core'=2,'z'=8] {'x','y'}, dimensions={0} | all-to-all | bytes 655360 | tf_op jit(solution)/shard_map/all_to_all | solution.py:363
  140.3 4.5 %collective-permute-start.1 = (bf16[16,16,640]{2,1,0:T(8,128)(2,1)S(1)}, bf16[16,16,640]{2,1,0:T(8,128)(2,1)S(1)}, u32[]{:S(2)}, u32[]{:S(2)}) collective-permute-start(bf16[16,16,640]{2,1,0:T(8,128)(2,1)S(1)} %all_to_all.51.mine_ref), channel_id=1, source_target_pairs={{0,8},{8,0},{1,9},{9,1},{2,10},{10,2},{3,11},{11,3},{4,12},{12,4},... | collective-permute-start | bytes 983048 | tf_op jit(solution)/shard_map/ppermute | solution.py:467
  144.9 1.3 collective-permute-done.1.other_ref
  146.9 3.3 %all-to-all-start.7 = ((f32[8,8,128]{2,1,0:T(8,128)}), f32[8,8,128]{2,1,0:T(8,128)S(1)}, u32[]{:S(2)}, u32[]{:S(2)}) async-start(f32[8,8,128]{2,1,0:T(8,128)} %shard_map.127), calls=%async_computation.8 | async-start | bytes 65536 | tf_op jit(solution)/shard_map/all_to_all | solution.py:363
  151.6 5.8 %all-to-all-done.7.squares_ref = f32[8,8,128]{2,1,0:T(8,128)S(1)} async-done(((f32[8,8,128]{2,1,0:T(8,128)}), f32[8,8,128]{2,1,0:T(8,128)S(1)}, u32[]{:S(2)}, u32[]{:S(2)}) %all-to-all-start.7) | async-done | bytes 32800 | tf_op jit(solution)/shard_map/all_to_all | solution.py:363
  157.4 1.2 shard_map.128
  158.6 3.0 %all-gather.5.cloned.1.call-done.rows_ref = bf16[1536,1024]{1,0:T(8,128)(2,1)} async-done(((bf16[192,1024]{1,0:T(8,128)(2,1)}), bf16[1536,1024]{1,0:T(8,128)(2,1)}) %all-gather.5.cloned.1.call-update) | async-done | bytes 3145744 | tf_op jit(solution)/shard_map/all_gather | solution.py:440
  161.5 4.1 %shard_map.129 = f32[256,1024]{1,0:T(8,128)} custom-call(bf16[1536,1024]{1,0:T(8,128)(2,1)} %all-gather.5.cloned.1.call-done.rows_ref, s32[16,128]{1,0:T(8,128)} %copy-done.3, f32[64,1024]{1,0:T(8,128)} %get-tuple-element.17.after_ref), custom_call_target="tpu_custom_call" | custom-call | bytes 9000000 | tf_op jit(solution)/shard_map/pallas_call | solution.py:349
  (31 shorter events, 3.0 us)
Async XLA Ops:
  7.2 50.9 %copy-start.1 = (bf16[128,1024]{1,0:T(8,128)(2,1)S(1)}, bf16[128,1024]{1,0:T(8,128)(2,1)}, u32[]{:S(2)}) copy-start(bf16[128,1024]{1,0:T(8,128)(2,1)} %ct_ref.1) | copy-start | bytes 786436
  7.2 50.9 %copy-start.5 = (f32[512]{0:T(512)S(1)}, f32[512]{0:T(512)}, u32[]{:S(2)}) copy-start(f32[512]{0:T(512)} %param.16) | copy-start | bytes 6148
  7.2 50.9 %copy-start.4 = (f32[1024]{0:T(1024)S(1)}, f32[1024]{0:T(1024)}, u32[]{:S(2)}) copy-start(f32[1024]{0:T(1024)} %param.15) | copy-start | bytes 12292
  7.2 50.8 %copy-start.6 = (s32[1,8]{1,0:T(1,128)S(1)}, s32[1,8]{1,0:T(1,128)}, u32[]{:S(2)}) copy-start(s32[1,8]{1,0:T(1,128)} %lens_ref.1) | copy-start | bytes 100
  7.2 50.8 %all-gather.3.cloned.1.call-start = ((), (), s32[]{:S(2)}) async-start(), calls=%async_computation.9 | async-start | bytes 5570560 | tf_op jit(solution)/shard_map/all_gather | solution.py:372
  9.1 107.9 %reduce-scatter.2.cloned.1.call-start = ((), (), s32[]{:S(2)}) async-start(), calls=%async_computation.11 | async-start | bytes 2359296 | tf_op jit(solution)/shard_map/reduce_scatter | solution.py:427
  10.9 47.1 %copy-start.2 = (s32[128,128]{1,0:T(8,128)S(1)}, s32[128,128]{1,0:T(8,128)}, u32[]{:S(2)}) copy-start(s32[128,128]{1,0:T(8,128)} %get-tuple-element.19.tgt_ref) | copy-start | bytes 196612
  58.1 2.5 %copy-start = (bf16[2560,1024]{1,0:T(8,128)(2,1)S(1)}, bf16[2560,1024]{1,0:T(8,128)(2,1)}, u32[]{:S(2)}) copy-start(bf16[2560,1024]{1,0:T(8,128)(2,1)} %all-gather.3.cloned.1.call-done) | copy-start | bytes 15728644
  67.7 2.4 %collective-permute-start = (bf16[128,3072]{1,0:T(8,128)(2,1)S(1)}, bf16[128,3072]{1,0:T(8,128)(2,1)S(1)}, u32[]{:S(2)}, u32[]{:S(2)}) collective-permute-start(bf16[128,3072]{1,0:T(8,128)(2,1)S(1)} %get-tuple-element.22), channel_id=1, source_target_pairs={{0,8},{8,0},{1,9},{9,1},{2,10},{10,2},{3,11},{11,3},{4,12},{12,4},... | collective-permute-start | bytes 2359304 | tf_op jit(solution)/shard_map/ppermute | solution.py:413
  71.8 89.7 %all-gather.5.cloned.1.call-start = ((), (), s32[]{:S(2)}) async-start(), calls=%async_computation.10 | async-start | bytes 3538944 | tf_op jit(solution)/shard_map/all_gather | solution.py:440
  117.0 12.1 %all-to-all-start.5 = ((bf16[16,16,512]{2,1,0:T(8,128)(2,1)}), bf16[16,16,512]{2,1,0:T(8,128)(2,1)S(1)}, u32[]{:S(2)}, u32[]{:S(2)}) async-start(bf16[16,16,512]{2,1,0:T(8,128)(2,1)} %bitcast.26), calls=%async_computation.6 | async-start | bytes 524288 | tf_op jit(solution)/shard_map/all_to_all | solution.py:363
  140.3 5.8 %collective-permute-start.1 = (bf16[16,16,640]{2,1,0:T(8,128)(2,1)S(1)}, bf16[16,16,640]{2,1,0:T(8,128)(2,1)S(1)}, u32[]{:S(2)}, u32[]{:S(2)}) collective-permute-start(bf16[16,16,640]{2,1,0:T(8,128)(2,1)S(1)} %all_to_all.51.mine_ref), channel_id=1, source_target_pairs={{0,8},{8,0},{1,9},{9,1},{2,10},{10,2},{3,11},{11,3},{4,12},{12,4},... | collective-permute-start | bytes 983048 | tf_op jit(solution)/shard_map/ppermute | solution.py:467
  146.9 10.5 %all-to-all-start.7 = ((f32[8,8,128]{2,1,0:T(8,128)}), f32[8,8,128]{2,1,0:T(8,128)S(1)}, u32[]{:S(2)}, u32[]{:S(2)}) async-start(f32[8,8,128]{2,1,0:T(8,128)} %shard_map.127), calls=%async_computation.8 | async-start | bytes 65536 | tf_op jit(solution)/shard_map/all_to_all | solution.py:363
  151.0 0.6 copy-start.3
Sparse Core Ops, SparseCore 0:
  10.4 47.5 all-gather.2
  72.0 36.0 reduce-scatter.1
  110.4 51.0 all-gather.4

commit v9 on v8

--- a/solution.py
+++ b/solution.py
@@ -74,34 +74,16 @@
     req_ref[...] = requests[:OWNERS].astype(jnp.int32)
 
 
+def chosen(tgt_ref):
+    return (tgt_ref[:, :1] == iota((TOK, OWNERS * SLOTS), 1)).astype(F32).astype(BF16)
+
+
 def layer_kernel(
     lens_ref, got_ref, tgt_ref, weights_ref, gin_ref, gat_ref, ct_ref,
-    out_ref, slots_ref, keep_ref, send_ref,
-    wm, wo, dmx, sems,
+    out_ref, keep_ref, send_ref, dmx, xhat_ref, rstd_ref,
 ):
     core = lax.axis_index("core")
-    copies = []
-    for half in range(2):
-        for part in range(4):
-            z = pl.ds(2 * part, 2)
-            copies.append(
-                pltpu.make_async_copy(
-                    weights_ref.at[half, z, pl.ds(0, TOK), :],
-                    wm.at[half, z],
-                    sems.at[len(copies)],
-                )
-            )
-    for half in range(2):
-        copies.append(
-            pltpu.make_async_copy(
-                weights_ref.at[half, :, pl.ds(TOK, 32), :], wo.at[:, half], sems.at[len(copies)]
-            )
-        )
-    for copy in copies:
-        copy.start()
-
-    pick = (tgt_ref[:, :1] == iota((TOK, OWNERS * SLOTS), 1)).astype(F32).astype(BF16)
-    emb = mm(pick, got_ref[...])
+    emb = mm(chosen(tgt_ref), got_ref[...])
     gin = gin_ref[...]
     gat = gat_ref[...]
     centered = emb - jnp.mean(emb, axis=1, keepdims=True)
@@ -119,16 +101,9 @@
         seg_col = seg_col + (other >= end).astype(jnp.int32)
     allowed = (seg_row == seg_col) & (other <= position)
 
-    mixtures = []
-    for half in range(2):
-        mixture = jnp.zeros((TOK, D), F32)
-        for part in range(4):
-            copies[4 * half + part].wait()
-            rows = wm[half, 2 * part : 2 * part + 2].reshape(2 * TOK, D)
-            mixture = mixture + mm(normed[:, 256 * part : 256 * part + 256], rows)
-        mixtures.append(mixture)
-    mix0, mix1 = mixtures
-    wm0, wm1 = wm[0].reshape(D, D), wm[1].reshape(D, D)
+    mix0, mix1 = (
+        mm(normed, weights_ref[half, :, :TOK, :].reshape(D, D)) for half in range(2)
+    )
 
     sig0, sig1 = jax.nn.sigmoid(mix0), jax.nn.sigmoid(mix1)
     act0, act1 = (mix0 * sig0).astype(BF16), (mix1 * sig1).astype(BF16)
@@ -157,9 +132,8 @@
     scaled = ahat * gat
     gated = (scaled * gate_u).astype(BF16)
 
-    copies[8].wait()
-    copies[9].wait()
-    w_out = wo[...].reshape(AW, D)
+    w_out = jnp.stack([weights_ref[half, :, TOK:, :] for half in range(2)], axis=1)
+    w_out = w_out.reshape(AW, D)
     ct = ct_ref[...]
     out_ref[...] = (emb + mm(gated, w_out)).astype(BF16)
 
@@ -187,18 +161,8 @@
     d_mix1 = (d_act1 * slope1).astype(BF16)
     dmx[0] = d_mix0
     dmx[1] = d_mix1
-    d_normed = (mm_nt(d_mix0, wm0) + mm_nt(d_mix1, wm1)).astype(BF16).astype(F32)
-    d_xhat = d_normed * gin
-    d_emb = (
-        rstd
-        * (
-            d_xhat
-            - jnp.mean(d_xhat, axis=1, keepdims=True)
-            - xhat * jnp.mean(d_xhat * xhat, axis=1, keepdims=True)
-        )
-        + ct.astype(F32)
-    ).astype(BF16)
-    slots_ref[...] = mm_tn(pick, d_emb).astype(BF16)
+    xhat_ref[...] = xhat
+    rstd_ref[...] = jnp.broadcast_to(rstd, (TOK, TOK))
     for side, dst in ((1 - core, send_ref), (core, keep_ref)):
         dst[:, 0:1024] = normed
         dst[:, 1024:2048] = dmx[side]
@@ -206,9 +170,35 @@
         dst[:, 2560:FACT] = ct_ref[:, pl.ds(pl.multiple_of(side * AW, AW), AW)]
 
 
-def grads_kernel(keep_ref, theirs_ref, mix_ref, out_ref, mix, out, sems):
+def rows_kernel(tgt_ref, weights_ref, gin_ref, ct_ref, dmx, xhat_ref, rstd_ref, slots_ref):
+    d_normed = mm_nt(dmx[0], weights_ref[0, :, :TOK, :].reshape(D, D))
+    d_normed = d_normed + mm_nt(dmx[1], weights_ref[1, :, :TOK, :].reshape(D, D))
+    d_xhat = d_normed.astype(BF16).astype(F32) * gin_ref[...]
+    xhat = xhat_ref[...]
+    d_emb = (
+        rstd_ref[:, :1]
+        * (
+            d_xhat
+            - jnp.mean(d_xhat, axis=1, keepdims=True)
+            - xhat * jnp.mean(d_xhat * xhat, axis=1, keepdims=True)
+        )
+        + ct_ref[...].astype(F32)
+    ).astype(BF16)
+    slots_ref[...] = mm_tn(chosen(tgt_ref), d_emb).astype(BF16)
+
+
+def grads_kernel(keep_ref, theirs_ref, out_ref, buf, sems):
     def both(first, last):
         return jnp.concatenate([keep_ref[:, first:last], theirs_ref[:, first:last]], axis=0)
+
+    grad = mm_tn(both(2048, 2560), both(2560, FACT))
+    for z in range(NZ):
+        for p in range(XY):
+            r, c = z * 64 + (p // 2) * 8, (p % 2) * 256
+            part = grad[r : r + 8, c : c + 256]
+            buf[z, p, :, 512:PCOLS] = jnp.concatenate(
+                [part[:, :128], part[:, 128:]], axis=0
+            ).astype(BF16)
 
     copies = []
     d_mix = both(1024, 2048)
@@ -216,32 +206,13 @@
         grad = mm_tn(both(z * TOK, (z + 1) * TOK), d_mix)
         for p in range(XY):
             part = grad[8 * p : 8 * p + 8]
-            mix[z, p] = jnp.concatenate([part[:, :512], part[:, 512:]], axis=0).astype(BF16)
-        copies.append(pltpu.make_async_copy(mix.at[z], mix_ref.at[z], sems.at[z]))
+            buf[z, p, :, 0:512] = jnp.concatenate(
+                [part[:, :512], part[:, 512:]], axis=0
+            ).astype(BF16)
+        copies.append(pltpu.make_async_copy(buf.at[z], out_ref.at[z], sems.at[z]))
         copies[-1].start()
-
-    grad = mm_tn(both(2048, 2560), both(2560, FACT))
-    for z in range(NZ):
-        for p in range(XY):
-            r, c = z * 64 + (p // 2) * 8, (p % 2) * 256
-            part = grad[r : r + 8, c : c + 256]
-            out[p, z * PROWS : (z + 1) * PROWS] = jnp.concatenate(
-                [part[:, :128], part[:, 128:]], axis=0
-            ).astype(BF16)
-    copies.append(pltpu.make_async_copy(out, out_ref, sems.at[NZ]))
-    copies[-1].start()
     for copy in copies:
         copy.wait()
-
-
-def column_kernel(plane_ref, asked_ref, out_ref):
-    total = jnp.sum(plane_ref[...].astype(F32), axis=0).astype(BF16)
-    asked = asked_ref[...]
-    low, high = ((part).astype(F32).astype(BF16) for part in (asked & 127, asked >> 7))
-    for z in range(NZ):
-        out_ref[z, :PROWS] = total[z * PROWS : (z + 1) * PROWS]
-        out_ref[z, PROWS : PROWS + OWNERS] = low
-        out_ref[z, PROWS + OWNERS :] = high
 
 
 def pack_kernel(rows_ref, out_ref):
@@ -250,11 +221,11 @@
     out_ref[...] = mm(take.astype(F32).astype(BF16), rows_ref[...]).astype(BF16)
 
 
-def names_kernel(column_ref, out_ref):
+def names_kernel(asked_ref, out_ref):
     first = lax.axis_index("z") * 256
     count = NZ * USED
-    low = column_ref[:, PROWS : PROWS + OWNERS].reshape(NZ * OWNERS, 128)
-    high = column_ref[:, PROWS + OWNERS :].reshape(NZ * OWNERS, 128)
+    asked = asked_ref[...].reshape(NZ * OWNERS, 128)
+    low, high = (part.astype(F32).astype(BF16) for part in (asked & 127, asked >> 7))
     row, col = iota((count, NZ * OWNERS), 0), iota((count, NZ * OWNERS), 1)
     owner = (row // CAP == col).astype(F32).astype(BF16)
     lane = iota((count, 128), 1)
@@ -382,52 +353,56 @@
     got = exchange(found.reshape(OWNERS, SLOTS, D), TABLE)
 
     smem = pl.BlockSpec(memory_space=pltpu.SMEM)
-    layer_out, grad_slots, keep, send = call(
+    gin = gain_in.reshape(1, D)
+    layer_out, keep, send, d_mix, xhat, rstd = call(
         layer_kernel,
         [
             ((TOK, D), BF16),
-            ((OWNERS * SLOTS, D), BF16),
             ((TOK, FACT), BF16),
             ((TOK, FACT), BF16),
+            ((2, TOK, D), BF16),
+            ((TOK, D), F32),
+            ((TOK, TOK), F32),
         ],
         (
             user_lengths,
             got.reshape(OWNERS * SLOTS, D),
             target,
             weights,
-            gain_in.reshape(1, D),
+            gin,
             gain_attn.reshape(1, AW),
             cotangent,
         ),
-        specs=[smem, vmem(), vmem(), pinned, vmem(), vmem(), vmem()],
+        specs=[smem] + [vmem()] * 6,
+        cost_estimate=cost(7),
+        compiler_params=pltpu.CompilerParams(vmem_limit_bytes=32 * MB),
+    )
+
+    theirs = lax.ppermute(send, "core", [(0, 1), (1, 0)])
+    grads = call(
+        grads_kernel,
+        [((NZ, XY, PROWS, PCOLS), BF16)],
+        (keep, theirs),
+        outs_specs=anywhere,
         scratch_shapes=[
-            pltpu.VMEM((2, NZ, TOK, D), BF16),
-            pltpu.VMEM((NZ, 2, 32, D), BF16),
-            pltpu.VMEM((2, TOK, D), BF16),
-            pltpu.SemaphoreType.DMA((10,)),
-        ],
-        cost_estimate=cost(9),
-        compiler_params=pltpu.CompilerParams(vmem_limit_bytes=32 * MB),
-    )
-
-    theirs = lax.ppermute(send, "core", [(0, 1), (1, 0)])
-    mix_part, out_part = call(
-        grads_kernel,
-        [((NZ, XY, PROWS, 512), BF16), ((XY, NZ * PROWS, 128), BF16)],
-        (keep, theirs),
-        outs_specs=[anywhere, anywhere],
-        scratch_shapes=[
-            pltpu.VMEM((NZ, XY, PROWS, 512), BF16),
-            pltpu.VMEM((XY, NZ * PROWS, 128), BF16),
-            pltpu.SemaphoreType.DMA((NZ + 1,)),
+            pltpu.VMEM((NZ, XY, PROWS, PCOLS), BF16),
+            pltpu.SemaphoreType.DMA((NZ,)),
         ],
         cost_estimate=cost(3),
         compiler_params=pltpu.CompilerParams(vmem_limit_bytes=30 * MB),
     )
-    mix_column = lax.psum_scatter(
-        mix_part.reshape(NZ * XY * PROWS, 512), "z", scatter_dimension=0, tiled=True
-    )
-
+    grads, d_mix = lax.optimization_barrier((grads, d_mix))
+    column = lax.psum_scatter(
+        grads.reshape(NZ * XY * PROWS, PCOLS), "z", scatter_dimension=0, tiled=True
+    )
+
+    grad_slots = call(
+        rows_kernel,
+        [((OWNERS * SLOTS, D), BF16)],
+        (target, weights, gin, cotangent, d_mix, xhat, rstd),
+        cost_estimate=cost(3),
+        compiler_params=pltpu.CompilerParams(vmem_limit_bytes=32 * MB),
+    )
     received = exchange(grad_slots.reshape(OWNERS, SLOTS, D), TABLE)
     packed = call(
         pack_kernel,
@@ -436,33 +411,19 @@
         cost_estimate=cost(2),
         compiler_params=pltpu.CompilerParams(vmem_limit_bytes=16 * MB),
     )
-    out_part, packed = lax.optimization_barrier((out_part, packed))
+    asked, packed = lax.optimization_barrier((asked, packed))
     gathered = lax.all_gather(packed, "z", axis=0, tiled=True)
-
-    out_column = call(
-        column_kernel,
-        [((NZ, PROWS + 2 * OWNERS, 128), BF16)],
-        (exchange(out_part, ("x", "y")), asked),
-        cost_estimate=cost(1),
-        compiler_params=pltpu.CompilerParams(vmem_limit_bytes=16 * MB),
-    )
-    out_column = exchange(out_column, "z")
-    mix_column, out_column = lax.optimization_barrier((mix_column, out_column))
+    asked = exchange(jnp.broadcast_to(asked[None], (NZ, OWNERS, 128)), "z")
     names = call(
         names_kernel,
         [((PROWS, 128), jnp.int32)],
-        (out_column,),
+        (asked,),
         cost_estimate=cost(2),
         compiler_params=pltpu.CompilerParams(vmem_limit_bytes=16 * MB),
     )
-    mix_plane = exchange(mix_column.reshape(XY, PROWS, 512), ("x", "y"))
-    whole = jnp.concatenate(
-        [
-            jnp.sum(mix_plane.astype(F32), axis=0),
-            jnp.sum(out_column[:, :PROWS].astype(F32), axis=0),
-        ],
-        axis=1,
-    ).astype(BF16)
+    column, names = lax.optimization_barrier((column, names))
+    plane = exchange(column.reshape(XY, PROWS, PCOLS), ("x", "y"))
+    whole = jnp.sum(plane.astype(F32), axis=0).astype(BF16)
     mine = exchange(jnp.broadcast_to(whole[None], (XY, PROWS, PCOLS)), ("x", "y"))
     other = lax.ppermute(mine, "core", [(0, 1), (1, 0)])
 

time: 173 us -> 173 us (level)
  blocking collectives: 86 us -> 101 us
  waiting for transfers between devices: 31.2 us -> 20.9 us
  starting transfers between devices: 13.1 us -> 6.93 us
  local copies, waits for them, and re-layouts: 7.5 us -> 9.99 us
    all_to_all x6 -> x7, blocking collectives: 86 us -> 101 us  [exchange(): return lax.all_to_all(array, axes, split_axis=0, concat_axis=0, tiled=True)]
    all_to_all x2 -> x0, waiting for transfers between devices: 13.1 us -> none  [exchange(): return lax.all_to_all(array, axes, split_axis=0, concat_axis=0, tiled=True)]
    all_to_all x2 -> x0, starting transfers between devices: 8.1 us -> none  [exchange(): return lax.all_to_all(array, axes, split_axis=0, concat_axis=0, tiled=True)]
    unnamed x14 -> x16, local copies, waits for them, and re-layouts: 3.1 us -> 5.58 us
    ppermute x1, starting transfers between devices: 4.55 us -> 6.45 us  [shards(): other = lax.ppermute(mine, 'core', [(0, 1), (1, 0)])]
  transfers between devices with their start and end apart: 7 -> 5, of which waited for: 6 -> 5; matrix products, arithmetic and copies ran while one was open for 3% -> 3% of each run, Pallas kernels for 3% -> 4%
where the time goes in v9:
time: 173 us; the launch traced here: 172 us
  blocking collectives  101 us (58%)
  waiting for transfers between devices  20.9 us (12%)
  Pallas kernels  18.8 us (11%)
  between operations  13.9 us (8%)
  local copies, waits for them, and re-layouts  9.99 us (6%)
  starting transfers between devices  6.93 us (4%)
    all_to_all x7, blocking collectives, exchange(): return lax.all_to_all(array, axes, split_axis=0, concat_axis=0, tiled=True)  101 us
    pallas_call x10, Pallas kernels, call(): pl.pallas_call(body, out_shape=shapes[0] if one else shapes, in_specs=spe...  18.8 us
    all_gather x1, waiting for transfers between devices, shards(): lax.all_gather(share, ('core', 'z'), axis=0, tiled=True)  11.8 us
    ppermute x1, starting transfers between devices, shards(): other = lax.ppermute(mine, 'core', [(0, 1), (1, 0)])  6.45 us
    unnamed x16, local copies, waits for them, and re-layouts  5.58 us
    gather x1, local copies, waits for them, and re-layouts, shards(): found = item_table.at[wanted].get(mode='promise_in_bounds')  4.29 us
    all_gather x1, waiting for transfers between devices, shards(): gathered = lax.all_gather(packed, 'z', axis=0, tiled=True)  4.11 us
  transfers between devices with their start and end apart: 5, of which 5 were waited for; matrix products, arithmetic and copies ran while one was open for 3% of the time, Pallas kernels for 4%

profile of v9, /device:TPU:1, one launch (start us, length us, event | category | flops | bytes accessed | tf_op | source)
XLA Modules:
  0.0 171.9 jit_solution(16378480451181353185)
XLA Ops:
  7.3 1.8 %shard_map.121 = bf16[160,1024]{1,0:T(8,128)(2,1)} custom-call(bf16[128,2048]{1,0:T(8,128)(2,1)} %mix_ref.1, bf16[64,1024]{1,0:T(8,128)(2,1)} %out_ref.1), custom_call_target="tpu_custom_call" | custom-call | tf_op jit(solution)/shard_map/pallas_call | solution.py:320
  9.2 1.7 %shard_map.120 = (s32[32,128]{1,0:T(8,128)}, s32[128,128]{1,0:T(8,128)}) custom-call(s32[1,128]{1,0:T(1,128)} %bitcast.31, s32[1,128]{1,0:T(1,128)} %bitcast.32), custom_call_target="tpu_custom_call" | custom-call | tf_op jit(solution)/shard_map/pallas_call | solution.py:320
  10.9 15.6 %all_to_all.42 = s32[32,1,128]{2,1,0:T(1,128)S(1)} all-to-all(s32[32,1,128]{2,1,0:T(1,128)} %bitcast.29), channel_id=1, replica_groups=mesh['x'=4,'y'=4,'core'=2,'z'=8] {'x','y','core'}, dimensions={0} | all-to-all | bytes 32768 | tf_op jit(solution)/shard_map/all_to_all | solution.py:334
  26.6 4.3 %gather_fusion = bf16[256,1024]{1,0:T(8,128)(2,1)S(1)} fusion(bf16[2048,1024]{1,0:T(8,128)(2,1)} %param.9, s32[1024]{0:T(1024)S(1)} %pad_clamp_fusion), kind=kCustom, calls=%fused_computation | custom fusion | bytes 1049600 | tf_op jit(solution)/shard_map/gather | solution.py:352
  30.9 15.3 %all_to_all.43 = bf16[32,8,1024]{2,1,0:T(8,128)(2,1)S(1)} all-to-all(bf16[32,8,1024]{2,1,0:T(8,128)(2,1)S(1)} %bitcast.25), channel_id=1, replica_groups=mesh['x'=4,'y'=4,'core'=2,'z'=8] {'x','y','core'}, dimensions={0} | all-to-all | bytes 1048576 | tf_op jit(solution)/shard_map/all_to_all | solution.py:334
  46.2 11.8 %all-gather.3.cloned.1.call-done = bf16[2560,1024]{1,0:T(8,128)(2,1)} async-done(((bf16[160,1024]{1,0:T(8,128)(2,1)}), bf16[2560,1024]{1,0:T(8,128)(2,1)}) %all-gather.3.cloned.1.call-update) | async-done | bytes 5242896 | tf_op jit(solution)/shard_map/all_gather | solution.py:343
  58.1 2.5 %copy-done = bf16[2560,1024]{1,0:T(8,128)(2,1)S(1)} copy-done((bf16[2560,1024]{1,0:T(8,128)(2,1)S(1)}, bf16[2560,1024]{1,0:T(8,128)(2,1)}, u32[]{:S(2)}) %copy-start) | copy-done | bytes 5242904
  60.5 4.1 %shard_map.122 = (bf16[128,1024]{1,0:T(8,128)(2,1)}, bf16[128,3072]{1,0:T(8,128)(2,1)S(1)}, bf16[128,3072]{1,0:T(8,128)(2,1)S(1)}, bf16[2,128,1024]{2,1,0:T(8,12...) custom-call(s32[1,8]{1,0:T(1,128)S(1)} %copy-done.7, bf16[256,1024]{1,0:T(8,128)(2,1)S(1)} %bitcast.19, ...), custom_call_target="tpu_custom_call" | custom-call | bytes 21000000 | tf_op jit(solution)/shard_map/pallas_call | solution.py:320
  65.0 2.0 %collective-permute-done.theirs_ref = bf16[128,3072]{1,0:T(8,128)(2,1)S(1)} collective-permute-done((bf16[128,3072]{1,0:T(8,128)(2,1)S(1)}, bf16[128,3072]{1,0:T(8,128)(2,1)S(1)}, u32[]{:S(2)}, u32[]{:S(2)}) %collective-permute-start) | collective-permute-done | bytes 786464 | tf_op jit(solution)/shard_map/ppermute | solution.py:381
  67.0 1.9 %shard_map.123 = bf16[8,16,16,640]{3,2,1,0:T(8,128)(2,1)} custom-call(bf16[128,3072]{1,0:T(8,128)(2,1)S(1)} %get-tuple-element.23.keep_ref, bf16[128,3072]{1,0:T(8,128)(2,1)S(1)} %collective-permute-done.theirs_ref), custom_call_target="tpu_custom_call" | custom-call | bytes 9000000 | tf_op jit(solution)/shard_map/pallas_call | solution.py:320
  69.1 2.5 %copy-done.1 = bf16[2560,1024]{1,0:T(8,128)(2,1)S(1)} copy-done((bf16[2560,1024]{1,0:T(8,128)(2,1)S(1)}, bf16[2560,1024]{1,0:T(8,128)(2,1)}, u32[]{:S(2)}) %copy-start.1) | copy-done | bytes 5242904
  71.5 1.9 %shard_map.124 = bf16[256,1024]{1,0:T(8,128)(2,1)S(1)} custom-call(s32[128,128]{1,0:T(8,128)S(1)} %copy-done.3, bf16[2,8,160,1024]{3,2,1,0:T(8,128)(2,1)S(1)} %bitcast.18, f32[1,1024]{1,0:T(1,128)S(1)} %bitcast.23, bf16[128,1024]{1,0:T(8,128)(2,1)S(1)} %copy-done.2, bf16[2,128,1024]{2,1,0:T(8,128)(2,1)S(1)} %get-tuple-element.26.dmx, ...), custom_call_target="tpu_custom_call" | custom-call | bytes 9000000 | tf_op jit(solution)/shard_map/pallas_call | solution.py:320
  73.5 18.5 %all_to_all.44 = bf16[32,8,1024]{2,1,0:T(8,128)(2,1)S(1)} all-to-all(bf16[32,8,1024]{2,1,0:T(8,128)(2,1)S(1)} %bitcast.20), channel_id=1, replica_groups=mesh['x'=4,'y'=4,'core'=2,'z'=8] {'x','y','core'}, dimensions={0} | all-to-all | bytes 1048576 | tf_op jit(solution)/shard_map/all_to_all | solution.py:334
  92.0 1.0 shard_map.125
  93.1 14.4 %all_to_all.45.asked_ref = s32[8,32,128]{2,1,0:T(8,128)S(1)} all-to-all(s32[8,32,128]{2,1,0:T(8,128)S(1)} %broadcast_in_dim.4), channel_id=1, replica_groups=mesh['x'=4,'y'=4,'core'=2,'z'=8] {'z'}, dimensions={0} | all-to-all | bytes 262144 | tf_op jit(solution)/shard_map/all_to_all | solution.py:334
  108.8 1.7 reduce-scatter.2.cloned.1.call-done
  110.5 14.4 %all_to_all.46 = bf16[16,16,640]{2,1,0:T(8,128)(2,1)S(1)} all-to-all(bf16[16,16,640]{2,1,0:T(8,128)(2,1)} %bitcast.26), channel_id=1, replica_groups=mesh['x'=4,'y'=4,'core'=2,'z'=8] {'x','y'}, dimensions={0} | all-to-all | bytes 655360 | tf_op jit(solution)/shard_map/all_to_all | solution.py:334
  125.1 10.9 %all_to_all.47.mine_ref = bf16[16,16,640]{2,1,0:T(8,128)(2,1)S(1)} all-to-all(bf16[16,16,640]{2,1,0:T(8,128)(2,1)S(1)} %broadcast_in_dim.5), channel_id=1, replica_groups=mesh['x'=4,'y'=4,'core'=2,'z'=8] {'x','y'}, dimensions={0} | all-to-all | bytes 655360 | tf_op jit(solution)/shard_map/all_to_all | solution.py:334
  135.9 6.5 %collective-permute-start.1 = (bf16[16,16,640]{2,1,0:T(8,128)(2,1)S(1)}, bf16[16,16,640]{2,1,0:T(8,128)(2,1)S(1)}, u32[]{:S(2)}, u32[]{:S(2)}) collective-permute-start(bf16[16,16,640]{2,1,0:T(8,128)(2,1)S(1)} %all_to_all.47.mine_ref), channel_id=1, source_target_pairs={{0,8},{8,0},{1,9},{9,1},{2,10},{10,2},{3,11},{11,3},{4,12},{12,4},... | collective-permute-start | bytes 983048 | tf_op jit(solution)/shard_map/ppermute | solution.py:428
  142.4 1.3 collective-permute-done.1.other_ref
  143.8 12.1 %all_to_all.48.squares_ref = f32[8,8,128]{2,1,0:T(8,128)S(1)} all-to-all(f32[8,8,128]{2,1,0:T(8,128)S(1)} %shard_map.127), channel_id=1, replica_groups=mesh['x'=4,'y'=4,'core'=2,'z'=8] {'z'}, dimensions={0} | all-to-all | bytes 65536 | tf_op jit(solution)/shard_map/all_to_all | solution.py:334
  156.0 1.2 shard_map.128
  157.1 4.1 %all-gather.5.cloned.1.call-done.rows_ref = bf16[1536,1024]{1,0:T(8,128)(2,1)} async-done(((bf16[192,1024]{1,0:T(8,128)(2,1)}), bf16[1536,1024]{1,0:T(8,128)(2,1)}) %all-gather.5.cloned.1.call-update) | async-done | bytes 3145744 | tf_op jit(solution)/shard_map/all_gather | solution.py:415
  161.3 4.1 %shard_map.129 = f32[256,1024]{1,0:T(8,128)} custom-call(bf16[1536,1024]{1,0:T(8,128)(2,1)} %all-gather.5.cloned.1.call-done.rows_ref, s32[16,128]{1,0:T(8,128)} %copy-done.4, f32[64,1024]{1,0:T(8,128)} %get-tuple-element.19.after_ref), custom_call_target="tpu_custom_call" | custom-call | bytes 9000000 | tf_op jit(solution)/shard_map/pallas_call | solution.py:320
  (29 shorter events, 2.3 us)
Async XLA Ops:
  7.2 50.9 %copy-start.2 = (bf16[128,1024]{1,0:T(8,128)(2,1)S(1)}, bf16[128,1024]{1,0:T(8,128)(2,1)}, u32[]{:S(2)}) copy-start(bf16[128,1024]{1,0:T(8,128)(2,1)} %ct_ref.3) | copy-start | bytes 786436
  7.2 50.9 %copy-start.6 = (f32[512]{0:T(512)S(1)}, f32[512]{0:T(512)}, u32[]{:S(2)}) copy-start(f32[512]{0:T(512)} %param.16) | copy-start | bytes 6148
  7.2 50.8 %copy-start.5 = (f32[1024]{0:T(1024)S(1)}, f32[1024]{0:T(1024)}, u32[]{:S(2)}) copy-start(f32[1024]{0:T(1024)} %param.15) | copy-start | bytes 12292
  7.2 50.8 %copy-start.7 = (s32[1,8]{1,0:T(1,128)S(1)}, s32[1,8]{1,0:T(1,128)}, u32[]{:S(2)}) copy-start(s32[1,8]{1,0:T(1,128)} %lens_ref.1) | copy-start | bytes 100
  7.2 50.8 %all-gather.3.cloned.1.call-start = ((), (), s32[]{:S(2)}) async-start(), calls=%async_computation.8 | async-start | bytes 5570560 | tf_op jit(solution)/shard_map/all_gather | solution.py:343
  9.1 101.4 %reduce-scatter.2.cloned.1.call-start = ((), (), s32[]{:S(2)}) async-start(), calls=%async_computation.10 | async-start | bytes 2949120 | tf_op jit(solution)/shard_map/reduce_scatter | solution.py:395
  10.9 47.1 %copy-start.3 = (s32[128,128]{1,0:T(8,128)S(1)}, s32[128,128]{1,0:T(8,128)}, u32[]{:S(2)}) copy-start(s32[128,128]{1,0:T(8,128)} %get-tuple-element.21.tgt_ref) | copy-start | bytes 196612
  58.1 2.5 %copy-start = (bf16[2560,1024]{1,0:T(8,128)(2,1)S(1)}, bf16[2560,1024]{1,0:T(8,128)(2,1)}, u32[]{:S(2)}) copy-start(bf16[2560,1024]{1,0:T(8,128)(2,1)} %all-gather.3.cloned.1.call-done) | copy-start | bytes 15728644
  64.7 2.4 %collective-permute-start = (bf16[128,3072]{1,0:T(8,128)(2,1)S(1)}, bf16[128,3072]{1,0:T(8,128)(2,1)S(1)}, u32[]{:S(2)}, u32[]{:S(2)}) collective-permute-start(bf16[128,3072]{1,0:T(8,128)(2,1)S(1)} %get-tuple-element.24), channel_id=1, source_target_pairs={{0,8},{8,0},{1,9},{9,1},{2,10},{10,2},{3,11},{11,3},{4,12},{12,4},... | collective-permute-start | bytes 2359304 | tf_op jit(solution)/shard_map/ppermute | solution.py:381
  69.0 92.2 %all-gather.5.cloned.1.call-start = ((), (), s32[]{:S(2)}) async-start(), calls=%async_computation.9 | async-start | bytes 3538944 | tf_op jit(solution)/shard_map/all_gather | solution.py:415
  69.1 2.5 %copy-start.1 = (bf16[2560,1024]{1,0:T(8,128)(2,1)S(1)}, bf16[2560,1024]{1,0:T(8,128)(2,1)}, u32[]{:S(2)}) copy-start(bf16[2560,1024]{1,0:T(8,128)(2,1)} %all-gather.3.cloned.1.call-done) | copy-start | bytes 15728644
  108.2 0.6 copy-start.4
  135.9 7.7 %collective-permute-start.1 = (bf16[16,16,640]{2,1,0:T(8,128)(2,1)S(1)}, bf16[16,16,640]{2,1,0:T(8,128)(2,1)S(1)}, u32[]{:S(2)}, u32[]{:S(2)}) collective-permute-start(bf16[16,16,640]{2,1,0:T(8,128)(2,1)S(1)} %all_to_all.47.mine_ref), channel_id=1, source_target_pairs={{0,8},{8,0},{1,9},{9,1},{2,10},{10,2},{3,11},{11,3},{4,12},{12,4},... | collective-permute-start | bytes 983048 | tf_op jit(solution)/shard_map/ppermute | solution.py:428
Sparse Core Ops, SparseCore 0:
  10.4 47.5 all-gather.2
  69.1 41.3 reduce-scatter.1
  112.9 48.2 all-gather.4

commit v10 on v9

--- a/solution.py
+++ b/solution.py
@@ -44,10 +44,25 @@
     return lax.broadcasted_iota(jnp.int32, shape, dim)
 
 
-def share_kernel(mix_ref, out_ref, share_ref):
+def share_kernel(mix_ref, out_ref, share_ref, buf, sems):
     core = lax.axis_index("core")
-    share_ref[:TOK] = mix_ref[:, pl.ds(pl.multiple_of(core * D, D), D)]
-    share_ref[TOK:] = out_ref[pl.ds(pl.multiple_of(core * 32, 32), 32), :]
+    parts = (
+        (mix_ref.at[:, pl.ds(pl.multiple_of(core * D, D), D)], pl.ds(0, TOK)),
+        (out_ref.at[pl.ds(pl.multiple_of(core * 32, 32), 32), :], pl.ds(TOK, 32)),
+    )
+    inward, outward = [], []
+    for i, (source, place) in enumerate(parts):
+        inward.append(pltpu.make_async_copy(source, buf.at[place, :], sems.at[i]))
+        outward.append(
+            pltpu.make_async_copy(buf.at[place, :], share_ref.at[place, :], sems.at[2 + i])
+        )
+    for copy in inward:
+        copy.start()
+    for arrived, copy in zip(inward, outward):
+        arrived.wait()
+        copy.start()
+    for copy in outward:
+        copy.wait()
 
 
 def plan_kernel(owner_ref, row_ref, req_ref, tgt_ref):
@@ -224,7 +239,7 @@
 def names_kernel(asked_ref, out_ref):
     first = lax.axis_index("z") * 256
     count = NZ * USED
-    asked = asked_ref[...].reshape(NZ * OWNERS, 128)
+    asked = asked_ref[:, 8:].reshape(NZ * OWNERS, 128).astype(jnp.int32)
     low, high = (part.astype(F32).astype(BF16) for part in (asked & 127, asked >> 7))
     row, col = iota((count, NZ * OWNERS), 0), iota((count, NZ * OWNERS), 1)
     owner = (row // CAP == col).astype(F32).astype(BF16)
@@ -279,7 +294,7 @@
         copy.wait()
 
 
-def square_kernel(mine_ref, other_ref, out_ref):
+def square_kernel(mine_ref, other_ref, asked_ref, out_ref):
     total = jnp.zeros((PROWS, PCOLS), F32)
     for sums_ref in (mine_ref, other_ref):
         for i in range(XY):
@@ -287,12 +302,16 @@
             total = total + part * part
     mix = jnp.sum(total[:, :512])
     out = jnp.sum(total[:, 512:])
-    lane = iota((NZ, 8, 128), 2)
-    out_ref[...] = jnp.where(lane == 0, mix, jnp.where(lane == 1, out, 0.0))
+    lane = iota((8, 128), 1)
+    squares = jnp.where(lane == 0, mix, jnp.where(lane == 1, out, 0.0))
+    asked = asked_ref[...].astype(F32)
+    for z in range(NZ):
+        out_ref[z, :8] = squares
+        out_ref[z, 8:] = asked
 
 
 def scale_kernel(mine_ref, other_ref, squares_ref, mix_ref, out_ref):
-    total = jnp.sum(squares_ref[...], axis=0)[0:1]
+    total = jnp.sum(squares_ref[:, :8], axis=0)[0:1]
     mix_sq, out_sq = total[:, 0:1], total[:, 1:2]
     mix_scale = jnp.minimum(1.0, 1.0 / jnp.sqrt(mix_sq / float(D * 4 * AW) + 1e-06))
     out_scale = jnp.minimum(1.0, 1.0 / jnp.sqrt(out_sq / float(D * AW) + 1e-06))
@@ -339,7 +358,15 @@
 ):
     anywhere = pl.BlockSpec(memory_space=pl.ANY)
     pinned = pl.BlockSpec(memory_space=pltpu.HBM)
-    share = call(share_kernel, [((TOK + 32, D), BF16)], (w_mix, w_out))
+    share = call(
+        share_kernel,
+        [((TOK + 32, D), BF16)],
+        (w_mix, w_out),
+        specs=[anywhere, anywhere],
+        outs_specs=anywhere,
+        scratch_shapes=[pltpu.VMEM((TOK + 32, D), BF16), pltpu.SemaphoreType.DMA((4,))],
+        compiler_params=pltpu.CompilerParams(vmem_limit_bytes=60 * MB),
+    )
     weights = lax.all_gather(share, ("core", "z"), axis=0, tiled=True).reshape(2, NZ, 160, D)
 
     requests, target = call(
@@ -411,17 +438,7 @@
         cost_estimate=cost(2),
         compiler_params=pltpu.CompilerParams(vmem_limit_bytes=16 * MB),
     )
-    asked, packed = lax.optimization_barrier((asked, packed))
     gathered = lax.all_gather(packed, "z", axis=0, tiled=True)
-    asked = exchange(jnp.broadcast_to(asked[None], (NZ, OWNERS, 128)), "z")
-    names = call(
-        names_kernel,
-        [((PROWS, 128), jnp.int32)],
-        (asked,),
-        cost_estimate=cost(2),
-        compiler_params=pltpu.CompilerParams(vmem_limit_bytes=16 * MB),
-    )
-    column, names = lax.optimization_barrier((column, names))
     plane = exchange(column.reshape(XY, PROWS, PCOLS), ("x", "y"))
     whole = jnp.sum(plane.astype(F32), axis=0).astype(BF16)
     mine = exchange(jnp.broadcast_to(whole[None], (XY, PROWS, PCOLS)), ("x", "y"))
@@ -429,8 +446,8 @@
 
     squares = call(
         square_kernel,
-        [((NZ, 8, 128), F32)],
-        (mine, other),
+        [((NZ, 8 + OWNERS, 128), F32)],
+        (mine, other, asked),
         cost_estimate=cost(1),
         compiler_params=pltpu.CompilerParams(vmem_limit_bytes=16 * MB),
     )
@@ -440,6 +457,13 @@
         [((TOK, 4 * AW), F32), ((64, D), F32)],
         (mine, other, squares),
         cost_estimate=cost(2),
+        compiler_params=pltpu.CompilerParams(vmem_limit_bytes=16 * MB),
+    )
+    names = call(
+        names_kernel,
+        [((PROWS, 128), jnp.int32)],
+        (squares,),
+        cost_estimate=cost(1),
         compiler_params=pltpu.CompilerParams(vmem_limit_bytes=16 * MB),
     )
     table_grad = call(

time: 173 us -> 173 us (level)
  blocking collectives: 101 us -> 90.6 us
  waiting for transfers between devices: 20.9 us -> 31 us
    reduce_scatter x1, waiting for transfers between devices: 1.7 us -> 14.8 us  [shards(): lax.psum_scatter(grads.reshape(NZ * XY * PROWS, PCOLS), 'z', scatter_dime...]
    all_to_all x7 -> x6, blocking collectives: 101 us -> 90.6 us  [exchange(): return lax.all_to_all(array, axes, split_axis=0, concat_axis=0, tiled=True)]
    all_gather x1, waiting for transfers between devices: 4.11 us -> 1.01 us  [shards(): gathered = lax.all_gather(packed, 'z', axis=0, tiled=True)]
where the time goes in v10:
time: 173 us; the launch traced here: 172 us
  blocking collectives  90.6 us (52%)
  waiting for transfers between devices  31 us (18%)
  Pallas kernels  18.7 us (11%)
  between operations  13.9 us (8%)
  local copies, waits for them, and re-layouts  9.98 us (6%)
  starting transfers between devices  7.96 us (5%)
    all_to_all x6, blocking collectives, exchange(): return lax.all_to_all(array, axes, split_axis=0, concat_axis=0, tiled=True)  90.6 us
    pallas_call x10, Pallas kernels, call(): pl.pallas_call(body, out_shape=shapes[0] if one else shapes, in_specs=spe...  18.7 us
    reduce_scatter x1, waiting for transfers between devices, shards(): lax.psum_scatter(grads.reshape(NZ * XY * PROWS, PCOLS), 'z', scatter_dime...  14.8 us
    all_gather x1, waiting for transfers between devices, shards(): lax.all_gather(share, ('core', 'z'), axis=0, tiled=True)  11.9 us
    ppermute x1, starting transfers between devices, shards(): other = lax.ppermute(mine, 'core', [(0, 1), (1, 0)])  7.49 us
    unnamed x16, local copies, waits for them, and re-layouts  5.58 us
    gather x1, local copies, waits for them, and re-layouts, shards(): found = item_table.at[wanted].get(mode='promise_in_bounds')  4.29 us
  transfers between devices with their start and end apart: 5, of which 5 were waited for; matrix products, arithmetic and copies ran while one was open for 3% of the time, Pallas kernels for 4%

profile of v10, /device:TPU:1, one launch (start us, length us, event | category | flops | bytes accessed | tf_op | source)
XLA Modules:
  0.0 172.2 jit_solution(1391680415184539980)
XLA Ops:
  7.3 1.7 %shard_map.121 = bf16[160,1024]{1,0:T(8,128)(2,1)} custom-call(bf16[128,2048]{1,0:T(8,128)(2,1)} %mix_ref.1, bf16[64,1024]{1,0:T(8,128)(2,1)} %out_ref.1), custom_call_target="tpu_custom_call" | custom-call | tf_op jit(solution)/shard_map/pallas_call | solution.py:339
  9.1 1.7 %shard_map.120 = (s32[32,128]{1,0:T(8,128)}, s32[128,128]{1,0:T(8,128)}) custom-call(s32[1,128]{1,0:T(1,128)} %bitcast.31, s32[1,128]{1,0:T(1,128)} %bitcast.32), custom_call_target="tpu_custom_call" | custom-call | tf_op jit(solution)/shard_map/pallas_call | solution.py:339
  10.8 15.6 %all_to_all.36 = s32[32,1,128]{2,1,0:T(1,128)S(1)} all-to-all(s32[32,1,128]{2,1,0:T(1,128)} %bitcast.29), channel_id=1, replica_groups=mesh['x'=4,'y'=4,'core'=2,'z'=8] {'x','y','core'}, dimensions={0} | all-to-all | bytes 32768 | tf_op jit(solution)/shard_map/all_to_all | solution.py:353
  26.5 4.3 %gather_fusion = bf16[256,1024]{1,0:T(8,128)(2,1)S(1)} fusion(bf16[2048,1024]{1,0:T(8,128)(2,1)} %param.9, s32[1024]{0:T(1024)S(1)} %pad_clamp_fusion), kind=kCustom, calls=%fused_computation | custom fusion | bytes 1049600 | tf_op jit(solution)/shard_map/gather | solution.py:379
  30.8 15.3 %all_to_all.37 = bf16[32,8,1024]{2,1,0:T(8,128)(2,1)S(1)} all-to-all(bf16[32,8,1024]{2,1,0:T(8,128)(2,1)S(1)} %bitcast.27), channel_id=1, replica_groups=mesh['x'=4,'y'=4,'core'=2,'z'=8] {'x','y','core'}, dimensions={0} | all-to-all | bytes 1048576 | tf_op jit(solution)/shard_map/all_to_all | solution.py:353
  46.1 11.9 %all-gather.3.cloned.1.call-done = bf16[2560,1024]{1,0:T(8,128)(2,1)} async-done(((bf16[160,1024]{1,0:T(8,128)(2,1)}), bf16[2560,1024]{1,0:T(8,128)(2,1)}) %all-gather.3.cloned.1.call-update) | async-done | bytes 5242896 | tf_op jit(solution)/shard_map/all_gather | solution.py:370
  58.1 2.5 %copy-done = bf16[2560,1024]{1,0:T(8,128)(2,1)S(1)} copy-done((bf16[2560,1024]{1,0:T(8,128)(2,1)S(1)}, bf16[2560,1024]{1,0:T(8,128)(2,1)}, u32[]{:S(2)}) %copy-start) | copy-done | bytes 5242904
  60.5 4.1 %shard_map.122 = (bf16[128,1024]{1,0:T(8,128)(2,1)}, bf16[128,3072]{1,0:T(8,128)(2,1)S(1)}, bf16[128,3072]{1,0:T(8,128)(2,1)S(1)}, bf16[2,128,1024]{2,1,0:T(8,12...) custom-call(s32[1,8]{1,0:T(1,128)S(1)} %copy-done.7, bf16[256,1024]{1,0:T(8,128)(2,1)S(1)} %bitcast.19, ...), custom_call_target="tpu_custom_call" | custom-call | bytes 21000000 | tf_op jit(solution)/shard_map/pallas_call | solution.py:339
  65.0 2.0 %collective-permute-done.theirs_ref = bf16[128,3072]{1,0:T(8,128)(2,1)S(1)} collective-permute-done((bf16[128,3072]{1,0:T(8,128)(2,1)S(1)}, bf16[128,3072]{1,0:T(8,128)(2,1)S(1)}, u32[]{:S(2)}, u32[]{:S(2)}) %collective-permute-start) | collective-permute-done | bytes 786464 | tf_op jit(solution)/shard_map/ppermute | solution.py:408
  67.0 1.9 %shard_map.123 = bf16[8,16,16,640]{3,2,1,0:T(8,128)(2,1)} custom-call(bf16[128,3072]{1,0:T(8,128)(2,1)S(1)} %get-tuple-element.19.keep_ref, bf16[128,3072]{1,0:T(8,128)(2,1)S(1)} %collective-permute-done.theirs_ref), custom_call_target="tpu_custom_call" | custom-call | bytes 9000000 | tf_op jit(solution)/shard_map/pallas_call | solution.py:339
  69.1 2.5 %copy-done.1 = bf16[2560,1024]{1,0:T(8,128)(2,1)S(1)} copy-done((bf16[2560,1024]{1,0:T(8,128)(2,1)S(1)}, bf16[2560,1024]{1,0:T(8,128)(2,1)}, u32[]{:S(2)}) %copy-start.1) | copy-done | bytes 5242904
  71.5 1.9 %shard_map.124 = bf16[256,1024]{1,0:T(8,128)(2,1)S(1)} custom-call(s32[128,128]{1,0:T(8,128)S(1)} %copy-done.3, bf16[2,8,160,1024]{3,2,1,0:T(8,128)(2,1)S(1)} %bitcast.18, f32[1,1024]{1,0:T(1,128)S(1)} %bitcast.25, bf16[128,1024]{1,0:T(8,128)(2,1)S(1)} %copy-done.2, bf16[2,128,1024]{2,1,0:T(8,128)(2,1)S(1)} %get-tuple-element.22.dmx, ...), custom_call_target="tpu_custom_call" | custom-call | bytes 9000000 | tf_op jit(solution)/shard_map/pallas_call | solution.py:339
  73.5 18.6 %all_to_all.38 = bf16[32,8,1024]{2,1,0:T(8,128)(2,1)S(1)} all-to-all(bf16[32,8,1024]{2,1,0:T(8,128)(2,1)S(1)} %bitcast.20), channel_id=1, replica_groups=mesh['x'=4,'y'=4,'core'=2,'z'=8] {'x','y','core'}, dimensions={0} | all-to-all | bytes 1048576 | tf_op jit(solution)/shard_map/all_to_all | solution.py:353
  92.0 1.0 shard_map.125
  93.1 14.8 %reduce-scatter.2.cloned.1.call-done = bf16[256,640]{1,0:T(8,128)(2,1)} async-done(((bf16[2048,640]{1,0:T(8,128)(2,1)}), bf16[256,640]{1,0:T(8,128)(2,1)}) %reduce-scatter.2.cloned.1.call-update) | async-done | bytes 327696 | tf_op jit(solution)/shard_map/reduce_scatter | solution.py:422
  107.9 13.8 %all_to_all.39 = bf16[16,16,640]{2,1,0:T(8,128)(2,1)S(1)} all-to-all(bf16[16,16,640]{2,1,0:T(8,128)(2,1)} %bitcast.28), channel_id=1, replica_groups=mesh['x'=4,'y'=4,'core'=2,'z'=8] {'x','y'}, dimensions={0} | all-to-all | bytes 655360 | tf_op jit(solution)/shard_map/all_to_all | solution.py:353
  121.7 10.9 %all_to_all.40.mine_ref = bf16[16,16,640]{2,1,0:T(8,128)(2,1)S(1)} all-to-all(bf16[16,16,640]{2,1,0:T(8,128)(2,1)S(1)} %broadcast_in_dim.2), channel_id=1, replica_groups=mesh['x'=4,'y'=4,'core'=2,'z'=8] {'x','y'}, dimensions={0} | all-to-all | bytes 655360 | tf_op jit(solution)/shard_map/all_to_all | solution.py:353
  132.6 7.5 %collective-permute-start.1 = (bf16[16,16,640]{2,1,0:T(8,128)(2,1)S(1)}, bf16[16,16,640]{2,1,0:T(8,128)(2,1)S(1)}, u32[]{:S(2)}, u32[]{:S(2)}) collective-permute-start(bf16[16,16,640]{2,1,0:T(8,128)(2,1)S(1)} %all_to_all.40.mine_ref), channel_id=1, source_target_pairs={{0,8},{8,0},{1,9},{9,1},{2,10},{10,2},{3,11},{11,3},{4,12},{12,4},... | collective-permute-start | bytes 983048 | tf_op jit(solution)/shard_map/ppermute | solution.py:445
  140.1 1.3 collective-permute-done.1.other_ref
  141.6 16.4 %all_to_all.41.asked_ref.squares_ref = f32[8,40,128]{2,1,0:T(8,128)S(1)} all-to-all(f32[8,40,128]{2,1,0:T(8,128)S(1)} %shard_map.126), channel_id=1, replica_groups=mesh['x'=4,'y'=4,'core'=2,'z'=8] {'z'}, dimensions={0} | all-to-all | bytes 327680 | tf_op jit(solution)/shard_map/all_to_all | solution.py:353
  158.0 0.8 shard_map.127.names_ref
  159.4 1.2 shard_map.128
  160.5 1.0 all-gather.5.cloned.1.call-done.rows_ref
  161.6 4.1 %shard_map.129 = f32[256,1024]{1,0:T(8,128)} custom-call(bf16[1536,1024]{1,0:T(8,128)(2,1)} %all-gather.5.cloned.1.call-done.rows_ref, s32[16,128]{1,0:T(8,128)} %copy-done.4, f32[64,1024]{1,0:T(8,128)} %get-tuple-element.15.after_ref), custom_call_target="tpu_custom_call" | custom-call | bytes 9000000 | tf_op jit(solution)/shard_map/pallas_call | solution.py:339
  (27 shorter events, 1.5 us)
Async XLA Ops:
  7.2 50.9 %copy-start.2 = (bf16[128,1024]{1,0:T(8,128)(2,1)S(1)}, bf16[128,1024]{1,0:T(8,128)(2,1)}, u32[]{:S(2)}) copy-start(bf16[128,1024]{1,0:T(8,128)(2,1)} %ct_ref.3) | copy-start | bytes 786436
  7.2 50.9 %copy-start.6 = (f32[512]{0:T(512)S(1)}, f32[512]{0:T(512)}, u32[]{:S(2)}) copy-start(f32[512]{0:T(512)} %param.16) | copy-start | bytes 6148
  7.2 50.8 %copy-start.5 = (f32[1024]{0:T(1024)S(1)}, f32[1024]{0:T(1024)}, u32[]{:S(2)}) copy-start(f32[1024]{0:T(1024)} %param.15) | copy-start | bytes 12292
  7.2 50.8 %copy-start.7 = (s32[1,8]{1,0:T(1,128)S(1)}, s32[1,8]{1,0:T(1,128)}, u32[]{:S(2)}) copy-start(s32[1,8]{1,0:T(1,128)} %lens_ref.1) | copy-start | bytes 100
  7.2 50.8 %all-gather.3.cloned.1.call-start = ((), (), s32[]{:S(2)}) async-start(), calls=%async_computation.7 | async-start | bytes 5570560 | tf_op jit(solution)/shard_map/all_gather | solution.py:370
  9.0 98.9 %reduce-scatter.2.cloned.1.call-start = ((), (), s32[]{:S(2)}) async-start(), calls=%async_computation.9 | async-start | bytes 2949120 | tf_op jit(solution)/shard_map/reduce_scatter | solution.py:422
  10.8 47.2 %copy-start.3 = (s32[128,128]{1,0:T(8,128)S(1)}, s32[128,128]{1,0:T(8,128)}, u32[]{:S(2)}) copy-start(s32[128,128]{1,0:T(8,128)} %get-tuple-element.17.tgt_ref) | copy-start | bytes 196612
  58.0 2.5 %copy-start = (bf16[2560,1024]{1,0:T(8,128)(2,1)S(1)}, bf16[2560,1024]{1,0:T(8,128)(2,1)}, u32[]{:S(2)}) copy-start(bf16[2560,1024]{1,0:T(8,128)(2,1)} %all-gather.3.cloned.1.call-done) | copy-start | bytes 15728644
  64.7 2.4 %collective-permute-start = (bf16[128,3072]{1,0:T(8,128)(2,1)S(1)}, bf16[128,3072]{1,0:T(8,128)(2,1)S(1)}, u32[]{:S(2)}, u32[]{:S(2)}) collective-permute-start(bf16[128,3072]{1,0:T(8,128)(2,1)S(1)} %get-tuple-element.20), channel_id=1, source_target_pairs={{0,8},{8,0},{1,9},{9,1},{2,10},{10,2},{3,11},{11,3},{4,12},{12,4},... | collective-permute-start | bytes 2359304 | tf_op jit(solution)/shard_map/ppermute | solution.py:408
  69.0 92.6 %all-gather.5.cloned.1.call-start = ((), (), s32[]{:S(2)}) async-start(), calls=%async_computation.8 | async-start | bytes 3538944 | tf_op jit(solution)/shard_map/all_gather | solution.py:441
  69.1 2.5 %copy-start.1 = (bf16[2560,1024]{1,0:T(8,128)(2,1)S(1)}, bf16[2560,1024]{1,0:T(8,128)(2,1)}, u32[]{:S(2)}) copy-start(bf16[2560,1024]{1,0:T(8,128)(2,1)} %all-gather.3.cloned.1.call-done) | copy-start | bytes 15728644
  132.6 8.7 %collective-permute-start.1 = (bf16[16,16,640]{2,1,0:T(8,128)(2,1)S(1)}, bf16[16,16,640]{2,1,0:T(8,128)(2,1)S(1)}, u32[]{:S(2)}, u32[]{:S(2)}) collective-permute-start(bf16[16,16,640]{2,1,0:T(8,128)(2,1)S(1)} %all_to_all.40.mine_ref), channel_id=1, source_target_pairs={{0,8},{8,0},{1,9},{9,1},{2,10},{10,2},{3,11},{11,3},{4,12},{12,4},... | collective-permute-start | bytes 983048 | tf_op jit(solution)/shard_map/ppermute | solution.py:445
  158.8 0.6 copy-start.4
Sparse Core Ops, SparseCore 0:
  10.4 47.5 all-gather.2
  69.1 38.7 reduce-scatter.1
  110.3 51.2 all-gather.4

commit v11 on v10

--- a/solution.py
+++ b/solution.py
@@ -202,18 +202,9 @@
     slots_ref[...] = mm_tn(chosen(tgt_ref), d_emb).astype(BF16)
 
 
-def grads_kernel(keep_ref, theirs_ref, out_ref, buf, sems):
+def grads_kernel(keep_ref, theirs_ref, mix_ref, out_ref, mix, out, sems):
     def both(first, last):
         return jnp.concatenate([keep_ref[:, first:last], theirs_ref[:, first:last]], axis=0)
-
-    grad = mm_tn(both(2048, 2560), both(2560, FACT))
-    for z in range(NZ):
-        for p in range(XY):
-            r, c = z * 64 + (p // 2) * 8, (p % 2) * 256
-            part = grad[r : r + 8, c : c + 256]
-            buf[z, p, :, 512:PCOLS] = jnp.concatenate(
-                [part[:, :128], part[:, 128:]], axis=0
-            ).astype(BF16)
 
     copies = []
     d_mix = both(1024, 2048)
@@ -221,13 +212,32 @@
         grad = mm_tn(both(z * TOK, (z + 1) * TOK), d_mix)
         for p in range(XY):
             part = grad[8 * p : 8 * p + 8]
-            buf[z, p, :, 0:512] = jnp.concatenate(
-                [part[:, :512], part[:, 512:]], axis=0
+            mix[z, p] = jnp.concatenate([part[:, :512], part[:, 512:]], axis=0).astype(BF16)
+        copies.append(pltpu.make_async_copy(mix.at[z], mix_ref.at[z], sems.at[z]))
+        copies[-1].start()
+
+    grad = mm_tn(both(2048, 2560), both(2560, FACT))
+    for z in range(NZ):
+        for p in range(XY):
+            r, c = z * 64 + (p // 2) * 8, (p % 2) * 256
+            part = grad[r : r + 8, c : c + 256]
+            out[p, z * PROWS : (z + 1) * PROWS] = jnp.concatenate(
+                [part[:, :128], part[:, 128:]], axis=0
             ).astype(BF16)
-        copies.append(pltpu.make_async_copy(buf.at[z], out_ref.at[z], sems.at[z]))
-        copies[-1].start()
+    copies.append(pltpu.make_async_copy(out, out_ref, sems.at[NZ]))
+    copies[-1].start()
     for copy in copies:
         copy.wait()
+
+
+def column_kernel(plane_ref, asked_ref, out_ref):
+    total = jnp.sum(plane_ref[...].astype(F32), axis=0).astype(BF16)
+    asked = asked_ref[...]
+    low, high = ((part).astype(F32).astype(BF16) for part in (asked & 127, asked >> 7))
+    for z in range(NZ):
+        out_ref[z, :PROWS] = total[z * PROWS : (z + 1) * PROWS]
+        out_ref[z, PROWS : PROWS + OWNERS] = low
+        out_ref[z, PROWS + OWNERS :] = high
 
 
 def pack_kernel(rows_ref, out_ref):
@@ -236,11 +246,11 @@
     out_ref[...] = mm(take.astype(F32).astype(BF16), rows_ref[...]).astype(BF16)
 
 
-def names_kernel(asked_ref, out_ref):
+def names_kernel(column_ref, out_ref):
     first = lax.axis_index("z") * 256
     count = NZ * USED
-    asked = asked_ref[:, 8:].reshape(NZ * OWNERS, 128).astype(jnp.int32)
-    low, high = (part.astype(F32).astype(BF16) for part in (asked & 127, asked >> 7))
+    low = column_ref[:, PROWS : PROWS + OWNERS].reshape(NZ * OWNERS, 128)
+    high = column_ref[:, PROWS + OWNERS :].reshape(NZ * OWNERS, 128)
     row, col = iota((count, NZ * OWNERS), 0), iota((count, NZ * OWNERS), 1)
     owner = (row // CAP == col).astype(F32).astype(BF16)
     lane = iota((count, 128), 1)
@@ -294,7 +304,7 @@
         copy.wait()
 
 
-def square_kernel(mine_ref, other_ref, asked_ref, out_ref):
+def square_kernel(mine_ref, other_ref, out_ref):
     total = jnp.zeros((PROWS, PCOLS), F32)
     for sums_ref in (mine_ref, other_ref):
         for i in range(XY):
@@ -302,16 +312,12 @@
             total = total + part * part
     mix = jnp.sum(total[:, :512])
     out = jnp.sum(total[:, 512:])
-    lane = iota((8, 128), 1)
-    squares = jnp.where(lane == 0, mix, jnp.where(lane == 1, out, 0.0))
-    asked = asked_ref[...].astype(F32)
-    for z in range(NZ):
-        out_ref[z, :8] = squares
-        out_ref[z, 8:] = asked
+    lane = iota((NZ, 8, 128), 2)
+    out_ref[...] = jnp.where(lane == 0, mix, jnp.where(lane == 1, out, 0.0))
 
 
 def scale_kernel(mine_ref, other_ref, squares_ref, mix_ref, out_ref):
-    total = jnp.sum(squares_ref[:, :8], axis=0)[0:1]
+    total = jnp.sum(squares_ref[...], axis=0)[0:1]
     mix_sq, out_sq = total[:, 0:1], total[:, 1:2]
     mix_scale = jnp.minimum(1.0, 1.0 / jnp.sqrt(mix_sq / float(D * 4 * AW) + 1e-06))
     out_scale = jnp.minimum(1.0, 1.0 / jnp.sqrt(out_sq / float(D * AW) + 1e-06))
@@ -406,21 +412,22 @@
     )
 
     theirs = lax.ppermute(send, "core", [(0, 1), (1, 0)])
-    grads = call(
+    mix_part, out_part = call(
         grads_kernel,
-        [((NZ, XY, PROWS, PCOLS), BF16)],
+        [((NZ, XY, PROWS, 512), BF16), ((XY, NZ * PROWS, 128), BF16)],
         (keep, theirs),
-        outs_specs=anywhere,
+        outs_specs=[anywhere, anywhere],
         scratch_shapes=[
-            pltpu.VMEM((NZ, XY, PROWS, PCOLS), BF16),
-            pltpu.SemaphoreType.DMA((NZ,)),
+            pltpu.VMEM((NZ, XY, PROWS, 512), BF16),
+            pltpu.VMEM((XY, NZ * PROWS, 128), BF16),
+            pltpu.SemaphoreType.DMA((NZ + 1,)),
         ],
         cost_estimate=cost(3),
         compiler_params=pltpu.CompilerParams(vmem_limit_bytes=30 * MB),
     )
-    grads, d_mix = lax.optimization_barrier((grads, d_mix))
-    column = lax.psum_scatter(
-        grads.reshape(NZ * XY * PROWS, PCOLS), "z", scatter_dimension=0, tiled=True
+    mix_part, d_mix = lax.optimization_barrier((mix_part, d_mix))
+    mix_column = lax.psum_scatter(
+        mix_part.reshape(NZ * XY * PROWS, 512), "z", scatter_dimension=0, tiled=True
     )
 
     grad_slots = call(
@@ -438,16 +445,40 @@
         cost_estimate=cost(2),
         compiler_params=pltpu.CompilerParams(vmem_limit_bytes=16 * MB),
     )
+    out_part, packed = lax.optimization_barrier((out_part, packed))
     gathered = lax.all_gather(packed, "z", axis=0, tiled=True)
-    plane = exchange(column.reshape(XY, PROWS, PCOLS), ("x", "y"))
-    whole = jnp.sum(plane.astype(F32), axis=0).astype(BF16)
+
+    out_column = call(
+        column_kernel,
+        [((NZ, PROWS + 2 * OWNERS, 128), BF16)],
+        (exchange(out_part, ("x", "y")), asked),
+        cost_estimate=cost(1),
+        compiler_params=pltpu.CompilerParams(vmem_limit_bytes=16 * MB),
+    )
+    out_column = exchange(out_column, "z")
+    mix_column, out_column = lax.optimization_barrier((mix_column, out_column))
+    names = call(
+        names_kernel,
+        [((PROWS, 128), jnp.int32)],
+        (out_column,),
+        cost_estimate=cost(2),
+        compiler_params=pltpu.CompilerParams(vmem_limit_bytes=16 * MB),
+    )
+    mix_plane = exchange(mix_column.reshape(XY, PROWS, 512), ("x", "y"))
+    whole = jnp.concatenate(
+        [
+            jnp.sum(mix_plane.astype(F32), axis=0),
+            jnp.sum(out_column[:, :PROWS].astype(F32), axis=0),
+        ],
+        axis=1,
+    ).astype(BF16)
     mine = exchange(jnp.broadcast_to(whole[None], (XY, PROWS, PCOLS)), ("x", "y"))
     other = lax.ppermute(mine, "core", [(0, 1), (1, 0)])
 
     squares = call(
         square_kernel,
-        [((NZ, 8 + OWNERS, 128), F32)],
-        (mine, other, asked),
+        [((NZ, 8, 128), F32)],
+        (mine, other),
         cost_estimate=cost(1),
         compiler_params=pltpu.CompilerParams(vmem_limit_bytes=16 * MB),
     )
@@ -457,13 +488,6 @@
         [((TOK, 4 * AW), F32), ((64, D), F32)],
         (mine, other, squares),
         cost_estimate=cost(2),
-        compiler_params=pltpu.CompilerParams(vmem_limit_bytes=16 * MB),
-    )
-    names = call(
-        names_kernel,
-        [((PROWS, 128), jnp.int32)],
-        (squares,),
-        cost_estimate=cost(1),
         compiler_params=pltpu.CompilerParams(vmem_limit_bytes=16 * MB),
     )
     table_grad = call(

time: 173 us -> 171 us (0.988)
  starting transfers between devices: 7.96 us -> 12.9 us
  blocking collectives: 90.6 us -> 86.1 us
  waiting for transfers between devices: 31 us -> 28 us
    reduce_scatter x1, waiting for transfers between devices: 14.8 us -> 0.01 us  [shards(): lax.psum_scatter(mix_part.reshape(NZ * XY * PROWS, 512), 'z', scatter_dim...]
    all_to_all x0 -> x2, waiting for transfers between devices: none -> 12.8 us  [exchange(): return lax.all_to_all(array, axes, split_axis=0, concat_axis=0, tiled=True)]
    all_to_all x0 -> x2, starting transfers between devices: none -> 7.35 us  [exchange(): return lax.all_to_all(array, axes, split_axis=0, concat_axis=0, tiled=True)]
    all_to_all x6, blocking collectives: 90.6 us -> 86.1 us  [exchange(): return lax.all_to_all(array, axes, split_axis=0, concat_axis=0, tiled=True)]
    ppermute x1, starting transfers between devices: 7.49 us -> 5.12 us  [shards(): other = lax.ppermute(mine, 'core', [(0, 1), (1, 0)])]
    pallas_call x10 -> x11, Pallas kernels: 18.7 us -> 19.2 us  [call(): pl.pallas_call(body, out_shape=shapes[0] if one else shapes, in_specs=spe...]
  transfers between devices with their start and end apart: 5 -> 7, of which waited for: 5 -> 5; matrix products, arithmetic and copies ran while one was open for 3% -> 3% of each run, Pallas kernels for 4% -> 4%
where the time goes in v11:
time: 171 us; the launch traced here: 170 us
  blocking collectives  86.1 us (50%)
  waiting for transfers between devices  28 us (16%)
  Pallas kernels  19.2 us (11%)
  between operations  13.9 us (8%)
  starting transfers between devices  12.9 us (8%)
  local copies, waits for them, and re-layouts  9.98 us (6%)
    all_to_all x6, blocking collectives, exchange(): return lax.all_to_all(array, axes, split_axis=0, concat_axis=0, tiled=True)  86.1 us
    pallas_call x11, Pallas kernels, call(): pl.pallas_call(body, out_shape=shapes[0] if one else shapes, in_specs=spe...  19.2 us
    all_to_all x2, waiting for transfers between devices, exchange(): return lax.all_to_all(array, axes, split_axis=0, concat_axis=0, tiled=True)  12.8 us
    all_gather x1, waiting for transfers between devices, shards(): lax.all_gather(share, ('core', 'z'), axis=0, tiled=True)  11.9 us
    all_to_all x2, starting transfers between devices, exchange(): return lax.all_to_all(array, axes, split_axis=0, concat_axis=0, tiled=True)  7.35 us
    unnamed x16, local copies, waits for them, and re-layouts  5.58 us
    ppermute x1, starting transfers between devices, shards(): other = lax.ppermute(mine, 'core', [(0, 1), (1, 0)])  5.12 us
    gather x1, local copies, waits for them, and re-layouts, shards(): found = item_table.at[wanted].get(mode='promise_in_bounds')  4.29 us
  transfers between devices with their start and end apart: 7, of which 5 were waited for; matrix products, arithmetic and copies ran while one was open for 3% of the time, Pallas kernels for 4%

profile of v11, /device:TPU:1, one launch (start us, length us, event | category | flops | bytes accessed | tf_op | source)
XLA Modules:
  0.0 170.2 jit_solution(5719670506339095394)
XLA Ops:
  7.3 1.7 %shard_map.121 = bf16[160,1024]{1,0:T(8,128)(2,1)} custom-call(bf16[128,2048]{1,0:T(8,128)(2,1)} %mix_ref.1, bf16[64,1024]{1,0:T(8,128)(2,1)} %out_ref.1), custom_call_target="tpu_custom_call" | custom-call | tf_op jit(solution)/shard_map/pallas_call | solution.py:345
  9.1 1.7 %shard_map.120 = (s32[32,128]{1,0:T(8,128)}, s32[128,128]{1,0:T(8,128)}) custom-call(s32[1,128]{1,0:T(1,128)} %bitcast.31, s32[1,128]{1,0:T(1,128)} %bitcast.32), custom_call_target="tpu_custom_call" | custom-call | tf_op jit(solution)/shard_map/pallas_call | solution.py:345
  10.8 15.6 %all_to_all.46 = s32[32,1,128]{2,1,0:T(1,128)S(1)} all-to-all(s32[32,1,128]{2,1,0:T(1,128)} %bitcast.29), channel_id=1, replica_groups=mesh['x'=4,'y'=4,'core'=2,'z'=8] {'x','y','core'}, dimensions={0} | all-to-all | bytes 32768 | tf_op jit(solution)/shard_map/all_to_all | solution.py:359
  26.5 4.3 %gather_fusion = bf16[256,1024]{1,0:T(8,128)(2,1)S(1)} fusion(bf16[2048,1024]{1,0:T(8,128)(2,1)} %param.9, s32[1024]{0:T(1024)S(1)} %pad_clamp_fusion), kind=kCustom, calls=%fused_computation | custom fusion | bytes 1049600 | tf_op jit(solution)/shard_map/gather | solution.py:385
  30.8 15.3 %all_to_all.47 = bf16[32,8,1024]{2,1,0:T(8,128)(2,1)S(1)} all-to-all(bf16[32,8,1024]{2,1,0:T(8,128)(2,1)S(1)} %bitcast.27), channel_id=1, replica_groups=mesh['x'=4,'y'=4,'core'=2,'z'=8] {'x','y','core'}, dimensions={0} | all-to-all | bytes 1048576 | tf_op jit(solution)/shard_map/all_to_all | solution.py:359
  46.1 11.9 %all-gather.3.cloned.1.call-done = bf16[2560,1024]{1,0:T(8,128)(2,1)} async-done(((bf16[160,1024]{1,0:T(8,128)(2,1)}), bf16[2560,1024]{1,0:T(8,128)(2,1)}) %all-gather.3.cloned.1.call-update) | async-done | bytes 5242896 | tf_op jit(solution)/shard_map/all_gather | solution.py:376
  58.1 2.5 %copy-done = bf16[2560,1024]{1,0:T(8,128)(2,1)S(1)} copy-done((bf16[2560,1024]{1,0:T(8,128)(2,1)S(1)}, bf16[2560,1024]{1,0:T(8,128)(2,1)}, u32[]{:S(2)}) %copy-start) | copy-done | bytes 5242904
  60.5 4.1 %shard_map.122 = (bf16[128,1024]{1,0:T(8,128)(2,1)}, bf16[128,3072]{1,0:T(8,128)(2,1)S(1)}, bf16[128,3072]{1,0:T(8,128)(2,1)S(1)}, bf16[2,128,1024]{2,1,0:T(8,12...) custom-call(s32[1,8]{1,0:T(1,128)S(1)} %copy-done.7, bf16[256,1024]{1,0:T(8,128)(2,1)S(1)} %bitcast.19, ...), custom_call_target="tpu_custom_call" | custom-call | bytes 21000000 | tf_op jit(solution)/shard_map/pallas_call | solution.py:345
  65.0 2.0 %collective-permute-done.theirs_ref = bf16[128,3072]{1,0:T(8,128)(2,1)S(1)} collective-permute-done((bf16[128,3072]{1,0:T(8,128)(2,1)S(1)}, bf16[128,3072]{1,0:T(8,128)(2,1)S(1)}, u32[]{:S(2)}, u32[]{:S(2)}) %collective-permute-start) | collective-permute-done | bytes 786464 | tf_op jit(solution)/shard_map/ppermute | solution.py:414
  67.0 1.7 %shard_map.123 = (bf16[8,16,16,512]{3,2,1,0:T(8,128)(2,1)}, bf16[16,128,128]{2,1,0:T(8,128)(2,1)S(1)}) custom-call(bf16[128,3072]{1,0:T(8,128)(2,1)S(1)} %get-tuple-element.25.keep_ref, bf16[128,3072]{1,0:T(8,128)(2,1)S(1)} %collective-permute-done.theirs_ref), custom_call_target="tpu_custom_call" | custom-call | bytes 9000000 | tf_op jit(solution)/shard_map/pallas_call | solution.py:345
  68.8 2.5 %copy-done.1 = bf16[2560,1024]{1,0:T(8,128)(2,1)S(1)} copy-done((bf16[2560,1024]{1,0:T(8,128)(2,1)S(1)}, bf16[2560,1024]{1,0:T(8,128)(2,1)}, u32[]{:S(2)}) %copy-start.1) | copy-done | bytes 5242904
  71.3 1.9 %shard_map.124 = bf16[256,1024]{1,0:T(8,128)(2,1)S(1)} custom-call(s32[128,128]{1,0:T(8,128)S(1)} %copy-done.3, bf16[2,8,160,1024]{3,2,1,0:T(8,128)(2,1)S(1)} %bitcast.18, f32[1,1024]{1,0:T(1,128)S(1)} %bitcast.25, bf16[128,1024]{1,0:T(8,128)(2,1)S(1)} %copy-done.2, bf16[2,128,1024]{2,1,0:T(8,128)(2,1)S(1)} %get-tuple-element.30.dmx, ...), custom_call_target="tpu_custom_call" | custom-call | bytes 9000000 | tf_op jit(solution)/shard_map/pallas_call | solution.py:345
  73.2 18.5 %all_to_all.48 = bf16[32,8,1024]{2,1,0:T(8,128)(2,1)S(1)} all-to-all(bf16[32,8,1024]{2,1,0:T(8,128)(2,1)S(1)} %bitcast.20), channel_id=1, replica_groups=mesh['x'=4,'y'=4,'core'=2,'z'=8] {'x','y','core'}, dimensions={0} | all-to-all | bytes 1048576 | tf_op jit(solution)/shard_map/all_to_all | solution.py:359
  92.8 13.2 %all_to_all.49.plane_ref = bf16[16,128,128]{2,1,0:T(8,128)(2,1)S(1)} all-to-all(bf16[16,128,128]{2,1,0:T(8,128)(2,1)S(1)} %get-tuple-element.35), channel_id=1, replica_groups=mesh['x'=4,'y'=4,'core'=2,'z'=8] {'x','y'}, dimensions={0} | all-to-all | bytes 1048576 | tf_op jit(solution)/shard_map/all_to_all | solution.py:359
  106.1 12.3 %all_to_all.50.column_ref = bf16[8,80,128]{2,1,0:T(8,128)(2,1)S(1)} all-to-all(bf16[8,80,128]{2,1,0:T(8,128)(2,1)S(1)} %shard_map.126), channel_id=1, replica_groups=mesh['x'=4,'y'=4,'core'=2,'z'=8] {'z'}, dimensions={0} | all-to-all | bytes 327680 | tf_op jit(solution)/shard_map/all_to_all | solution.py:359
  118.3 4.0 %all-to-all-start.5 = ((bf16[16,16,512]{2,1,0:T(8,128)(2,1)}), bf16[16,16,512]{2,1,0:T(8,128)(2,1)S(1)}, u32[]{:S(2)}, u32[]{:S(2)}) async-start(bf16[16,16,512]{2,1,0:T(8,128)(2,1)} %bitcast.28), calls=%async_computation.6 | async-start | bytes 524288 | tf_op jit(solution)/shard_map/all_to_all | solution.py:359
  122.4 7.3 %all-to-all-done.5 = bf16[16,16,512]{2,1,0:T(8,128)(2,1)S(1)} async-done(((bf16[16,16,512]{2,1,0:T(8,128)(2,1)}), bf16[16,16,512]{2,1,0:T(8,128)(2,1)S(1)}, u32[]{:S(2)}, u32[]{:S(2)}) %all-to-all-start.5) | async-done | bytes 262176 | tf_op jit(solution)/shard_map/all_to_all | solution.py:359
  129.8 11.2 %all_to_all.51.mine_ref = bf16[16,16,640]{2,1,0:T(8,128)(2,1)S(1)} all-to-all(bf16[16,16,640]{2,1,0:T(8,128)(2,1)S(1)} %broadcast_in_dim.2), channel_id=1, replica_groups=mesh['x'=4,'y'=4,'core'=2,'z'=8] {'x','y'}, dimensions={0} | all-to-all | bytes 655360 | tf_op jit(solution)/shard_map/all_to_all | solution.py:359
  141.0 5.1 %collective-permute-start.1 = (bf16[16,16,640]{2,1,0:T(8,128)(2,1)S(1)}, bf16[16,16,640]{2,1,0:T(8,128)(2,1)S(1)}, u32[]{:S(2)}, u32[]{:S(2)}) collective-permute-start(bf16[16,16,640]{2,1,0:T(8,128)(2,1)S(1)} %all_to_all.51.mine_ref), channel_id=1, source_target_pairs={{0,8},{8,0},{1,9},{9,1},{2,10},{10,2},{3,11},{11,3},{4,12},{12,4},... | collective-permute-start | bytes 983048 | tf_op jit(solution)/shard_map/ppermute | solution.py:476
  146.2 1.3 collective-permute-done.1.other_ref
  148.2 3.3 %all-to-all-start.7 = ((f32[8,8,128]{2,1,0:T(8,128)}), f32[8,8,128]{2,1,0:T(8,128)S(1)}, u32[]{:S(2)}, u32[]{:S(2)}) async-start(f32[8,8,128]{2,1,0:T(8,128)} %shard_map.128), calls=%async_computation.8 | async-start | bytes 65536 | tf_op jit(solution)/shard_map/all_to_all | solution.py:359
  152.9 5.4 %all-to-all-done.7.squares_ref = f32[8,8,128]{2,1,0:T(8,128)S(1)} async-done(((f32[8,8,128]{2,1,0:T(8,128)}), f32[8,8,128]{2,1,0:T(8,128)S(1)}, u32[]{:S(2)}, u32[]{:S(2)}) %all-to-all-start.7) | async-done | bytes 32800 | tf_op jit(solution)/shard_map/all_to_all | solution.py:359
  158.4 1.2 shard_map.129
  159.5 4.1 %shard_map.130 = f32[256,1024]{1,0:T(8,128)} custom-call(bf16[1536,1024]{1,0:T(8,128)(2,1)} %all-gather.5.cloned.1.call-done.rows_ref, s32[16,128]{1,0:T(8,128)} %copy-done.4, f32[64,1024]{1,0:T(8,128)} %get-tuple-element.21.after_ref), custom_call_target="tpu_custom_call" | custom-call | bytes 9000000 | tf_op jit(solution)/shard_map/pallas_call | solution.py:345
  (34 shorter events, 4.0 us)
Async XLA Ops:
  7.2 50.9 %copy-start.2 = (bf16[128,1024]{1,0:T(8,128)(2,1)S(1)}, bf16[128,1024]{1,0:T(8,128)(2,1)}, u32[]{:S(2)}) copy-start(bf16[128,1024]{1,0:T(8,128)(2,1)} %ct_ref.3) | copy-start | bytes 786436
  7.2 50.9 %copy-start.6 = (f32[512]{0:T(512)S(1)}, f32[512]{0:T(512)}, u32[]{:S(2)}) copy-start(f32[512]{0:T(512)} %param.16) | copy-start | bytes 6148
  7.2 50.8 %copy-start.5 = (f32[1024]{0:T(1024)S(1)}, f32[1024]{0:T(1024)}, u32[]{:S(2)}) copy-start(f32[1024]{0:T(1024)} %param.15) | copy-start | bytes 12292
  7.2 50.8 %copy-start.7 = (s32[1,8]{1,0:T(1,128)S(1)}, s32[1,8]{1,0:T(1,128)}, u32[]{:S(2)}) copy-start(s32[1,8]{1,0:T(1,128)} %lens_ref.1) | copy-start | bytes 100
  7.2 50.8 %all-gather.3.cloned.1.call-start = ((), (), s32[]{:S(2)}) async-start(), calls=%async_computation.9 | async-start | bytes 5570560 | tf_op jit(solution)/shard_map/all_gather | solution.py:376
  9.0 109.3 %reduce-scatter.2.cloned.1.call-start = ((), (), s32[]{:S(2)}) async-start(), calls=%async_computation.11 | async-start | bytes 2359296 | tf_op jit(solution)/shard_map/reduce_scatter | solution.py:429
  10.8 47.2 %copy-start.3 = (s32[128,128]{1,0:T(8,128)S(1)}, s32[128,128]{1,0:T(8,128)}, u32[]{:S(2)}) copy-start(s32[128,128]{1,0:T(8,128)} %get-tuple-element.23.tgt_ref) | copy-start | bytes 196612
  58.0 2.5 %copy-start = (bf16[2560,1024]{1,0:T(8,128)(2,1)S(1)}, bf16[2560,1024]{1,0:T(8,128)(2,1)}, u32[]{:S(2)}) copy-start(bf16[2560,1024]{1,0:T(8,128)(2,1)} %all-gather.3.cloned.1.call-done) | copy-start | bytes 15728644
  64.7 2.4 %collective-permute-start = (bf16[128,3072]{1,0:T(8,128)(2,1)S(1)}, bf16[128,3072]{1,0:T(8,128)(2,1)S(1)}, u32[]{:S(2)}, u32[]{:S(2)}) collective-permute-start(bf16[128,3072]{1,0:T(8,128)(2,1)S(1)} %get-tuple-element.26), channel_id=1, source_target_pairs={{0,8},{8,0},{1,9},{9,1},{2,10},{10,2},{3,11},{11,3},{4,12},{12,4},... | collective-permute-start | bytes 2359304 | tf_op jit(solution)/shard_map/ppermute | solution.py:414
  68.8 90.8 %all-gather.5.cloned.1.call-start = ((), (), s32[]{:S(2)}) async-start(), calls=%async_computation.10 | async-start | bytes 3538944 | tf_op jit(solution)/shard_map/all_gather | solution.py:449
  68.8 2.5 %copy-start.1 = (bf16[2560,1024]{1,0:T(8,128)(2,1)S(1)}, bf16[2560,1024]{1,0:T(8,128)(2,1)}, u32[]{:S(2)}) copy-start(bf16[2560,1024]{1,0:T(8,128)(2,1)} %all-gather.3.cloned.1.call-done) | copy-start | bytes 15728644
  118.3 11.4 %all-to-all-start.5 = ((bf16[16,16,512]{2,1,0:T(8,128)(2,1)}), bf16[16,16,512]{2,1,0:T(8,128)(2,1)S(1)}, u32[]{:S(2)}, u32[]{:S(2)}) async-start(bf16[16,16,512]{2,1,0:T(8,128)(2,1)} %bitcast.28), calls=%async_computation.6 | async-start | bytes 524288 | tf_op jit(solution)/shard_map/all_to_all | solution.py:359
  141.0 6.4 %collective-permute-start.1 = (bf16[16,16,640]{2,1,0:T(8,128)(2,1)S(1)}, bf16[16,16,640]{2,1,0:T(8,128)(2,1)S(1)}, u32[]{:S(2)}, u32[]{:S(2)}) collective-permute-start(bf16[16,16,640]{2,1,0:T(8,128)(2,1)S(1)} %all_to_all.51.mine_ref), channel_id=1, source_target_pairs={{0,8},{8,0},{1,9},{9,1},{2,10},{10,2},{3,11},{11,3},{4,12},{12,4},... | collective-permute-start | bytes 983048 | tf_op jit(solution)/shard_map/ppermute | solution.py:476
  148.2 10.1 %all-to-all-start.7 = ((f32[8,8,128]{2,1,0:T(8,128)}), f32[8,8,128]{2,1,0:T(8,128)S(1)}, u32[]{:S(2)}, u32[]{:S(2)}) async-start(f32[8,8,128]{2,1,0:T(8,128)} %shard_map.128), calls=%async_computation.8 | async-start | bytes 65536 | tf_op jit(solution)/shard_map/all_to_all | solution.py:359
  152.3 0.6 copy-start.4
Sparse Core Ops, SparseCore 0:
  10.4 47.5 all-gather.2
  68.9 36.2 reduce-scatter.1
  107.5 47.6 all-gather.4

commit v12 on v11

--- a/solution.py
+++ b/solution.py
@@ -266,7 +266,7 @@
     out_ref[...] = names.T[:PROWS].astype(jnp.int32) - first
 
 
-def table_kernel(rows_ref, names_ref, after_ref, out_ref, buf, total, sems):
+def table_kernel(rows_ref, names_ref, out_ref, buf, total, sems):
     half = NZ * USED // 2
     copies = [
         pltpu.make_async_copy(
@@ -483,18 +483,11 @@
         compiler_params=pltpu.CompilerParams(vmem_limit_bytes=16 * MB),
     )
     squares = exchange(squares, "z")
-    mix_grad, out_grad = call(
-        scale_kernel,
-        [((TOK, 4 * AW), F32), ((64, D), F32)],
-        (mine, other, squares),
-        cost_estimate=cost(2),
-        compiler_params=pltpu.CompilerParams(vmem_limit_bytes=16 * MB),
-    )
     table_grad = call(
         table_kernel,
         [((256, D), F32)],
-        (gathered, names, out_grad),
-        specs=[pinned, vmem(), anywhere],
+        (gathered, names),
+        specs=[pinned, vmem()],
         outs_specs=anywhere,
         scratch_shapes=[
             pltpu.VMEM((2, NZ * USED // 2, D), BF16),
@@ -503,6 +496,14 @@
         ],
         cost_estimate=cost(3),
         compiler_params=pltpu.CompilerParams(vmem_limit_bytes=60 * MB),
+    )
+    squares, table_grad = lax.optimization_barrier((squares, table_grad))
+    mix_grad, out_grad = call(
+        scale_kernel,
+        [((TOK, 4 * AW), F32), ((64, D), F32)],
+        (mine, other, squares),
+        cost_estimate=cost(2),
+        compiler_params=pltpu.CompilerParams(vmem_limit_bytes=16 * MB),
     )
     return (layer_out, table_grad, mix_grad, out_grad)
 

time: 171 us -> 168 us (0.982)
  waiting for transfers between devices: 28 us -> 24.8 us
    all_to_all x2, waiting for transfers between devices: 12.8 us -> 7.33 us  [exchange(): return lax.all_to_all(array, axes, split_axis=0, concat_axis=0, tiled=True)]
    all_gather x1, waiting for transfers between devices: 0.01 us -> 2.3 us  [shards(): gathered = lax.all_gather(packed, 'z', axis=0, tiled=True)]
  transfers between devices with their start and end apart: 7 -> 7, of which waited for: 5 -> 5; matrix products, arithmetic and copies ran while one was open for 3% -> 3% of each run, Pallas kernels for 4% -> 6%
where the time goes in v12:
time: 168 us; the launch traced here: 167 us
  blocking collectives  86.1 us (51%)
  waiting for transfers between devices  24.8 us (15%)
  Pallas kernels  19.2 us (11%)
  between operations  13.9 us (8%)
  starting transfers between devices  12.9 us (8%)
  local copies, waits for them, and re-layouts  9.98 us (6%)
    all_to_all x6, blocking collectives, exchange(): return lax.all_to_all(array, axes, split_axis=0, concat_axis=0, tiled=True)  86.1 us
    pallas_call x11, Pallas kernels, call(): pl.pallas_call(body, out_shape=shapes[0] if one else shapes, in_specs=spe...  19.2 us
    all_gather x1, waiting for transfers between devices, shards(): lax.all_gather(share, ('core', 'z'), axis=0, tiled=True)  11.9 us
    all_to_all x2, starting transfers between devices, exchange(): return lax.all_to_all(array, axes, split_axis=0, concat_axis=0, tiled=True)  7.35 us
    all_to_all x2, waiting for transfers between devices, exchange(): return lax.all_to_all(array, axes, split_axis=0, concat_axis=0, tiled=True)  7.33 us
    unnamed x16, local copies, waits for them, and re-layouts  5.58 us
    ppermute x1, starting transfers between devices, shards(): other = lax.ppermute(mine, 'core', [(0, 1), (1, 0)])  5.12 us
    gather x1, local copies, waits for them, and re-layouts, shards(): found = item_table.at[wanted].get(mode='promise_in_bounds')  4.29 us
  transfers between devices with their start and end apart: 7, of which 5 were waited for; matrix products, arithmetic and copies ran while one was open for 3% of the time, Pallas kernels for 6%

profile of v12, /device:TPU:1, one launch (start us, length us, event | category | flops | bytes accessed | tf_op | source)
XLA Modules:
  0.0 167.1 jit_solution(9582481259490046589)
XLA Ops:
  7.3 1.7 %shard_map.121 = bf16[160,1024]{1,0:T(8,128)(2,1)} custom-call(bf16[128,2048]{1,0:T(8,128)(2,1)} %mix_ref.1, bf16[64,1024]{1,0:T(8,128)(2,1)} %out_ref.1), custom_call_target="tpu_custom_call" | custom-call | tf_op jit(solution)/shard_map/pallas_call | solution.py:345
  9.1 1.7 %shard_map.120 = (s32[32,128]{1,0:T(8,128)}, s32[128,128]{1,0:T(8,128)}) custom-call(s32[1,128]{1,0:T(1,128)} %bitcast.31, s32[1,128]{1,0:T(1,128)} %bitcast.32), custom_call_target="tpu_custom_call" | custom-call | tf_op jit(solution)/shard_map/pallas_call | solution.py:345
  10.8 15.6 %all_to_all.46 = s32[32,1,128]{2,1,0:T(1,128)S(1)} all-to-all(s32[32,1,128]{2,1,0:T(1,128)} %bitcast.29), channel_id=1, replica_groups=mesh['x'=4,'y'=4,'core'=2,'z'=8] {'x','y','core'}, dimensions={0} | all-to-all | bytes 32768 | tf_op jit(solution)/shard_map/all_to_all | solution.py:359
  26.5 4.3 %gather_fusion = bf16[256,1024]{1,0:T(8,128)(2,1)S(1)} fusion(bf16[2048,1024]{1,0:T(8,128)(2,1)} %param.9, s32[1024]{0:T(1024)S(1)} %pad_clamp_fusion), kind=kCustom, calls=%fused_computation | custom fusion | bytes 1049600 | tf_op jit(solution)/shard_map/gather | solution.py:385
  30.8 15.3 %all_to_all.47 = bf16[32,8,1024]{2,1,0:T(8,128)(2,1)S(1)} all-to-all(bf16[32,8,1024]{2,1,0:T(8,128)(2,1)S(1)} %bitcast.27), channel_id=1, replica_groups=mesh['x'=4,'y'=4,'core'=2,'z'=8] {'x','y','core'}, dimensions={0} | all-to-all | bytes 1048576 | tf_op jit(solution)/shard_map/all_to_all | solution.py:359
  46.1 11.9 %all-gather.3.cloned.1.call-done = bf16[2560,1024]{1,0:T(8,128)(2,1)} async-done(((bf16[160,1024]{1,0:T(8,128)(2,1)}), bf16[2560,1024]{1,0:T(8,128)(2,1)}) %all-gather.3.cloned.1.call-update) | async-done | bytes 5242896 | tf_op jit(solution)/shard_map/all_gather | solution.py:376
  58.1 2.5 %copy-done = bf16[2560,1024]{1,0:T(8,128)(2,1)S(1)} copy-done((bf16[2560,1024]{1,0:T(8,128)(2,1)S(1)}, bf16[2560,1024]{1,0:T(8,128)(2,1)}, u32[]{:S(2)}) %copy-start) | copy-done | bytes 5242904
  60.5 4.1 %shard_map.122 = (bf16[128,1024]{1,0:T(8,128)(2,1)}, bf16[128,3072]{1,0:T(8,128)(2,1)S(1)}, bf16[128,3072]{1,0:T(8,128)(2,1)S(1)}, bf16[2,128,1024]{2,1,0:T(8,12...) custom-call(s32[1,8]{1,0:T(1,128)S(1)} %copy-done.7, bf16[256,1024]{1,0:T(8,128)(2,1)S(1)} %bitcast.19, ...), custom_call_target="tpu_custom_call" | custom-call | bytes 21000000 | tf_op jit(solution)/shard_map/pallas_call | solution.py:345
  65.0 2.0 %collective-permute-done.theirs_ref = bf16[128,3072]{1,0:T(8,128)(2,1)S(1)} collective-permute-done((bf16[128,3072]{1,0:T(8,128)(2,1)S(1)}, bf16[128,3072]{1,0:T(8,128)(2,1)S(1)}, u32[]{:S(2)}, u32[]{:S(2)}) %collective-permute-start) | collective-permute-done | bytes 786464 | tf_op jit(solution)/shard_map/ppermute | solution.py:414
  67.0 1.7 %shard_map.123 = (bf16[8,16,16,512]{3,2,1,0:T(8,128)(2,1)}, bf16[16,128,128]{2,1,0:T(8,128)(2,1)S(1)}) custom-call(bf16[128,3072]{1,0:T(8,128)(2,1)S(1)} %get-tuple-element.27.keep_ref, bf16[128,3072]{1,0:T(8,128)(2,1)S(1)} %collective-permute-done.theirs_ref), custom_call_target="tpu_custom_call" | custom-call | bytes 9000000 | tf_op jit(solution)/shard_map/pallas_call | solution.py:345
  68.8 2.5 %copy-done.1 = bf16[2560,1024]{1,0:T(8,128)(2,1)S(1)} copy-done((bf16[2560,1024]{1,0:T(8,128)(2,1)S(1)}, bf16[2560,1024]{1,0:T(8,128)(2,1)}, u32[]{:S(2)}) %copy-start.1) | copy-done | bytes 5242904
  71.3 1.9 %shard_map.124 = bf16[256,1024]{1,0:T(8,128)(2,1)S(1)} custom-call(s32[128,128]{1,0:T(8,128)S(1)} %copy-done.3, bf16[2,8,160,1024]{3,2,1,0:T(8,128)(2,1)S(1)} %bitcast.18, f32[1,1024]{1,0:T(1,128)S(1)} %bitcast.25, bf16[128,1024]{1,0:T(8,128)(2,1)S(1)} %copy-done.2, bf16[2,128,1024]{2,1,0:T(8,128)(2,1)S(1)} %get-tuple-element.33.dmx, ...), custom_call_target="tpu_custom_call" | custom-call | bytes 9000000 | tf_op jit(solution)/shard_map/pallas_call | solution.py:345
  73.2 18.5 %all_to_all.48 = bf16[32,8,1024]{2,1,0:T(8,128)(2,1)S(1)} all-to-all(bf16[32,8,1024]{2,1,0:T(8,128)(2,1)S(1)} %bitcast.20), channel_id=1, replica_groups=mesh['x'=4,'y'=4,'core'=2,'z'=8] {'x','y','core'}, dimensions={0} | all-to-all | bytes 1048576 | tf_op jit(solution)/shard_map/all_to_all | solution.py:359
  92.8 13.2 %all_to_all.49.plane_ref = bf16[16,128,128]{2,1,0:T(8,128)(2,1)S(1)} all-to-all(bf16[16,128,128]{2,1,0:T(8,128)(2,1)S(1)} %get-tuple-element.36), channel_id=1, replica_groups=mesh['x'=4,'y'=4,'core'=2,'z'=8] {'x','y'}, dimensions={0} | all-to-all | bytes 1048576 | tf_op jit(solution)/shard_map/all_to_all | solution.py:359
  106.1 12.3 %all_to_all.50.column_ref = bf16[8,80,128]{2,1,0:T(8,128)(2,1)S(1)} all-to-all(bf16[8,80,128]{2,1,0:T(8,128)(2,1)S(1)} %shard_map.126), channel_id=1, replica_groups=mesh['x'=4,'y'=4,'core'=2,'z'=8] {'z'}, dimensions={0} | all-to-all | bytes 327680 | tf_op jit(solution)/shard_map/all_to_all | solution.py:359
  118.3 4.0 %all-to-all-start.5 = ((bf16[16,16,512]{2,1,0:T(8,128)(2,1)}), bf16[16,16,512]{2,1,0:T(8,128)(2,1)S(1)}, u32[]{:S(2)}, u32[]{:S(2)}) async-start(bf16[16,16,512]{2,1,0:T(8,128)(2,1)} %bitcast.28), calls=%async_computation.6 | async-start | bytes 524288 | tf_op jit(solution)/shard_map/all_to_all | solution.py:359
  122.4 7.3 %all-to-all-done.5 = bf16[16,16,512]{2,1,0:T(8,128)(2,1)S(1)} async-done(((bf16[16,16,512]{2,1,0:T(8,128)(2,1)}), bf16[16,16,512]{2,1,0:T(8,128)(2,1)S(1)}, u32[]{:S(2)}, u32[]{:S(2)}) %all-to-all-start.5) | async-done | bytes 262176 | tf_op jit(solution)/shard_map/all_to_all | solution.py:359
  129.8 11.2 %all_to_all.51.mine_ref = bf16[16,16,640]{2,1,0:T(8,128)(2,1)S(1)} all-to-all(bf16[16,16,640]{2,1,0:T(8,128)(2,1)S(1)} %broadcast_in_dim.2), channel_id=1, replica_groups=mesh['x'=4,'y'=4,'core'=2,'z'=8] {'x','y'}, dimensions={0} | all-to-all | bytes 655360 | tf_op jit(solution)/shard_map/all_to_all | solution.py:359
  141.0 5.1 %collective-permute-start.1 = (bf16[16,16,640]{2,1,0:T(8,128)(2,1)S(1)}, bf16[16,16,640]{2,1,0:T(8,128)(2,1)S(1)}, u32[]{:S(2)}, u32[]{:S(2)}) collective-permute-start(bf16[16,16,640]{2,1,0:T(8,128)(2,1)S(1)} %all_to_all.51.mine_ref), channel_id=1, source_target_pairs={{0,8},{8,0},{1,9},{9,1},{2,10},{10,2},{3,11},{11,3},{4,12},{12,4},... | collective-permute-start | bytes 983048 | tf_op jit(solution)/shard_map/ppermute | solution.py:476
  146.2 1.3 collective-permute-done.1.other_ref
  148.2 3.3 %all-to-all-start.7 = ((f32[8,8,128]{2,1,0:T(8,128)}), f32[8,8,128]{2,1,0:T(8,128)S(1)}, u32[]{:S(2)}, u32[]{:S(2)}) async-start(f32[8,8,128]{2,1,0:T(8,128)} %shard_map.127), calls=%async_computation.8 | async-start | bytes 65536 | tf_op jit(solution)/shard_map/all_to_all | solution.py:359
  152.9 2.3 %all-gather.5.cloned.1.call-done.rows_ref = bf16[1536,1024]{1,0:T(8,128)(2,1)} async-done(((bf16[192,1024]{1,0:T(8,128)(2,1)}), bf16[1536,1024]{1,0:T(8,128)(2,1)}) %all-gather.5.cloned.1.call-update) | async-done | bytes 3145744 | tf_op jit(solution)/shard_map/all_gather | solution.py:449
  155.2 4.1 %shard_map.129 = f32[256,1024]{1,0:T(8,128)} custom-call(bf16[1536,1024]{1,0:T(8,128)(2,1)} %all-gather.5.cloned.1.call-done.rows_ref, s32[16,128]{1,0:T(8,128)} %copy-done.4), custom_call_target="tpu_custom_call" | custom-call | bytes 9000000 | tf_op jit(solution)/shard_map/pallas_call | solution.py:345
  159.4 1.2 shard_map.130
  (34 shorter events, 4.0 us)
Async XLA Ops:
  7.2 50.9 %copy-start.2 = (bf16[128,1024]{1,0:T(8,128)(2,1)S(1)}, bf16[128,1024]{1,0:T(8,128)(2,1)}, u32[]{:S(2)}) copy-start(bf16[128,1024]{1,0:T(8,128)(2,1)} %ct_ref.3) | copy-start | bytes 786436
  7.2 50.9 %copy-start.6 = (f32[512]{0:T(512)S(1)}, f32[512]{0:T(512)}, u32[]{:S(2)}) copy-start(f32[512]{0:T(512)} %param.16) | copy-start | bytes 6148
  7.2 50.8 %copy-start.5 = (f32[1024]{0:T(1024)S(1)}, f32[1024]{0:T(1024)}, u32[]{:S(2)}) copy-start(f32[1024]{0:T(1024)} %param.15) | copy-start | bytes 12292
  7.2 50.8 %copy-start.7 = (s32[1,8]{1,0:T(1,128)S(1)}, s32[1,8]{1,0:T(1,128)}, u32[]{:S(2)}) copy-start(s32[1,8]{1,0:T(1,128)} %lens_ref.1) | copy-start | bytes 100
  7.2 50.8 %all-gather.3.cloned.1.call-start = ((), (), s32[]{:S(2)}) async-start(), calls=%async_computation.9 | async-start | bytes 5570560 | tf_op jit(solution)/shard_map/all_gather | solution.py:376
  9.0 109.3 %reduce-scatter.2.cloned.1.call-start = ((), (), s32[]{:S(2)}) async-start(), calls=%async_computation.10 | async-start | bytes 2359296 | tf_op jit(solution)/shard_map/reduce_scatter | solution.py:429
  10.8 47.2 %copy-start.3 = (s32[128,128]{1,0:T(8,128)S(1)}, s32[128,128]{1,0:T(8,128)}, u32[]{:S(2)}) copy-start(s32[128,128]{1,0:T(8,128)} %get-tuple-element.25.tgt_ref) | copy-start | bytes 196612
  58.0 2.5 %copy-start = (bf16[2560,1024]{1,0:T(8,128)(2,1)S(1)}, bf16[2560,1024]{1,0:T(8,128)(2,1)}, u32[]{:S(2)}) copy-start(bf16[2560,1024]{1,0:T(8,128)(2,1)} %all-gather.3.cloned.1.call-done) | copy-start | bytes 15728644
  64.7 2.4 %collective-permute-start = (bf16[128,3072]{1,0:T(8,128)(2,1)S(1)}, bf16[128,3072]{1,0:T(8,128)(2,1)S(1)}, u32[]{:S(2)}, u32[]{:S(2)}) collective-permute-start(bf16[128,3072]{1,0:T(8,128)(2,1)S(1)} %get-tuple-element.28), channel_id=1, source_target_pairs={{0,8},{8,0},{1,9},{9,1},{2,10},{10,2},{3,11},{11,3},{4,12},{12,4},... | collective-permute-start | bytes 2359304 | tf_op jit(solution)/shard_map/ppermute | solution.py:414
  68.8 86.5 %all-gather.5.cloned.1.call-start = ((), (), s32[]{:S(2)}) async-start(), calls=%async_computation.11 | async-start | bytes 3538944 | tf_op jit(solution)/shard_map/all_gather | solution.py:449
  68.8 2.5 %copy-start.1 = (bf16[2560,1024]{1,0:T(8,128)(2,1)S(1)}, bf16[2560,1024]{1,0:T(8,128)(2,1)}, u32[]{:S(2)}) copy-start(bf16[2560,1024]{1,0:T(8,128)(2,1)} %all-gather.3.cloned.1.call-done) | copy-start | bytes 15728644
  118.3 11.4 %all-to-all-start.5 = ((bf16[16,16,512]{2,1,0:T(8,128)(2,1)}), bf16[16,16,512]{2,1,0:T(8,128)(2,1)S(1)}, u32[]{:S(2)}, u32[]{:S(2)}) async-start(bf16[16,16,512]{2,1,0:T(8,128)(2,1)} %bitcast.28), calls=%async_computation.6 | async-start | bytes 524288 | tf_op jit(solution)/shard_map/all_to_all | solution.py:359
  141.0 6.4 %collective-permute-start.1 = (bf16[16,16,640]{2,1,0:T(8,128)(2,1)S(1)}, bf16[16,16,640]{2,1,0:T(8,128)(2,1)S(1)}, u32[]{:S(2)}, u32[]{:S(2)}) collective-permute-start(bf16[16,16,640]{2,1,0:T(8,128)(2,1)S(1)} %all_to_all.51.mine_ref), channel_id=1, source_target_pairs={{0,8},{8,0},{1,9},{9,1},{2,10},{10,2},{3,11},{11,3},{4,12},{12,4},... | collective-permute-start | bytes 983048 | tf_op jit(solution)/shard_map/ppermute | solution.py:476
  148.2 11.1 %all-to-all-start.7 = ((f32[8,8,128]{2,1,0:T(8,128)}), f32[8,8,128]{2,1,0:T(8,128)S(1)}, u32[]{:S(2)}, u32[]{:S(2)}) async-start(f32[8,8,128]{2,1,0:T(8,128)} %shard_map.127), calls=%async_computation.8 | async-start | bytes 65536 | tf_op jit(solution)/shard_map/all_to_all | solution.py:359
  152.3 0.6 copy-start.4
Sparse Core Ops, SparseCore 0:
  10.4 47.5 all-gather.2
  68.9 36.2 reduce-scatter.1
  107.5 47.6 all-gather.4

commit v13 on v12

--- a/solution.py
+++ b/solution.py
@@ -19,7 +19,6 @@
 XY = 16
 PROWS = 16
 PCOLS = 640
-FACT = 3072
 USED = OWNERS * CAP
 TABLE = ("x", "y", "core")
 ALL = ("x", "y", "core", "z")
@@ -95,7 +94,7 @@
 
 def layer_kernel(
     lens_ref, got_ref, tgt_ref, weights_ref, gin_ref, gat_ref, ct_ref,
-    out_ref, keep_ref, send_ref, dmx, xhat_ref, rstd_ref,
+    out_ref, keep_ref, send_ref, keep2_ref, send2_ref, dmx, xhat_ref, rstd_ref,
 ):
     core = lax.axis_index("core")
     emb = mm(chosen(tgt_ref), got_ref[...])
@@ -178,11 +177,11 @@
     dmx[1] = d_mix1
     xhat_ref[...] = xhat
     rstd_ref[...] = jnp.broadcast_to(rstd, (TOK, TOK))
-    for side, dst in ((1 - core, send_ref), (core, keep_ref)):
+    for side, dst, dst2 in ((1 - core, send_ref, send2_ref), (core, keep_ref, keep2_ref)):
         dst[:, 0:1024] = normed
         dst[:, 1024:2048] = dmx[side]
-        dst[:, 2048:2560] = gated
-        dst[:, 2560:FACT] = ct_ref[:, pl.ds(pl.multiple_of(side * AW, AW), AW)]
+        dst2[:, 0:512] = gated
+        dst2[:, 512:1024] = ct_ref[:, pl.ds(pl.multiple_of(side * AW, AW), AW)]
 
 
 def rows_kernel(tgt_ref, weights_ref, gin_ref, ct_ref, dmx, xhat_ref, rstd_ref, slots_ref):
@@ -202,21 +201,26 @@
     slots_ref[...] = mm_tn(chosen(tgt_ref), d_emb).astype(BF16)
 
 
-def grads_kernel(keep_ref, theirs_ref, mix_ref, out_ref, mix, out, sems):
-    def both(first, last):
-        return jnp.concatenate([keep_ref[:, first:last], theirs_ref[:, first:last]], axis=0)
-
+def both(keep_ref, theirs_ref, first, last):
+    return jnp.concatenate([keep_ref[:, first:last], theirs_ref[:, first:last]], axis=0)
+
+
+def mix_kernel(keep_ref, theirs_ref, mix_ref, mix, sems):
     copies = []
-    d_mix = both(1024, 2048)
+    d_mix = both(keep_ref, theirs_ref, 1024, 2048)
     for z in range(NZ):
-        grad = mm_tn(both(z * TOK, (z + 1) * TOK), d_mix)
+        grad = mm_tn(both(keep_ref, theirs_ref, z * TOK, (z + 1) * TOK), d_mix)
         for p in range(XY):
             part = grad[8 * p : 8 * p + 8]
             mix[z, p] = jnp.concatenate([part[:, :512], part[:, 512:]], axis=0).astype(BF16)
         copies.append(pltpu.make_async_copy(mix.at[z], mix_ref.at[z], sems.at[z]))
         copies[-1].start()
-
-    grad = mm_tn(both(2048, 2560), both(2560, FACT))
+    for copy in copies:
+        copy.wait()
+
+
+def out_kernel(keep_ref, theirs_ref, out):
+    grad = mm_tn(both(keep_ref, theirs_ref, 0, 512), both(keep_ref, theirs_ref, 512, 1024))
     for z in range(NZ):
         for p in range(XY):
             r, c = z * 64 + (p // 2) * 8, (p % 2) * 256
@@ -224,10 +228,6 @@
             out[p, z * PROWS : (z + 1) * PROWS] = jnp.concatenate(
                 [part[:, :128], part[:, 128:]], axis=0
             ).astype(BF16)
-    copies.append(pltpu.make_async_copy(out, out_ref, sems.at[NZ]))
-    copies[-1].start()
-    for copy in copies:
-        copy.wait()
 
 
 def column_kernel(plane_ref, asked_ref, out_ref):
@@ -387,12 +387,14 @@
 
     smem = pl.BlockSpec(memory_space=pltpu.SMEM)
     gin = gain_in.reshape(1, D)
-    layer_out, keep, send, d_mix, xhat, rstd = call(
+    layer_out, keep, send, keep2, send2, d_mix, xhat, rstd = call(
         layer_kernel,
         [
             ((TOK, D), BF16),
-            ((TOK, FACT), BF16),
-            ((TOK, FACT), BF16),
+            ((TOK, 2 * D), BF16),
+            ((TOK, 2 * D), BF16),
+            ((TOK, D), BF16),
+            ((TOK, D), BF16),
             ((2, TOK, D), BF16),
             ((TOK, D), F32),
             ((TOK, TOK), F32),
@@ -412,20 +414,19 @@
     )
 
     theirs = lax.ppermute(send, "core", [(0, 1), (1, 0)])
-    mix_part, out_part = call(
-        grads_kernel,
-        [((NZ, XY, PROWS, 512), BF16), ((XY, NZ * PROWS, 128), BF16)],
+    mix_part = call(
+        mix_kernel,
+        [((NZ, XY, PROWS, 512), BF16)],
         (keep, theirs),
-        outs_specs=[anywhere, anywhere],
+        outs_specs=anywhere,
         scratch_shapes=[
             pltpu.VMEM((NZ, XY, PROWS, 512), BF16),
-            pltpu.VMEM((XY, NZ * PROWS, 128), BF16),
-            pltpu.SemaphoreType.DMA((NZ + 1,)),
+            pltpu.SemaphoreType.DMA((NZ,)),
         ],
         cost_estimate=cost(3),
         compiler_params=pltpu.CompilerParams(vmem_limit_bytes=30 * MB),
     )
-    mix_part, d_mix = lax.optimization_barrier((mix_part, d_mix))
+    mix_part, d_mix, send2 = lax.optimization_barrier((mix_part, d_mix, send2))
     mix_column = lax.psum_scatter(
         mix_part.reshape(NZ * XY * PROWS, 512), "z", scatter_dimension=0, tiled=True
     )
@@ -443,6 +444,13 @@
         [((USED, D), BF16)],
         (received.reshape(OWNERS * SLOTS, D),),
         cost_estimate=cost(2),
+        compiler_params=pltpu.CompilerParams(vmem_limit_bytes=16 * MB),
+    )
+    out_part = call(
+        out_kernel,
+        [((XY, NZ * PROWS, 128), BF16)],
+        (keep2, lax.ppermute(send2, "core", [(0, 1), (1, 0)])),
+        cost_estimate=cost(1),
         compiler_params=pltpu.CompilerParams(vmem_limit_bytes=16 * MB),
     )
     out_part, packed = lax.optimization_barrier((out_part, packed))

time: 168 us -> 168 us (level)
  blocking collectives: 86.1 us -> 67.6 us
  waiting for transfers between devices: 24.8 us -> 34.4 us
  starting transfers between devices: 12.9 us -> 20.3 us
    all_to_all x6 -> x5, blocking collectives: 86.1 us -> 67.6 us  [exchange(): return lax.all_to_all(array, axes, split_axis=0, concat_axis=0, tiled=True)]
    all_to_all x2 -> x3, waiting for transfers between devices: 7.33 us -> 16.9 us  [exchange(): return lax.all_to_all(array, axes, split_axis=0, concat_axis=0, tiled=True)]
    all_to_all x2 -> x3, starting transfers between devices: 7.35 us -> 14.4 us  [exchange(): return lax.all_to_all(array, axes, split_axis=0, concat_axis=0, tiled=True)]
    pallas_call x11 -> x12, Pallas kernels: 19.2 us -> 20.5 us  [call(): pl.pallas_call(body, out_shape=shapes[0] if one else shapes, in_specs=spe...]
  transfers between devices with their start and end apart: 7 -> 9, of which waited for: 5 -> 7; matrix products, arithmetic and copies ran while one was open for 3% -> 3% of each run, Pallas kernels for 6% -> 7%
where the time goes in v13:
time: 168 us; the launch traced here: 167 us
  blocking collectives  67.6 us (40%)
  waiting for transfers between devices  34.4 us (20%)
  Pallas kernels  20.5 us (12%)
  starting transfers between devices  20.3 us (12%)
  between operations  13.9 us (8%)
  local copies, waits for them, and re-layouts  9.98 us (6%)
    all_to_all x5, blocking collectives, exchange(): return lax.all_to_all(array, axes, split_axis=0, concat_axis=0, tiled=True)  67.6 us
    pallas_call x12, Pallas kernels, call(): pl.pallas_call(body, out_shape=shapes[0] if one else shapes, in_specs=spe...  20.5 us
    all_to_all x3, waiting for transfers between devices, exchange(): return lax.all_to_all(array, axes, split_axis=0, concat_axis=0, tiled=True)  16.9 us
    all_to_all x3, starting transfers between devices, exchange(): return lax.all_to_all(array, axes, split_axis=0, concat_axis=0, tiled=True)  14.4 us
    all_gather x1, waiting for transfers between devices, shards(): lax.all_gather(share, ('core', 'z'), axis=0, tiled=True)  11.9 us
    unnamed x16, local copies, waits for them, and re-layouts  5.58 us
    ppermute x1, starting transfers between devices, shards(): other = lax.ppermute(mine, 'core', [(0, 1), (1, 0)])  5.23 us
    gather x1, local copies, waits for them, and re-layouts, shards(): found = item_table.at[wanted].get(mode='promise_in_bounds')  4.29 us
  transfers between devices with their start and end apart: 9, of which 7 were waited for; matrix products, arithmetic and copies ran while one was open for 3% of the time, Pallas kernels for 7%

profile of v13, /device:TPU:1, one launch (start us, length us, event | category | flops | bytes accessed | tf_op | source)
XLA Modules:
  0.0 166.8 jit_solution(12974492885391620174)
XLA Ops:
  7.3 1.7 %shard_map.121 = bf16[160,1024]{1,0:T(8,128)(2,1)} custom-call(bf16[128,2048]{1,0:T(8,128)(2,1)} %mix_ref.1, bf16[64,1024]{1,0:T(8,128)(2,1)} %out_ref.1), custom_call_target="tpu_custom_call" | custom-call | tf_op jit(solution)/shard_map/pallas_call | solution.py:345
  9.1 1.7 %shard_map.120 = (s32[32,128]{1,0:T(8,128)}, s32[128,128]{1,0:T(8,128)}) custom-call(s32[1,128]{1,0:T(1,128)} %bitcast.30, s32[1,128]{1,0:T(1,128)} %bitcast.31), custom_call_target="tpu_custom_call" | custom-call | tf_op jit(solution)/shard_map/pallas_call | solution.py:345
  10.8 15.6 %all_to_all.46 = s32[32,1,128]{2,1,0:T(1,128)S(1)} all-to-all(s32[32,1,128]{2,1,0:T(1,128)} %bitcast.28), channel_id=1, replica_groups=mesh['x'=4,'y'=4,'core'=2,'z'=8] {'x','y','core'}, dimensions={0} | all-to-all | bytes 32768 | tf_op jit(solution)/shard_map/all_to_all | solution.py:359
  26.5 4.3 %gather_fusion = bf16[256,1024]{1,0:T(8,128)(2,1)S(1)} fusion(bf16[2048,1024]{1,0:T(8,128)(2,1)} %param.9, s32[1024]{0:T(1024)S(1)} %pad_clamp_fusion), kind=kCustom, calls=%fused_computation | custom fusion | bytes 1049600 | tf_op jit(solution)/shard_map/gather | solution.py:385
  30.8 15.3 %all_to_all.47 = bf16[32,8,1024]{2,1,0:T(8,128)(2,1)S(1)} all-to-all(bf16[32,8,1024]{2,1,0:T(8,128)(2,1)S(1)} %bitcast.26), channel_id=1, replica_groups=mesh['x'=4,'y'=4,'core'=2,'z'=8] {'x','y','core'}, dimensions={0} | all-to-all | bytes 1048576 | tf_op jit(solution)/shard_map/all_to_all | solution.py:359
  46.1 11.9 %all-gather.3.cloned.1.call-done = bf16[2560,1024]{1,0:T(8,128)(2,1)} async-done(((bf16[160,1024]{1,0:T(8,128)(2,1)}), bf16[2560,1024]{1,0:T(8,128)(2,1)}) %all-gather.3.cloned.1.call-update) | async-done | bytes 5242896 | tf_op jit(solution)/shard_map/all_gather | solution.py:376
  58.1 2.5 %copy-done = bf16[2560,1024]{1,0:T(8,128)(2,1)S(1)} copy-done((bf16[2560,1024]{1,0:T(8,128)(2,1)S(1)}, bf16[2560,1024]{1,0:T(8,128)(2,1)}, u32[]{:S(2)}) %copy-start) | copy-done | bytes 5242904
  60.5 4.4 %shard_map.122 = (bf16[128,1024]{1,0:T(8,128)(2,1)}, bf16[128,2048]{1,0:T(8,128)(2,1)S(1)}, bf16[128,2048]{1,0:T(8,128)(2,1)S(1)}, bf16[128,1024]{1,0:T(8,128)(2...) custom-call(s32[1,8]{1,0:T(1,128)S(1)} %copy-done.7, ...), custom_call_target="tpu_custom_call" | custom-call | bytes 21000000 | tf_op jit(solution)/shard_map/pallas_call | solution.py:345
  65.2 1.7 collective-permute-done.theirs_ref
  66.8 1.7 %shard_map.123 = bf16[8,16,16,512]{3,2,1,0:T(8,128)(2,1)} custom-call(bf16[128,2048]{1,0:T(8,128)(2,1)S(1)} %get-tuple-element.28.keep_ref, bf16[128,2048]{1,0:T(8,128)(2,1)S(1)} %collective-permute-done.theirs_ref), custom_call_target="tpu_custom_call" | custom-call | bytes 9000000 | tf_op jit(solution)/shard_map/pallas_call | solution.py:345
  68.5 2.5 %copy-done.1 = bf16[2560,1024]{1,0:T(8,128)(2,1)S(1)} copy-done((bf16[2560,1024]{1,0:T(8,128)(2,1)S(1)}, bf16[2560,1024]{1,0:T(8,128)(2,1)}, u32[]{:S(2)}) %copy-start.1) | copy-done | bytes 5242904
  71.0 2.7 %shard_map.125 = bf16[256,1024]{1,0:T(8,128)(2,1)} custom-call(s32[128,128]{1,0:T(8,128)S(1)} %copy-done.3, bf16[2,8,160,1024]{3,2,1,0:T(8,128)(2,1)S(1)} %bitcast.18, f32[1,1024]{1,0:T(1,128)S(1)} %bitcast.24, bf16[128,1024]{1,0:T(8,128)(2,1)S(1)} %copy-done.2, bf16[2,128,1024]{2,1,0:T(8,128)(2,1)S(1)} %get-tuple-element.35.dmx, ...), custom_call_target="tpu_custom_call" | custom-call | bytes 9000000 | tf_op jit(solution)/shard_map/pallas_call | solution.py:345
  73.7 7.1 %all-to-all-start.2 = ((bf16[32,8,1024]{2,1,0:T(8,128)(2,1)}), bf16[32,8,1024]{2,1,0:T(8,128)(2,1)S(1)}, u32[]{:S(2)}, u32[]{:S(2)}) async-start(bf16[32,8,1024]{2,1,0:T(8,128)(2,1)} %bitcast.12), calls=%async_computation.3 | async-start | bytes 1048576 | tf_op jit(solution)/shard_map/all_to_all | solution.py:359
  81.3 1.3 collective-permute-done.1.theirs_ref
  82.9 9.6 %all-to-all-done.2 = bf16[32,8,1024]{2,1,0:T(8,128)(2,1)S(1)} async-done(((bf16[32,8,1024]{2,1,0:T(8,128)(2,1)}), bf16[32,8,1024]{2,1,0:T(8,128)(2,1)S(1)}, u32[]{:S(2)}, u32[]{:S(2)}) %all-to-all-start.2) | async-done | bytes 524320 | tf_op jit(solution)/shard_map/all_to_all | solution.py:359
  93.6 13.2 %all_to_all.48.plane_ref = bf16[16,128,128]{2,1,0:T(8,128)(2,1)S(1)} all-to-all(bf16[16,128,128]{2,1,0:T(8,128)(2,1)S(1)} %shard_map.124), channel_id=1, replica_groups=mesh['x'=4,'y'=4,'core'=2,'z'=8] {'x','y'}, dimensions={0} | all-to-all | bytes 1048576 | tf_op jit(solution)/shard_map/all_to_all | solution.py:359
  106.8 12.2 %all_to_all.49.column_ref = bf16[8,80,128]{2,1,0:T(8,128)(2,1)S(1)} all-to-all(bf16[8,80,128]{2,1,0:T(8,128)(2,1)S(1)} %shard_map.127), channel_id=1, replica_groups=mesh['x'=4,'y'=4,'core'=2,'z'=8] {'z'}, dimensions={0} | all-to-all | bytes 327680 | tf_op jit(solution)/shard_map/all_to_all | solution.py:359
  119.0 3.9 %all-to-all-start.5 = ((bf16[16,16,512]{2,1,0:T(8,128)(2,1)}), bf16[16,16,512]{2,1,0:T(8,128)(2,1)S(1)}, u32[]{:S(2)}, u32[]{:S(2)}) async-start(bf16[16,16,512]{2,1,0:T(8,128)(2,1)} %bitcast.27), calls=%async_computation.6 | async-start | bytes 524288 | tf_op jit(solution)/shard_map/all_to_all | solution.py:359
  123.0 7.3 %all-to-all-done.5 = bf16[16,16,512]{2,1,0:T(8,128)(2,1)S(1)} async-done(((bf16[16,16,512]{2,1,0:T(8,128)(2,1)}), bf16[16,16,512]{2,1,0:T(8,128)(2,1)S(1)}, u32[]{:S(2)}, u32[]{:S(2)}) %all-to-all-start.5) | async-done | bytes 262176 | tf_op jit(solution)/shard_map/all_to_all | solution.py:359
  130.4 11.3 %all_to_all.50.mine_ref = bf16[16,16,640]{2,1,0:T(8,128)(2,1)S(1)} all-to-all(bf16[16,16,640]{2,1,0:T(8,128)(2,1)S(1)} %broadcast_in_dim.2), channel_id=1, replica_groups=mesh['x'=4,'y'=4,'core'=2,'z'=8] {'x','y'}, dimensions={0} | all-to-all | bytes 655360 | tf_op jit(solution)/shard_map/all_to_all | solution.py:359
  141.6 5.2 %collective-permute-start.2 = (bf16[16,16,640]{2,1,0:T(8,128)(2,1)S(1)}, bf16[16,16,640]{2,1,0:T(8,128)(2,1)S(1)}, u32[]{:S(2)}, u32[]{:S(2)}) collective-permute-start(bf16[16,16,640]{2,1,0:T(8,128)(2,1)S(1)} %all_to_all.50.mine_ref), channel_id=1, source_target_pairs={{0,8},{8,0},{1,9},{9,1},{2,10},{10,2},{3,11},{11,3},{4,12},{12,4},... | collective-permute-start | bytes 983048 | tf_op jit(solution)/shard_map/ppermute | solution.py:484
  148.9 3.3 %all-to-all-start.7 = ((f32[8,8,128]{2,1,0:T(8,128)}), f32[8,8,128]{2,1,0:T(8,128)S(1)}, u32[]{:S(2)}, u32[]{:S(2)}) async-start(f32[8,8,128]{2,1,0:T(8,128)} %shard_map.128), calls=%async_computation.8 | async-start | bytes 65536 | tf_op jit(solution)/shard_map/all_to_all | solution.py:359
  153.6 1.3 all-gather.5.cloned.1.call-done.rows_ref
  154.9 4.1 %shard_map.130 = f32[256,1024]{1,0:T(8,128)} custom-call(bf16[1536,1024]{1,0:T(8,128)(2,1)} %all-gather.5.cloned.1.call-done.rows_ref, s32[16,128]{1,0:T(8,128)} %copy-done.4), custom_call_target="tpu_custom_call" | custom-call | bytes 9000000 | tf_op jit(solution)/shard_map/pallas_call | solution.py:345
  (38 shorter events, 7.0 us)
Async XLA Ops:
  7.2 50.9 %copy-start.2 = (bf16[128,1024]{1,0:T(8,128)(2,1)S(1)}, bf16[128,1024]{1,0:T(8,128)(2,1)}, u32[]{:S(2)}) copy-start(bf16[128,1024]{1,0:T(8,128)(2,1)} %ct_ref.3) | copy-start | bytes 786436
  7.2 50.9 %copy-start.6 = (f32[512]{0:T(512)S(1)}, f32[512]{0:T(512)}, u32[]{:S(2)}) copy-start(f32[512]{0:T(512)} %param.16) | copy-start | bytes 6148
  7.2 50.8 %copy-start.5 = (f32[1024]{0:T(1024)S(1)}, f32[1024]{0:T(1024)}, u32[]{:S(2)}) copy-start(f32[1024]{0:T(1024)} %param.15) | copy-start | bytes 12292
  7.2 50.8 %copy-start.7 = (s32[1,8]{1,0:T(1,128)S(1)}, s32[1,8]{1,0:T(1,128)}, u32[]{:S(2)}) copy-start(s32[1,8]{1,0:T(1,128)} %lens_ref.1) | copy-start | bytes 100
  7.2 50.8 %all-gather.3.cloned.1.call-start = ((), (), s32[]{:S(2)}) async-start(), calls=%async_computation.9 | async-start | bytes 5570560 | tf_op jit(solution)/shard_map/all_gather | solution.py:376
  9.0 110.0 %reduce-scatter.2.cloned.1.call-start = ((), (), s32[]{:S(2)}) async-start(), calls=%async_computation.10 | async-start | bytes 2359296 | tf_op jit(solution)/shard_map/reduce_scatter | solution.py:430
  10.8 47.2 %copy-start.3 = (s32[128,128]{1,0:T(8,128)S(1)}, s32[128,128]{1,0:T(8,128)}, u32[]{:S(2)}) copy-start(s32[128,128]{1,0:T(8,128)} %get-tuple-element.26.tgt_ref) | copy-start | bytes 196612
  58.0 2.5 %copy-start = (bf16[2560,1024]{1,0:T(8,128)(2,1)S(1)}, bf16[2560,1024]{1,0:T(8,128)(2,1)}, u32[]{:S(2)}) copy-start(bf16[2560,1024]{1,0:T(8,128)(2,1)} %all-gather.3.cloned.1.call-done) | copy-start | bytes 15728644
  64.9 1.9 %collective-permute-start = (bf16[128,2048]{1,0:T(8,128)(2,1)S(1)}, bf16[128,2048]{1,0:T(8,128)(2,1)S(1)}, u32[]{:S(2)}, u32[]{:S(2)}) collective-permute-start(bf16[128,2048]{1,0:T(8,128)(2,1)S(1)} %get-tuple-element.29), channel_id=1, source_target_pairs={{0,8},{8,0},{1,9},{9,1},{2,10},{10,2},{3,11},{11,3},{4,12},{12,4},... | collective-permute-start | bytes 1572872 | tf_op jit(solution)/shard_map/ppermute | solution.py:416
  68.5 2.5 %copy-start.1 = (bf16[2560,1024]{1,0:T(8,128)(2,1)S(1)}, bf16[2560,1024]{1,0:T(8,128)(2,1)}, u32[]{:S(2)}) copy-start(bf16[2560,1024]{1,0:T(8,128)(2,1)} %all-gather.3.cloned.1.call-done) | copy-start | bytes 15728644
  73.7 18.8 %all-to-all-start.2 = ((bf16[32,8,1024]{2,1,0:T(8,128)(2,1)}), bf16[32,8,1024]{2,1,0:T(8,128)(2,1)S(1)}, u32[]{:S(2)}, u32[]{:S(2)}) async-start(bf16[32,8,1024]{2,1,0:T(8,128)(2,1)} %bitcast.12), calls=%async_computation.3 | async-start | bytes 1048576 | tf_op jit(solution)/shard_map/all_to_all | solution.py:359
  80.9 74.1 %all-gather.5.cloned.1.call-start = ((), (), s32[]{:S(2)}) async-start(), calls=%async_computation.11 | async-start | bytes 3538944 | tf_op jit(solution)/shard_map/all_gather | solution.py:457
  80.9 1.6 collective-permute-start.1
  119.0 11.2 %all-to-all-start.5 = ((bf16[16,16,512]{2,1,0:T(8,128)(2,1)}), bf16[16,16,512]{2,1,0:T(8,128)(2,1)S(1)}, u32[]{:S(2)}, u32[]{:S(2)}) async-start(bf16[16,16,512]{2,1,0:T(8,128)(2,1)} %bitcast.27), calls=%async_computation.6 | async-start | bytes 524288 | tf_op jit(solution)/shard_map/all_to_all | solution.py:359
  141.6 6.5 %collective-permute-start.2 = (bf16[16,16,640]{2,1,0:T(8,128)(2,1)S(1)}, bf16[16,16,640]{2,1,0:T(8,128)(2,1)S(1)}, u32[]{:S(2)}, u32[]{:S(2)}) collective-permute-start(bf16[16,16,640]{2,1,0:T(8,128)(2,1)S(1)} %all_to_all.50.mine_ref), channel_id=1, source_target_pairs={{0,8},{8,0},{1,9},{9,1},{2,10},{10,2},{3,11},{11,3},{4,12},{12,4},... | collective-permute-start | bytes 983048 | tf_op jit(solution)/shard_map/ppermute | solution.py:484
  148.9 10.1 %all-to-all-start.7 = ((f32[8,8,128]{2,1,0:T(8,128)}), f32[8,8,128]{2,1,0:T(8,128)S(1)}, u32[]{:S(2)}, u32[]{:S(2)}) async-start(f32[8,8,128]{2,1,0:T(8,128)} %shard_map.128), calls=%async_computation.8 | async-start | bytes 65536 | tf_op jit(solution)/shard_map/all_to_all | solution.py:359
  153.0 0.6 copy-start.4
Sparse Core Ops, SparseCore 0:
  10.4 47.5 all-gather.2
  68.7 36.2 reduce-scatter.1
  107.3 47.5 all-gather.4
